TPU v7x, 128 devices: a whole 4x4x4 slice. The times are simulated.
128 devices in a mesh: row: 16 (over x, z_lo, core), col: 8 (over z_hi, y).
Axes of the slice: x: 4, y: 4, z: 4 (z_hi: 2, z_lo: 2; z = z_hi * 2 + z_lo), core: 2. Of those that a mesh axis runs over, the one named last changes fastest.
Arguments:
- features: bfloat16 [512, 8, 8192], P(None, 'col', 'row'), may hold values from 0 to 40
- block_values: bfloat16 [2, 16, 8, 320, 128, 128], P(None, 'row', 'col'), may hold values from -0.078125 to 0.078125
- block_rows: int32 [2, 16, 8, 320], P(None, 'row', 'col'), may hold values from 0 to 63, as said below
- block_cols: int32 [2, 16, 8, 320], P(None, 'row', 'col'), may hold values from 0 to 31
- block_counts: int32 [2, 16, 8], P(None, 'row', 'col'), may hold values from 80 to 320, as said below
- bias: float32 [2, 8, 8192], P(None, 'col', 'row'), may hold values from -1 to 0
Outputs:
- activations: bfloat16 [512, 8, 8192], P(None, 'col', 'row')
Inputs may be any that keep to these rules, and one draw needn't show every extreme that they name: `block_rows`: each device's live slots in a layer name distinct block positions. `block_counts`: in every layer some device has all 320 slots live.
All inputs are finite; a program needn't handle non-finite values.
Results may differ from a plain program's by a relative error of at most 0.0036.
Values may be sent and summed in bfloat16 or wider, within the bound.
No kernel may reach another device: no remote copies, remote signals or barrier semaphores. Data moves between devices by JAX's collectives and lax.ppermute only.
A program may use at most 192 MiB of HBM per device.

v0:
```python
import jax
import jax.numpy as jnp
from jax import lax
from jax.sharding import PartitionSpec as P

N = 65536


def add_slots(
    running, panel_blocks, values, slot_rows, slot_cols, slot_order, first_slot, last_slot, row_base
):
    slots = values.shape[0]
    group_size = min(32, slots)
    turns = (last_slot - first_slot + group_size - 1) // group_size
    offsets = jnp.arange(group_size, dtype=jnp.int32)
    last_block = panel_blocks.shape[1] - 1

    def advance(turn_index, inner):
        where_at = first_slot + turn_index * group_size + offsets
        live_slot = where_at < last_slot
        picked = slot_order[jnp.minimum(where_at, slots - 1)]
        local_rows = jnp.clip(slot_rows[picked] - row_base, 0, last_block)
        left_rows = panel_blocks[:, local_rows, :]
        blocks = values[picked]
        product = jnp.einsum("bgi,gij->bgj", left_rows, blocks, preferred_element_type=jnp.float32)
        product = jnp.where(live_slot[None, :, None], product, jnp.zeros_like(product))
        return inner.at[:, slot_cols[picked], :].add(product)

    return lax.fori_loop(0, turns, advance, running)


def on_device(features, block_values, block_rows, block_cols, block_counts, bias):
    layers = block_values.shape[0]
    slots = block_values.shape[3]
    blk = block_values.shape[4]
    batch_rows = features.shape[0]
    out_width = N // lax.axis_size("row")
    current = features
    for layer_index in range(layers):
        values = block_values[layer_index, 0, 0]
        slot_rows = block_rows[layer_index, 0, 0]
        slot_cols = block_cols[layer_index, 0, 0]
        live_count = block_counts[layer_index, 0, 0]
        slot_index = jnp.arange(slots, dtype=jnp.int32)
        empty = jnp.zeros((batch_rows, out_width // blk, blk), jnp.float32)
        panel_full = lax.all_gather(current[:, 0, :], "row", axis=1, tiled=True)
        panel_blocks = panel_full.reshape(batch_rows, -1, blk)
        summed = add_slots(
            empty, panel_blocks, values, slot_rows, slot_cols, slot_index, 0, live_count, 0
        )
        shares = lax.psum_scatter(
            summed.reshape(batch_rows, out_width), "col", scatter_dimension=1, tiled=True
        )
        current = jnp.clip(shares + bias[layer_index, 0, :], 0.0, 32.0).astype(jnp.bfloat16)[
            :, None, :
        ]
    return current


def solution(mesh):
    in_specs = (
        P(None, "col", "row"),
        P(None, "row", "col", None, None, None),
        P(None, "row", "col", None),
        P(None, "row", "col", None),
        P(None, "row", "col"),
        P(None, "col", "row"),
    )
    out_specs = P(None, "col", "row")
    return jax.shard_map(
        on_device, mesh=mesh, in_specs=in_specs, out_specs=out_specs, check_vma=False
    )
```

profile of v0, /device:TPU:0, one launch (start us, length us, event | category | flops | bytes accessed | tf_op | source)
XLA Modules:
  0.0 1371.3 jit_solution(17525113062541178021)
XLA Ops:
  11.3 16.6 %slice_bitcast_fusion = (bf16[320,128,128]{2,1,0:T(8,128)(2,1)}, bf16[320,128,128]{2,1,0:T(8,128)(2,1)}) fusion(bf16[2,1,1,320,128,128]{5,4,3,2,1,0:T(8,128)(2,1)} %param.11), kind=kLoop, calls=%fused_computation.50 | loop fusion | bytes 41943040 | tf_op jit(solution)/shard_map/squeeze | solution.py:40
  27.9 35.8 %all-gather.6.cloned.1.call-done = bf16[512,1,8192]{0,2,1:T(8,128)(2,1)} async-done(((bf16[512,1,512]{0,2,1:T(8,128)(2,1)}), bf16[512,1,8192]{0,2,1:T(8,128)(2,1)}) %all-gather.6.cloned.1.call-update) | async-done | bytes 8388624 | tf_op jit(solution)/shard_map/all_gather | solution.py:46
  63.7 11.9 copy.27
  79.8 485.0 %while.22 = (s32[]{:T(128)}, f32[512,32,128]{2,0,1:T(8,128)}, s32[]{:T(128)}, s32[320]{0:T(512)S(1)}, s32[]{:T(128)}, /*index=5*/bf16[320,128,128]{2,1,0:T(8,128...) while((s32[]{:T(128)}, f32[512,32,128]{2,0,1:T(8,128)}, s32[]{:T(128)}, ...), condition=%wide.region_2.3_spmd.clone, body=%wide.region_0.2_spmd.clone.sunk | while | flops 541068864 | bytes 66076860 | solution.py:29
  100.0 9.0 copy.41
  109.7 18.4 %scatter_fusion = f32[512,32,128]{2,0,1:T(8,128)} fusion(f32[512,32,128]{2,0,1:T(8,128)} %get-tuple-element.332, s32[32]{0:T(128)S(1)} %fusion.54, f32[32,512,128]{2,1,0:T(8,128)} %copy.41), kind=kCustom, calls=%fused_computation.10.clone.clone.1 | custom fusion | flops 2097152 | bytes 25165952 | tf_op jit(solution)/shard_map/while/body/scatter-add | solution.py:27
  148.4 9.0 copy.41
  158.0 18.6 %scatter_fusion = f32[512,32,128]{2,0,1:T(8,128)} fusion(f32[512,32,128]{2,0,1:T(8,128)} %get-tuple-element.332, s32[32]{0:T(128)S(1)} %fusion.54, f32[32,512,128]{2,1,0:T(8,128)} %copy.41), kind=kCustom, calls=%fused_computation.10.clone.clone.1 | custom fusion | flops 2097152 | bytes 25165952 | tf_op jit(solution)/shard_map/while/body/scatter-add | solution.py:27
  196.9 9.0 copy.41
  206.5 18.6 %scatter_fusion = f32[512,32,128]{2,0,1:T(8,128)} fusion(f32[512,32,128]{2,0,1:T(8,128)} %get-tuple-element.332, s32[32]{0:T(128)S(1)} %fusion.54, f32[32,512,128]{2,1,0:T(8,128)} %copy.41), kind=kCustom, calls=%fused_computation.10.clone.clone.1 | custom fusion | flops 2097152 | bytes 25165952 | tf_op jit(solution)/shard_map/while/body/scatter-add | solution.py:27
  245.4 9.0 copy.41
  255.0 18.5 %scatter_fusion = f32[512,32,128]{2,0,1:T(8,128)} fusion(f32[512,32,128]{2,0,1:T(8,128)} %get-tuple-element.332, s32[32]{0:T(128)S(1)} %fusion.54, f32[32,512,128]{2,1,0:T(8,128)} %copy.41), kind=kCustom, calls=%fused_computation.10.clone.clone.1 | custom fusion | flops 2097152 | bytes 25165952 | tf_op jit(solution)/shard_map/while/body/scatter-add | solution.py:27
  293.8 9.0 copy.41
  303.4 18.5 %scatter_fusion = f32[512,32,128]{2,0,1:T(8,128)} fusion(f32[512,32,128]{2,0,1:T(8,128)} %get-tuple-element.332, s32[32]{0:T(128)S(1)} %fusion.54, f32[32,512,128]{2,1,0:T(8,128)} %copy.41), kind=kCustom, calls=%fused_computation.10.clone.clone.1 | custom fusion | flops 2097152 | bytes 25165952 | tf_op jit(solution)/shard_map/while/body/scatter-add | solution.py:27
  342.2 9.0 copy.41
  351.9 18.7 %scatter_fusion = f32[512,32,128]{2,0,1:T(8,128)} fusion(f32[512,32,128]{2,0,1:T(8,128)} %get-tuple-element.332, s32[32]{0:T(128)S(1)} %fusion.54, f32[32,512,128]{2,1,0:T(8,128)} %copy.41), kind=kCustom, calls=%fused_computation.10.clone.clone.1 | custom fusion | flops 2097152 | bytes 25165952 | tf_op jit(solution)/shard_map/while/body/scatter-add | solution.py:27
  390.9 9.0 copy.41
  400.5 18.6 %scatter_fusion = f32[512,32,128]{2,0,1:T(8,128)} fusion(f32[512,32,128]{2,0,1:T(8,128)} %get-tuple-element.332, s32[32]{0:T(128)S(1)} %fusion.54, f32[32,512,128]{2,1,0:T(8,128)} %copy.41), kind=kCustom, calls=%fused_computation.10.clone.clone.1 | custom fusion | flops 2097152 | bytes 25165952 | tf_op jit(solution)/shard_map/while/body/scatter-add | solution.py:27
  449.1 18.5 %scatter_fusion = f32[512,32,128]{2,0,1:T(8,128)} fusion(f32[512,32,128]{2,0,1:T(8,128)} %get-tuple-element.332, s32[32]{0:T(128)S(1)} %fusion.54, f32[32,512,128]{2,1,0:T(8,128)} %copy.41), kind=kCustom, calls=%fused_computation.10.clone.clone.1 | custom fusion | flops 2097152 | bytes 25165952 | tf_op jit(solution)/shard_map/while/body/scatter-add | solution.py:27
  497.5 18.7 %scatter_fusion = f32[512,32,128]{2,0,1:T(8,128)} fusion(f32[512,32,128]{2,0,1:T(8,128)} %get-tuple-element.332, s32[32]{0:T(128)S(1)} %fusion.54, f32[32,512,128]{2,1,0:T(8,128)} %copy.41), kind=kCustom, calls=%fused_computation.10.clone.clone.1 | custom fusion | flops 2097152 | bytes 25165952 | tf_op jit(solution)/shard_map/while/body/scatter-add | solution.py:27
  546.1 18.7 %scatter_fusion = f32[512,32,128]{2,0,1:T(8,128)} fusion(f32[512,32,128]{2,0,1:T(8,128)} %get-tuple-element.332, s32[32]{0:T(128)S(1)} %fusion.54, f32[32,512,128]{2,1,0:T(8,128)} %copy.41), kind=kCustom, calls=%fused_computation.10.clone.clone.1 | custom fusion | flops 2097152 | bytes 25165952 | tf_op jit(solution)/shard_map/while/body/scatter-add | solution.py:27
  573.3 114.3 %reduce-scatter.3.cloned.1.call-done = f32[512,512]{1,0:T(8,128)} async-done(((f32[512,4096]{1,0:T(8,128)}), f32[512,512]{1,0:T(8,128)}) %reduce-scatter.3.cloned.1.call-update) | async-done | bytes 1048592 | tf_op jit(solution)/shard_map/reduce_scatter | solution.py:51
  690.4 49.3 %all-gather.4.cloned.1.call-done = bf16[512,8192]{1,0:T(8,128)(2,1)} async-done(((bf16[512,512]{1,0:T(8,128)(2,1)}), bf16[512,8192]{1,0:T(8,128)(2,1)}) %all-gather.4.cloned.1.call-update) | async-done | bytes 8388624 | tf_op jit(solution)/shard_map/all_gather | solution.py:46
  739.7 9.1 copy_bitcast_fusion.2
  753.1 145.9 %while.23 = (s32[]{:T(128)}, f32[512,32,128]{2,0,1:T(8,128)}, s32[]{:T(128)}, s32[320]{0:T(512)S(1)}, s32[]{:T(128)}, /*index=5*/bf16[320,128,128]{2,1,0:T(8,128...) while((s32[]{:T(128)}, f32[512,32,128]{2,0,1:T(8,128)}, s32[]{:T(128)}, ...), condition=%wide.region_6.7_spmd.clone, body=%wide.region_4.6_spmd.clone.sunk | while | flops 541068864 | bytes 66076860 | solution.py:29
  773.5 9.0 copy.42
  783.2 18.3 %scatter_fusion.1 = f32[512,32,128]{2,0,1:T(8,128)} fusion(f32[512,32,128]{2,0,1:T(8,128)} %get-tuple-element.362, s32[32]{0:T(128)S(1)} %fusion.61, f32[32,512,128]{2,1,0:T(8,128)} %copy.42), kind=kCustom, calls=%fused_computation.11.clone.clone.1 | custom fusion | flops 2097152 | bytes 25165952 | tf_op jit(solution)/shard_map/while/body/scatter-add | solution.py:27
  821.9 9.0 copy.42
  831.6 18.7 %scatter_fusion.1 = f32[512,32,128]{2,0,1:T(8,128)} fusion(f32[512,32,128]{2,0,1:T(8,128)} %get-tuple-element.362, s32[32]{0:T(128)S(1)} %fusion.61, f32[32,512,128]{2,1,0:T(8,128)} %copy.42), kind=kCustom, calls=%fused_computation.11.clone.clone.1 | custom fusion | flops 2097152 | bytes 25165952 | tf_op jit(solution)/shard_map/while/body/scatter-add | solution.py:27
  870.6 9.0 copy.42
  880.3 18.6 %scatter_fusion.1 = f32[512,32,128]{2,0,1:T(8,128)} fusion(f32[512,32,128]{2,0,1:T(8,128)} %get-tuple-element.362, s32[32]{0:T(128)S(1)} %fusion.61, f32[32,512,128]{2,1,0:T(8,128)} %copy.42), kind=kCustom, calls=%fused_computation.11.clone.clone.1 | custom fusion | flops 2097152 | bytes 25165952 | tf_op jit(solution)/shard_map/while/body/scatter-add | solution.py:27
  906.7 455.9 %reduce-scatter.5.cloned.1.call-done = f32[512,512]{1,0:T(8,128)} async-done(((f32[512,4096]{1,0:T(8,128)}), f32[512,512]{1,0:T(8,128)}) %reduce-scatter.5.cloned.1.call-update) | async-done | bytes 1048592 | tf_op jit(solution)/shard_map/reduce_scatter | solution.py:51
  (218 shorter events, 332.7 us)
Async XLA Ops:
  6.5 57.2 %all-gather.6.cloned.1.call-start = ((), (), s32[]{:S(2)}) async-start(), calls=%async_computation.5 | async-start | bytes 8912896 | tf_op jit(solution)/shard_map/all_gather | solution.py:46
  8.6 679.0 %reduce-scatter.3.cloned.1.call-start = ((), (), s32[]{:S(2)}) async-start(), calls=%async_computation.2 | async-start | bytes 9437184 | tf_op jit(solution)/shard_map/reduce_scatter | solution.py:51
  572.6 0.7 copy-start
  572.6 167.1 %all-gather.4.cloned.1.call-start = ((), (), s32[]{:S(2)}) async-start(), calls=%async_computation.3 | async-start | bytes 8912896 | tf_op jit(solution)/shard_map/all_gather | solution.py:46
  689.8 672.8 %reduce-scatter.5.cloned.1.call-start = ((), (), s32[]{:S(2)}) async-start(), calls=%async_computation.4 | async-start | bytes 9437184 | tf_op jit(solution)/shard_map/reduce_scatter | solution.py:51
Sparse Core Ops, SparseCore 0:
  9.1 54.6 all-gather.5
  572.8 114.8 reduce-scatter.2
  689.9 49.7 all-gather.3
  906.8 455.7 reduce-scatter.4
where the time goes:
time: 1380 us; the launch traced here: 1370 us
  waiting for transfers between devices  655 us (47%)
  local copies, waits for them, and re-layouts  355 us (26%)
  other arithmetic  254 us (18%)
  matrix products  91.7 us (7%)
  between operations  14.3 us (1%)
    reduce_scatter x2, waiting for transfers between devices, on_device(): lax.psum_scatter(summed.reshape(batch_rows, out_width), 'col', scatter_di...  570 us
    scatter-add x13, other arithmetic, advance(): return inner.at[:, slot_cols[picked], :].add(product)  241 us
    select_n x13, local copies, waits for them, and re-layouts, advance(): jnp.where(live_slot[None, :, None], product, jnp.zeros_like(product))  116 us
    dot_general x13, matrix products, advance(): jnp.einsum('bgi,gij->bgj', left_rows, blocks, preferred_element_type=jnp....  91.7 us
    all_gather x2, waiting for transfers between devices, on_device(): panel_full = lax.all_gather(current[:, 0, :], 'row', axis=1, tiled=True)  85.1 us
    gather x13, local copies, waits for them, and re-layouts, advance(): left_rows = panel_blocks[:, local_rows, :]  83.6 us
    gather x13, local copies, waits for them, and re-layouts, advance(): blocks = values[picked]  61.4 us
  transfers between devices with their start and end apart: 4, of which 4 were waited for; matrix products, arithmetic and copies ran while one was open for 1% of the time, Pallas kernels for 0%

commit v1 on v0

v1 whole, which is shorter than its diff:
```python
import functools

import jax
import jax.numpy as jnp
from jax import lax
from jax.experimental import pallas as pl
from jax.experimental.pallas import tpu as pltpu
from jax.sharding import PartitionSpec as P

BLK = 128
CB = 32
N_ROW = 16
N_COL = 8
N_X = 4
N_Y = 4
SUB = CB // N_COL
GROUP = 32
UNROLL = 16
HEIGHTS = (256, 256)
GATHER = 'sc'
GATE = False
ORDER = True
STEPS = 16.0
TOP = 32000.0
VMEM = pl.BlockSpec(memory_space=pltpu.VMEM)
SMEM = pl.BlockSpec(memory_space=pltpu.SMEM)
ANY = pl.BlockSpec(memory_space=pl.ANY)
HBM = pl.BlockSpec(memory_space=pltpu.HBM)

TO_Z_LO = [(r, r ^ 2) for r in range(N_ROW)]
TO_CORE = [(r, r ^ 1) for r in range(N_ROW)]
TO_Z_HI = [(c, c ^ 4) for c in range(N_COL)]


def from_x(d):
    return [(r, (r - 4 * d) % N_ROW) for r in range(N_ROW)]


def to_y(d):
    return [(c, (c & 4) + ((c + d) & 3)) for c in range(N_COL)]


def product_kernel(n_parts, layer, place, col, info, *refs):
    parts, (values, *refs) = refs[:n_parts], refs[n_parts:]
    *outs, panel, held, acc, part_sems, sems = refs[-N_COL - 5 :]
    height = panel.shape[1]
    count = info[0]
    groups = (count + GROUP - 1) // GROUP

    def weights(group):
        spot = pl.ds(group * GROUP, GROUP)
        return pltpu.make_async_copy(values.at[layer, 0, 0, spot], held.at[spot], sems.at[group])

    copies = [
        pltpu.make_async_copy(
            part, panel if len(part.shape) == 3 else panel.at[i], part_sems.at[i]
        )
        for i, part in enumerate(parts)
    ]
    for copy in copies:
        copy.start()

    def begin(group, _):
        weights(group).start()
        return 0

    lax.fori_loop(0, groups, begin, 0)
    acc[...] = jnp.zeros_like(acc)
    for copy in copies:
        copy.wait()

    def one_group(group, _):
        weights(group).wait()

        def one_step(step, _):
            for u in range(UNROLL):
                slot = group * GROUP + step * UNROLL + u
                where_at = place[slot]
                lanes = pl.ds(pl.multiple_of((where_at & (SUB - 1)) * BLK, BLK), BLK)
                left = panel[where_at >> 2, :, lanes]
                acc[col[slot]] += jnp.dot(left, held[slot], preferred_element_type=jnp.float32)
            return 0

        steps = (jnp.minimum(count - group * GROUP, GROUP) + UNROLL - 1) // UNROLL
        return lax.fori_loop(0, steps, one_step, 0)

    lax.fori_loop(0, groups, one_group, 0)

    for e in range(2):
        for d in range(N_Y):
            share = (info[1] ^ e) * N_Y + ((info[2] + d) & 3)
            encode(lambda t, share=share: acc[share * SUB + t], outs[e * N_Y + d], height)


def encode(sums_of, out, height):
    codes = []
    for t in range(SUB):
        sums = sums_of(t)
        most = jnp.max(jnp.abs(sums), axis=0, keepdims=True)
        code = jnp.ceil(jnp.log2(jnp.maximum(most, 1e-30)) * STEPS)
        codes.append(code)
        inverse = TOP * jnp.exp2(code * (-1.0 / STEPS))
        whole = jnp.round(sums * inverse).astype(jnp.int32)
        out[pl.ds(t * height, height), :] = whole.astype(jnp.int16)
    codes = jnp.concatenate(codes + [jnp.zeros((16 - SUB, BLK), jnp.float32)], axis=0)
    out[pl.ds(SUB * height, 16), :] = codes.astype(jnp.int32).astype(jnp.int16)


def product_vmem(height, slots):
    panel = N_ROW * height * SUB * BLK * 2
    totals = (CB + 1) * height * BLK * 4
    outs = N_COL * (SUB * height + 16) * BLK * 2
    return panel + totals + outs + slots * BLK * BLK * 2 + (3 << 20)


def product(layer, place, col, info, parts, values, height, after):
    slots = values.shape[3]
    piece = jax.ShapeDtypeStruct((SUB * height + 16, BLK), jnp.int16)
    return pl.pallas_call(
        functools.partial(product_kernel, len(parts), layer),
        out_shape=(piece,) * N_COL,
        in_specs=[SMEM] * 3 + [HBM] * (len(parts) + 1) + [ANY] * len(after),
        out_specs=(VMEM,) * N_COL,
        scratch_shapes=[
            pltpu.VMEM((N_ROW, height, SUB * BLK), jnp.bfloat16),
            pltpu.VMEM((slots, BLK, BLK), jnp.bfloat16),
            pltpu.VMEM((CB + 1, height, BLK), jnp.float32),
            pltpu.SemaphoreType.DMA((len(parts),)),
            pltpu.SemaphoreType.DMA((slots // GROUP,)),
        ],
        compiler_params=pltpu.CompilerParams(vmem_limit_bytes=58 * 1024 * 1024),
        cost_estimate=pl.CostEstimate(
            flops=4 * 2 * height * BLK * BLK * slots,
            bytes_accessed=slots * BLK * BLK * 2,
            transcendentals=0,
        ),
        name="product",
    )(place, col, info, *parts, values, *after)


def rows_at_once(height):
    return next(r for r in (64, 48, 32, 16) if height % r == 0)


def scales_of(piece, height):
    codes = piece[pl.ds(SUB * height, 16), :].astype(jnp.int32).astype(jnp.float32)
    return jnp.exp2(codes * (1.0 / STEPS)) * (1.0 / TOP)


def add_pieces(pieces, scales, t, spot):
    total = None
    for piece, scale in zip(pieces, scales):
        term = piece[spot, :].astype(jnp.int32).astype(jnp.float32) * scale[t : t + 1, :]
        total = term if total is None else total + term
    return total


def middle_kernel(a, b, c, d, out, totals):
    height = totals.shape[0]
    rows = rows_at_once(height)
    pieces = (a, b, c, d)
    scales = [scales_of(piece, height) for piece in pieces]
    codes = []
    for t in range(SUB):

        def add(i, most, t=t):
            first = pl.multiple_of(i * rows, rows)
            total = add_pieces(pieces, scales, t, pl.ds(t * height + first, rows))
            totals[pl.ds(first, rows), :] = total
            return jnp.maximum(most, jnp.max(jnp.abs(total).reshape(rows // 8, 8, BLK), axis=0))

        most = lax.fori_loop(0, height // rows, add, jnp.zeros((8, BLK), jnp.float32))
        most = jnp.max(most, axis=0, keepdims=True)
        code = jnp.ceil(jnp.log2(jnp.maximum(most, 1e-30)) * STEPS)
        codes.append(code)
        inverse = TOP * jnp.exp2(code * (-1.0 / STEPS))

        def store(i, _, t=t, inverse=inverse):
            first = pl.multiple_of(i * rows, rows)
            whole = jnp.round(totals[pl.ds(first, rows), :] * inverse).astype(jnp.int32)
            out[pl.ds(t * height + first, rows), :] = whole.astype(jnp.int16)
            return 0

        lax.fori_loop(0, height // rows, store, 0)
    codes = jnp.concatenate(codes + [jnp.zeros((16 - SUB, BLK), jnp.float32)], axis=0)
    out[pl.ds(SUB * height, 16), :] = codes.astype(jnp.int32).astype(jnp.int16)


def middle(pieces):
    height = (pieces[0].shape[0] - 16) // SUB
    return pl.pallas_call(
        middle_kernel,
        out_shape=jax.ShapeDtypeStruct(pieces[0].shape, jnp.int16),
        in_specs=[VMEM] * 4,
        out_specs=VMEM,
        scratch_shapes=[pltpu.VMEM((height, BLK), jnp.float32)],
        cost_estimate=pl.CostEstimate(
            flops=16 * pieces[0].size, bytes_accessed=8 * pieces[0].size, transcendentals=0
        ),
        name="middle",
    )(*pieces)


def add_and_clip(pieces, bias, out, height):
    rows = rows_at_once(height)
    scales = [scales_of(piece, height) for piece in pieces]
    for t in range(SUB):
        lanes = slice(t * BLK, (t + 1) * BLK)

        def part(i, _, t=t, lanes=lanes):
            first = pl.multiple_of(i * rows, rows)
            total = add_pieces(pieces, scales, t, pl.ds(t * height + first, rows)) + bias[:, lanes]
            kept = jnp.minimum(jnp.maximum(total, 0.0), 32.0)
            out[pl.ds(first, rows), lanes] = kept.astype(jnp.bfloat16)
            return 0

        lax.fori_loop(0, height // rows, part, 0)


def combine_kernel(a, b, c, d, other, bias, out, kept, sem):
    add_and_clip((a, b, c, d, other), bias, kept, kept.shape[0])
    copy = pltpu.make_async_copy(kept, out, sem)
    copy.start()
    copy.wait()


def finish_kernel(first, a, b, c, d, other, bias, *refs):
    out, kept, sem = refs[-3:]
    pieces = (a, b, c, d, other)
    add_and_clip(pieces, bias, kept, kept.shape[0])
    copy = pltpu.make_async_copy(kept, out.at[pl.ds(first, kept.shape[0])], sem)
    copy.start()
    copy.wait()


def combine(pieces, other, bias):
    height = (other.shape[0] - 16) // SUB
    return pl.pallas_call(
        combine_kernel,
        out_shape=jax.ShapeDtypeStruct((height, SUB * BLK), jnp.bfloat16),
        in_specs=[VMEM] * 6,
        out_specs=HBM,
        scratch_shapes=[
            pltpu.VMEM((height, SUB * BLK), jnp.bfloat16),
            pltpu.SemaphoreType.DMA,
        ],
        cost_estimate=pl.CostEstimate(
            flops=16 * other.size, bytes_accessed=10 * other.size, transcendentals=0
        ),
        name="combine",
    )(*pieces, other, bias)


def finish(pieces, other, bias, first, batch, earlier):
    height = (other.shape[0] - 16) // SUB
    more = [] if earlier is None else [earlier]
    return pl.pallas_call(
        functools.partial(finish_kernel, first),
        out_shape=jax.ShapeDtypeStruct((batch, SUB * BLK), jnp.bfloat16),
        in_specs=[VMEM] * 6 + [ANY] * len(more),
        out_specs=ANY,
        scratch_shapes=[
            pltpu.VMEM((height, SUB * BLK), jnp.bfloat16),
            pltpu.SemaphoreType.DMA,
        ],
        input_output_aliases={6: 0} if more else {},
        cost_estimate=pl.CostEstimate(
            flops=16 * other.size, bytes_accessed=10 * other.size, transcendentals=0
        ),
        name="finish",
    )(*pieces, other, bias, *more)


def take_kernel(first, whole, *refs):
    out, held, sem = refs[-3:]
    rows = pl.ds(first, out.shape[0])
    for copy in (
        pltpu.make_async_copy(whole.at[rows], held, sem),
        pltpu.make_async_copy(held, out, sem),
    ):
        copy.start()
        copy.wait()


def take(whole, first, height, after):
    return pl.pallas_call(
        functools.partial(take_kernel, first),
        out_shape=jax.ShapeDtypeStruct((height,) + whole.shape[1:], whole.dtype),
        in_specs=[ANY] * (1 + len(after)),
        out_specs=HBM,
        scratch_shapes=[
            pltpu.VMEM((height,) + whole.shape[1:], whole.dtype),
            pltpu.SemaphoreType.DMA,
        ],
        name="take",
    )(whole, *after)


def gather(current, gate):
    if GATHER == "sc":
        return [lax.all_gather(current, "row", axis=0, tiled=False)]
    near = [current] + [lax.ppermute(current, "row", from_x(d)) for d in range(1, N_X)]
    other = lax.ppermute(current, "row", TO_Z_LO)
    if gate:
        other = take(other, 0, other.shape[0], gate)
    far = [other] + [lax.ppermute(other, "row", from_x(d)) for d in range(1, N_X)]
    mine = [part for both in zip(near, far) for part in both]
    return mine + [lax.ppermute(part, "row", TO_CORE) for part in mine]


def on_device(features, block_values, block_rows, block_cols, block_counts, bias):
    layers, slots = block_values.shape[0], block_values.shape[3]
    batch = features.shape[0]
    here, there = lax.axis_index("row"), lax.axis_index("col")
    counts = block_counts[:, 0, 0]
    live = jnp.arange(slots, dtype=jnp.int32)[None, :] < counts[:, None]
    col = jnp.where(live, block_cols[:, 0, 0], CB)
    absolute = block_rows[:, 0, 0]
    shard, sub = absolute >> 2, absolute & 3
    apart_x = ((shard >> 2) - (here >> 2)) & 3
    apart_z = ((shard >> 1) ^ (here >> 1)) & 1
    apart_core = (shard ^ here) & 1
    place = (((apart_core * 4 + apart_x) * 2 + apart_z) << 2) + sub
    firsts = [sum(HEIGHTS[:c]) for c in range(len(HEIGHTS))]
    whole = features[:, 0, :]
    current = []
    result = None
    for layer in range(layers):
        info = jnp.stack([counts[layer], there >> 2, there & 3])
        after, gate, earlier = [], [], []
        for c, height in enumerate(HEIGHTS):
            if layer == 0:
                current.append(take(whole, firsts[c], height, after))
            parts = gather(current[c], gate)
            after = [] if GATHER == 'sc' else parts[3 : N_ROW // 2 : 2]
            sums = product(
                layer, (absolute if GATHER == 'sc' else place)[layer], col[layer], info, parts, block_values, height, earlier
            )
            gate = [sums[0]] if GATE else []
            away = [sums[N_Y]] + [
                lax.ppermute(sums[N_Y + d], "col", to_y(d)) for d in range(1, N_Y)
            ]
            sent = middle(away)
            earlier = [sent] if ORDER else []
            other = lax.ppermute(sent, "col", TO_Z_HI)
            pieces = [sums[0]] + [lax.ppermute(sums[d], "col", to_y(d)) for d in range(1, N_Y)]
            if layer < layers - 1:
                current[c] = combine(pieces, other, bias[layer])
            else:
                result = finish(pieces, other, bias[layer], firsts[c], batch, result)
    return result[:, None, :]


def solution(mesh):
    in_specs = (
        P(None, "col", "row"),
        P(None, "row", "col", None, None, None),
        P(None, "row", "col", None),
        P(None, "row", "col", None),
        P(None, "row", "col"),
        P(None, "col", "row"),
    )
    out_specs = P(None, "col", "row")
    return jax.shard_map(
        on_device, mesh=mesh, in_specs=in_specs, out_specs=out_specs, check_vma=False
    )
```

time: 1380 us -> 241 us (0.17)
  waiting for transfers between devices: 655 us -> 96.9 us
  local copies, waits for them, and re-layouts: 355 us -> 9.58 us
  other arithmetic: 254 us -> 3.37 us
  matrix products: 91.7 us -> 0 us
  Pallas kernels: 0 us -> 69.1 us
  starting transfers between devices: 0.13 us -> 46.1 us
    reduce_scatter x2 -> x0, waiting for transfers between devices: 570 us -> none  [on_device(): lax.psum_scatter(summed.reshape(batch_rows, out_width), 'col', scatter_di...]
    scatter-add x13 -> x0, other arithmetic: 241 us -> none  [advance(): return inner.at[:, slot_cols[picked], :].add(product)]
    gather x65 -> x0, local copies, waits for them, and re-layouts: 173 us -> none  [the longest x13 83.6 us: advance(): left_rows = panel_blocks[:, local_rows, :]]
    select_n x13 -> x0, local copies, waits for them, and re-layouts: 116 us -> none  [advance(): jnp.where(live_slot[None, :, None], product, jnp.zeros_like(product))]
    dot_general x13 -> x0, matrix products: 91.7 us -> none  [advance(): jnp.einsum('bgi,gij->bgj', left_rows, blocks, preferred_element_type=jnp....]
    pallas_call x0 -> x14, Pallas kernels: none -> 69.1 us  [the longest x4 45.8 us: product(): pl.pallas_call(functools.partial(product_kernel, len(parts), layer), out_...]
    ppermute x0 -> x28, waiting for transfers between devices: none -> 58.5 us  [the longest x12 37.7 us: on_device(): lax.ppermute(sums[N_Y + d], 'col', to_y(d))]
    all_gather x2 -> x4, waiting for transfers between devices: 85.1 us -> 38.4 us  [gather(): return [lax.all_gather(current, 'row', axis=0, tiled=False)]]
  transfers between devices with their start and end apart: 4 -> 32, of which waited for: 4 -> 19; matrix products, arithmetic and copies ran while one was open for 1% -> 3% of each run, Pallas kernels for 0% -> 23%
where the time goes in v1:
time: 241 us; the launch traced here: 238 us
  waiting for transfers between devices  96.9 us (40%)
  Pallas kernels  69.1 us (29%)
  starting transfers between devices  46.1 us (19%)
  between operations  13.4 us (6%)
  local copies, waits for them, and re-layouts  9.58 us (4%)
  other arithmetic  3.37 us (1%)
    pallas_call x4, Pallas kernels, product(): pl.pallas_call(functools.partial(product_kernel, len(parts), layer), out_...  45.8 us
    all_gather x4, waiting for transfers between devices, gather(): return [lax.all_gather(current, 'row', axis=0, tiled=False)]  38.4 us
    ppermute x12, waiting for transfers between devices, on_device(): lax.ppermute(sums[N_Y + d], 'col', to_y(d))  37.7 us
    ppermute x12, starting transfers between devices, on_device(): lax.ppermute(sums[N_Y + d], 'col', to_y(d))  24 us
    ppermute x12, starting transfers between devices, on_device(): lax.ppermute(sums[d], 'col', to_y(d))  14.1 us
    ppermute x12, waiting for transfers between devices, on_device(): lax.ppermute(sums[d], 'col', to_y(d))  13.2 us
    pallas_call x4, Pallas kernels, middle(): pl.pallas_call(middle_kernel, out_shape=jax.ShapeDtypeStruct(pieces[0].sh...  9.97 us
    ppermute x4, starting transfers between devices, on_device(): other = lax.ppermute(sent, 'col', TO_Z_HI)  7.89 us
  transfers between devices with their start and end apart: 32, of which 19 were waited for; matrix products, arithmetic and copies ran while one was open for 3% of the time, Pallas kernels for 23%

profile of v1, /device:TPU:0, one launch (start us, length us, event | category | flops | bytes accessed | tf_op | source)
XLA Modules:
  0.0 238.4 jit_solution(4048893323063367826)
XLA Ops:
  15.3 33.7 %all-gather.11.cloned.1.call-done = bf16[4096,512]{1,0:T(8,128)(2,1)} async-done(((bf16[256,512]{1,0:T(8,128)(2,1)}), bf16[4096,512]{1,0:T(8,128)(2,1)}) %all-gather.11.cloned.1.call-update) | async-done | bytes 4194320 | tf_op jit(solution)/shard_map/all_gather | solution.py:301
  49.0 14.0 %product.4 = (s16[1040,128]{1,0:T(8,128)(2,1)}, s16[1040,128]{1,0:T(8,128)(2,1)}, s16[1040,128]{1,0:T(8,128)(2,1)}, s16[1040,128]{1,0:T(8,128)(2,1)}, s16[1040,1...) custom-call(s32[320]{0:T(512)} %get-tuple-element.71.place, ...), custom_call_target="tpu_custom_call" | custom-call | flops 10737418240 | bytes 10485760 | tf_op jit(solution)/shard_map/product/pallas_call | solution.py:119
  69.3 10.3 %collective-permute-done.b = s16[1040,128]{1,0:T(8,128)(2,1)S(1)} collective-permute-done((s16[1040,128]{1,0:T(8,128)(2,1)}, s16[1040,128]{1,0:T(8,128)(2,1)S(1)}, u32[]{:S(2)}, u32[]{:S(2)}) %collective-permute-start) | collective-permute-done | bytes 266272 | tf_op jit(solution)/shard_map/ppermute | solution.py:341
  81.2 2.5 %middle.4.refs_2_ = s16[1040,128]{1,0:T(8,128)(2,1)} custom-call(s16[1040,128]{1,0:T(8,128)(2,1)} %get-tuple-element.37.a, s16[1040,128]{1,0:T(8,128)(2,1)} %copy-done.16, s16[1040,128]{1,0:T(8,128)(2,1)} %copy-done.18, s16[1040,128]{1,0:T(8,128)(2,1)} %copy-done.20), custom_call_target="tpu_custom_call" | custom-call | flops 2129920 | bytes 1064960 | tf_op jit(solution)/shard_map/middle/pallas_call | solution.py:191
  84.3 4.6 %collective-permute-done.10.b = s16[1040,128]{1,0:T(8,128)(2,1)S(1)} collective-permute-done((s16[1040,128]{1,0:T(8,128)(2,1)}, s16[1040,128]{1,0:T(8,128)(2,1)S(1)}, u32[]{:S(2)}, u32[]{:S(2)}) %collective-permute-start.10) | collective-permute-done | bytes 266272 | tf_op jit(solution)/shard_map/ppermute | solution.py:346
  89.5 3.4 %collective-permute-done.13.other = s16[1040,128]{1,0:T(8,128)(2,1)S(1)} collective-permute-done((s16[1040,128]{1,0:T(8,128)(2,1)}, s16[1040,128]{1,0:T(8,128)(2,1)S(1)}, u32[]{:S(2)}, u32[]{:S(2)}) %collective-permute-start.13) | collective-permute-done | bytes 266272 | tf_op jit(solution)/shard_map/ppermute | solution.py:345
  93.6 2.5 %combine.3 = bf16[256,512]{1,0:T(8,128)(2,1)} custom-call(s16[1040,128]{1,0:T(8,128)(2,1)} %get-tuple-element.49.a, s16[1040,128]{1,0:T(8,128)(2,1)} %copy-done, s16[1040,128]{1,0:T(8,128)(2,1)} %copy-done.2, s16[1040,128]{1,0:T(8,128)(2,1)} %copy-done.4, s16[1040,128]{1,0:T(8,128)(2,1)} %copy-done.6, f32[1,512]{1,0:T(1,128)} %get-tuple-element.74.bias), custom_call_target="tpu_custom_call" | custom-call | flops 2129920 | bytes 1331200 | tf_op jit(solution)/shard_map/combine/pallas_call | solution.py:238
  96.2 13.9 %product.5 = (s16[1040,128]{1,0:T(8,128)(2,1)}, s16[1040,128]{1,0:T(8,128)(2,1)}, s16[1040,128]{1,0:T(8,128)(2,1)}, s16[1040,128]{1,0:T(8,128)(2,1)}, s16[1040,1...) custom-call(s32[320]{0:T(512)} %get-tuple-element.71.place, ...), custom_call_target="tpu_custom_call" | custom-call | flops 10737418240 | bytes 10485760 | tf_op jit(solution)/shard_map/product/pallas_call | solution.py:119
  110.2 3.1 %collective-permute-start.7 = (s16[1040,128]{1,0:T(8,128)(2,1)}, s16[1040,128]{1,0:T(8,128)(2,1)S(1)}, u32[]{:S(2)}, u32[]{:S(2)}) collective-permute-start(s16[1040,128]{1,0:T(8,128)(2,1)} %get-tuple-element.47), channel_id=1, source_target_pairs={{0,2},{1,3},{2,0},{3,1},{4,6},{5,7},{6,4},{7,5},{8,10},{9,11},{10,... | collective-permute-start | bytes 798728 | tf_op jit(solution)/shard_map/ppermute | solution.py:341
  116.3 10.3 %collective-permute-done.6.b = s16[1040,128]{1,0:T(8,128)(2,1)S(1)} collective-permute-done((s16[1040,128]{1,0:T(8,128)(2,1)}, s16[1040,128]{1,0:T(8,128)(2,1)S(1)}, u32[]{:S(2)}, u32[]{:S(2)}) %collective-permute-start.6) | collective-permute-done | bytes 266272 | tf_op jit(solution)/shard_map/ppermute | solution.py:341
  128.2 2.5 %middle.5 = s16[1040,128]{1,0:T(8,128)(2,1)} custom-call(s16[1040,128]{1,0:T(8,128)(2,1)} %get-tuple-element.45.a, s16[1040,128]{1,0:T(8,128)(2,1)} %copy-done.17, s16[1040,128]{1,0:T(8,128)(2,1)} %copy-done.19, s16[1040,128]{1,0:T(8,128)(2,1)} %copy-done.21), custom_call_target="tpu_custom_call" | custom-call | flops 2129920 | bytes 1064960 | tf_op jit(solution)/shard_map/middle/pallas_call | solution.py:191
  130.7 3.3 %collective-permute-done.3.b = s16[1040,128]{1,0:T(8,128)(2,1)S(1)} collective-permute-done((s16[1040,128]{1,0:T(8,128)(2,1)}, s16[1040,128]{1,0:T(8,128)(2,1)S(1)}, u32[]{:S(2)}, u32[]{:S(2)}) %collective-permute-start.3) | collective-permute-done | bytes 266272 | tf_op jit(solution)/shard_map/ppermute | solution.py:346
  134.7 4.1 %collective-permute-done.9.other = s16[1040,128]{1,0:T(8,128)(2,1)S(1)} collective-permute-done((s16[1040,128]{1,0:T(8,128)(2,1)}, s16[1040,128]{1,0:T(8,128)(2,1)S(1)}, u32[]{:S(2)}, u32[]{:S(2)}) %collective-permute-start.9) | collective-permute-done | bytes 266272 | tf_op jit(solution)/shard_map/ppermute | solution.py:345
  139.6 2.5 %combine.2 = bf16[256,512]{1,0:T(8,128)(2,1)} custom-call(s16[1040,128]{1,0:T(8,128)(2,1)} %get-tuple-element.41.a, s16[1040,128]{1,0:T(8,128)(2,1)} %copy-done.1, s16[1040,128]{1,0:T(8,128)(2,1)} %copy-done.3, s16[1040,128]{1,0:T(8,128)(2,1)} %copy-done.5, s16[1040,128]{1,0:T(8,128)(2,1)} %copy-done.7, f32[1,512]{1,0:T(1,128)} %get-tuple-element.74.bias), custom_call_target="tpu_custom_call" | custom-call | flops 2129920 | bytes 1331200 | tf_op jit(solution)/shard_map/combine/pallas_call | solution.py:238
  143.5 8.8 %product.6 = (s16[1040,128]{1,0:T(8,128)(2,1)}, s16[1040,128]{1,0:T(8,128)(2,1)}, s16[1040,128]{1,0:T(8,128)(2,1)}, s16[1040,128]{1,0:T(8,128)(2,1)}, s16[1040,1...) custom-call(s32[320]{0:T(512)} %get-tuple-element.72.place, ...), custom_call_target="tpu_custom_call" | custom-call | flops 10737418240 | bytes 10485760 | tf_op jit(solution)/shard_map/product/pallas_call | solution.py:119
  152.3 6.2 %collective-permute-start.14 = (s16[1040,128]{1,0:T(8,128)(2,1)}, s16[1040,128]{1,0:T(8,128)(2,1)S(1)}, u32[]{:S(2)}, u32[]{:S(2)}) collective-permute-start(s16[1040,128]{1,0:T(8,128)(2,1)} %get-tuple-element.54), channel_id=1, source_target_pairs={{0,1},{1,2},{2,3},{3,0},{4,5},{5,6},{6,7},{7,4},{8,9},{9,10},{10,1... | collective-permute-start | bytes 798728 | tf_op jit(solution)/shard_map/ppermute | solution.py:341
  158.6 2.8 %collective-permute-start.16 = (s16[1040,128]{1,0:T(8,128)(2,1)}, s16[1040,128]{1,0:T(8,128)(2,1)S(1)}, u32[]{:S(2)}, u32[]{:S(2)}) collective-permute-start(s16[1040,128]{1,0:T(8,128)(2,1)} %get-tuple-element.56), channel_id=1, source_target_pairs={{0,3},{1,0},{2,1},{3,2},{4,7},{5,4},{6,5},{7,6},{8,11},{9,8},{10,9... | collective-permute-start | bytes 798728 | tf_op jit(solution)/shard_map/ppermute | solution.py:341
  161.3 2.8 %collective-permute-done.14.b = s16[1040,128]{1,0:T(8,128)(2,1)S(1)} collective-permute-done((s16[1040,128]{1,0:T(8,128)(2,1)}, s16[1040,128]{1,0:T(8,128)(2,1)S(1)}, u32[]{:S(2)}, u32[]{:S(2)}) %collective-permute-start.14) | collective-permute-done | bytes 266272 | tf_op jit(solution)/shard_map/ppermute | solution.py:341
  164.1 4.9 %collective-permute-done.15.c = s16[1040,128]{1,0:T(8,128)(2,1)S(1)} collective-permute-done((s16[1040,128]{1,0:T(8,128)(2,1)}, s16[1040,128]{1,0:T(8,128)(2,1)S(1)}, u32[]{:S(2)}, u32[]{:S(2)}) %collective-permute-start.15) | collective-permute-done | bytes 266272 | tf_op jit(solution)/shard_map/ppermute | solution.py:341
  170.6 2.5 %middle.6.refs_2_ = s16[1040,128]{1,0:T(8,128)(2,1)} custom-call(s16[1040,128]{1,0:T(8,128)(2,1)} %get-tuple-element.53.a, s16[1040,128]{1,0:T(8,128)(2,1)} %copy-done.22, s16[1040,128]{1,0:T(8,128)(2,1)} %copy-done.23, s16[1040,128]{1,0:T(8,128)(2,1)} %copy-done.24), custom_call_target="tpu_custom_call" | custom-call | flops 2129920 | bytes 1064960 | tf_op jit(solution)/shard_map/middle/pallas_call | solution.py:191
  173.1 4.6 %all-gather.13.cloned.1.call-done = bf16[4096,512]{1,0:T(8,128)(2,1)} async-done(((bf16[256,512]{1,0:T(8,128)(2,1)}), bf16[4096,512]{1,0:T(8,128)(2,1)}) %all-gather.13.cloned.1.call-update) | async-done | bytes 4194320 | tf_op jit(solution)/shard_map/all_gather | solution.py:301
  177.7 9.0 %product.7 = (s16[1040,128]{1,0:T(8,128)(2,1)}, s16[1040,128]{1,0:T(8,128)(2,1)}, s16[1040,128]{1,0:T(8,128)(2,1)}, s16[1040,128]{1,0:T(8,128)(2,1)}, s16[1040,1...) custom-call(s32[320]{0:T(512)} %get-tuple-element.72.place, ...), custom_call_target="tpu_custom_call" | custom-call | flops 10737418240 | bytes 10485760 | tf_op jit(solution)/shard_map/product/pallas_call | solution.py:119
  186.7 5.6 %collective-permute-start.20 = (s16[1040,128]{1,0:T(8,128)(2,1)}, s16[1040,128]{1,0:T(8,128)(2,1)S(1)}, u32[]{:S(2)}, u32[]{:S(2)}) collective-permute-start(s16[1040,128]{1,0:T(8,128)(2,1)} %get-tuple-element.62), channel_id=1, source_target_pairs={{0,1},{1,2},{2,3},{3,0},{4,5},{5,6},{6,7},{7,4},{8,9},{9,10},{10,1... | collective-permute-start | bytes 798728 | tf_op jit(solution)/shard_map/ppermute | solution.py:341
  192.3 2.8 %collective-permute-start.22 = (s16[1040,128]{1,0:T(8,128)(2,1)}, s16[1040,128]{1,0:T(8,128)(2,1)S(1)}, u32[]{:S(2)}, u32[]{:S(2)}) collective-permute-start(s16[1040,128]{1,0:T(8,128)(2,1)} %get-tuple-element.64), channel_id=1, source_target_pairs={{0,3},{1,0},{2,1},{3,2},{4,7},{5,4},{6,5},{7,6},{8,11},{9,8},{10,9... | collective-permute-start | bytes 798728 | tf_op jit(solution)/shard_map/ppermute | solution.py:341
  195.1 2.8 %collective-permute-start.25 = (s16[1040,128]{1,0:T(8,128)(2,1)S(1)}, s16[1040,128]{1,0:T(8,128)(2,1)S(1)}, u32[]{:S(2)}, u32[]{:S(2)}) collective-permute-start(s16[1040,128]{1,0:T(8,128)(2,1)S(1)} %copy-done.31), channel_id=1, source_target_pairs={{0,2},{1,3},{2,0},{3,1},{4,6},{5,7},{6,4},{7,5},{8,10},{9,11},{10,... | collective-permute-start | bytes 798728 | tf_op jit(solution)/shard_map/ppermute | solution.py:346
  199.1 5.7 %collective-permute-done.21.c = s16[1040,128]{1,0:T(8,128)(2,1)S(1)} collective-permute-done((s16[1040,128]{1,0:T(8,128)(2,1)}, s16[1040,128]{1,0:T(8,128)(2,1)S(1)}, u32[]{:S(2)}, u32[]{:S(2)}) %collective-permute-start.21) | collective-permute-done | bytes 266272 | tf_op jit(solution)/shard_map/ppermute | solution.py:341
  204.8 5.0 %collective-permute-start.27 = (s16[1040,128]{1,0:T(8,128)(2,1)S(1)}, s16[1040,128]{1,0:T(8,128)(2,1)S(1)}, u32[]{:S(2)}, u32[]{:S(2)}) collective-permute-start(s16[1040,128]{1,0:T(8,128)(2,1)S(1)} %copy-done.8), channel_id=1, source_target_pairs={{0,4},{1,5},{2,6},{3,7},{4,0},{5,1},{6,2},{7,3},{8,12},{9,13},{10,... | collective-permute-start | bytes 798728 | tf_op jit(solution)/shard_map/ppermute | solution.py:345
  210.5 2.5 %middle.7 = s16[1040,128]{1,0:T(8,128)(2,1)} custom-call(s16[1040,128]{1,0:T(8,128)(2,1)} %get-tuple-element.61.a, s16[1040,128]{1,0:T(8,128)(2,1)} %copy-done.13, s16[1040,128]{1,0:T(8,128)(2,1)} %copy-done.14, s16[1040,128]{1,0:T(8,128)(2,1)} %copy-done.15), custom_call_target="tpu_custom_call" | custom-call | flops 2129920 | bytes 1064960 | tf_op jit(solution)/shard_map/middle/pallas_call | solution.py:191
  212.9 4.9 %collective-permute-start.18 = (s16[1040,128]{1,0:T(8,128)(2,1)}, s16[1040,128]{1,0:T(8,128)(2,1)S(1)}, u32[]{:S(2)}, u32[]{:S(2)}) collective-permute-start(s16[1040,128]{1,0:T(8,128)(2,1)} %get-tuple-element.59), channel_id=1, source_target_pairs={{0,2},{1,3},{2,0},{3,1},{4,6},{5,7},{6,4},{7,5},{8,10},{9,11},{10,... | collective-permute-start | bytes 798728 | tf_op jit(solution)/shard_map/ppermute | solution.py:346
  218.4 2.9 %collective-permute-start.23 = (s16[1040,128]{1,0:T(8,128)(2,1)}, s16[1040,128]{1,0:T(8,128)(2,1)S(1)}, u32[]{:S(2)}, u32[]{:S(2)}) collective-permute-start(s16[1040,128]{1,0:T(8,128)(2,1)} %middle.7), channel_id=1, source_target_pairs={{0,4},{1,5},{2,6},{3,7},{4,0},{5,1},{6,2},{7,3},{8,12},{9,13},{10,... | collective-permute-start | bytes 798728 | tf_op jit(solution)/shard_map/ppermute | solution.py:345
  222.0 2.5 %finish.2.refs_0_ = bf16[512,512]{1,0:T(8,128)(2,1)} custom-call(s16[1040,128]{1,0:T(8,128)(2,1)} %get-tuple-element.65.a, s16[1040,128]{1,0:T(8,128)(2,1)} %copy-done.9, s16[1040,128]{1,0:T(8,128)(2,1)} %copy-done.10, s16[1040,128]{1,0:T(8,128)(2,1)} %copy-done.11, s16[1040,128]{1,0:T(8,128)(2,1)} %copy-done.12, f32[1,512]{1,0:T(1,128)} %get-tuple-element.73.bias), custom_call_target="tpu_custom_call" | custom-call | flops 2129920 | bytes 1331200 | tf_op jit(solution)/shard_map/finish/pallas_call | solution.py:257
  229.3 2.5 %finish.3 = bf16[512,512]{1,0:T(8,128)(2,1)} custom-call(s16[1040,128]{1,0:T(8,128)(2,1)} %get-tuple-element.57.a, s16[1040,128]{1,0:T(8,128)(2,1)} %copy-done.25, s16[1040,128]{1,0:T(8,128)(2,1)} %copy-done.26, s16[1040,128]{1,0:T(8,128)(2,1)} %copy-done.27, s16[1040,128]{1,0:T(8,128)(2,1)} %copy-done.28, ...), custom_call_target="tpu_custom_call", output_to_operand_aliasing={{}: (6, {})} | custom-call | flops 2129920 | bytes 1331200 | tf_op jit(solution)/shard_map/finish/pallas_call | solution.py:257
  (123 shorter events, 35.5 us)
Async XLA Ops:
  6.5 42.5 %all-gather.11.cloned.1.call-start = ((), (), s32[]{:S(2)}) async-start(), calls=%async_computation.1 | async-start | bytes 4456448 | tf_op jit(solution)/shard_map/all_gather | solution.py:301
  8.2 88.0 %all-gather.9.cloned.1.call-start = ((), (), s32[]{:S(2)}) async-start(), calls=%async_computation | async-start | bytes 4456448 | tf_op jit(solution)/shard_map/all_gather | solution.py:301
  10.0 133.5 %all-gather.15.cloned.1.call-start = ((), (), s32[]{:S(2)}) async-start(), calls=%async_computation.3 | async-start | bytes 4456448 | tf_op jit(solution)/shard_map/all_gather | solution.py:301
  63.1 16.5 %collective-permute-start = (s16[1040,128]{1,0:T(8,128)(2,1)}, s16[1040,128]{1,0:T(8,128)(2,1)S(1)}, u32[]{:S(2)}, u32[]{:S(2)}) collective-permute-start(s16[1040,128]{1,0:T(8,128)(2,1)} %get-tuple-element.38), channel_id=1, source_target_pairs={{0,1},{1,2},{2,3},{3,0},{4,5},{5,6},{6,7},{7,4},{8,9},{9,10},{10,1... | collective-permute-start | bytes 798728 | tf_op jit(solution)/shard_map/ppermute | solution.py:341
  63.2 16.5 %collective-permute-start.1 = (s16[1040,128]{1,0:T(8,128)(2,1)}, s16[1040,128]{1,0:T(8,128)(2,1)S(1)}, u32[]{:S(2)}, u32[]{:S(2)}) collective-permute-start(s16[1040,128]{1,0:T(8,128)(2,1)} %get-tuple-element.39), channel_id=1, source_target_pairs={{0,2},{1,3},{2,0},{3,1},{4,6},{5,7},{6,4},{7,5},{8,10},{9,11},{10,... | collective-permute-start | bytes 798728 | tf_op jit(solution)/shard_map/ppermute | solution.py:341
  65.4 15.1 %collective-permute-start.2 = (s16[1040,128]{1,0:T(8,128)(2,1)}, s16[1040,128]{1,0:T(8,128)(2,1)S(1)}, u32[]{:S(2)}, u32[]{:S(2)}) collective-permute-start(s16[1040,128]{1,0:T(8,128)(2,1)} %get-tuple-element.40), channel_id=1, source_target_pairs={{0,3},{1,0},{2,1},{3,2},{4,7},{5,4},{6,5},{7,6},{8,11},{9,8},{10,9... | collective-permute-start | bytes 798728 | tf_op jit(solution)/shard_map/ppermute | solution.py:341
  66.4 22.5 %collective-permute-start.10 = (s16[1040,128]{1,0:T(8,128)(2,1)}, s16[1040,128]{1,0:T(8,128)(2,1)S(1)}, u32[]{:S(2)}, u32[]{:S(2)}) collective-permute-start(s16[1040,128]{1,0:T(8,128)(2,1)} %get-tuple-element.50), channel_id=1, source_target_pairs={{0,1},{1,2},{2,3},{3,0},{4,5},{5,6},{6,7},{7,4},{8,9},{9,10},{10,1... | collective-permute-start | bytes 798728 | tf_op jit(solution)/shard_map/ppermute | solution.py:346
  67.4 21.4 %collective-permute-start.11 = (s16[1040,128]{1,0:T(8,128)(2,1)}, s16[1040,128]{1,0:T(8,128)(2,1)S(1)}, u32[]{:S(2)}, u32[]{:S(2)}) collective-permute-start(s16[1040,128]{1,0:T(8,128)(2,1)} %get-tuple-element.51), channel_id=1, source_target_pairs={{0,2},{1,3},{2,0},{3,1},{4,6},{5,7},{6,4},{7,5},{8,10},{9,11},{10,... | collective-permute-start | bytes 798728 | tf_op jit(solution)/shard_map/ppermute | solution.py:346
  79.6 9.9 %collective-permute-start.12 = (s16[1040,128]{1,0:T(8,128)(2,1)}, s16[1040,128]{1,0:T(8,128)(2,1)S(1)}, u32[]{:S(2)}, u32[]{:S(2)}) collective-permute-start(s16[1040,128]{1,0:T(8,128)(2,1)} %get-tuple-element.52), channel_id=1, source_target_pairs={{0,3},{1,0},{2,1},{3,2},{4,7},{5,4},{6,5},{7,6},{8,11},{9,8},{10,9... | collective-permute-start | bytes 798728 | tf_op jit(solution)/shard_map/ppermute | solution.py:346
  83.7 9.2 %collective-permute-start.13 = (s16[1040,128]{1,0:T(8,128)(2,1)}, s16[1040,128]{1,0:T(8,128)(2,1)S(1)}, u32[]{:S(2)}, u32[]{:S(2)}) collective-permute-start(s16[1040,128]{1,0:T(8,128)(2,1)} %middle.4.refs_2_), channel_id=1, source_target_pairs={{0,4},{1,5},{2,6},{3,7},{4,0},{5,1},{6,2},{7,3},{8,12},{9,13},{10,... | collective-permute-start | bytes 798728 | tf_op jit(solution)/shard_map/ppermute | solution.py:345
  96.1 81.6 %all-gather.13.cloned.1.call-start = ((), (), s32[]{:S(2)}) async-start(), calls=%async_computation.2 | async-start | bytes 4456448 | tf_op jit(solution)/shard_map/all_gather | solution.py:301
  110.1 16.5 %collective-permute-start.6 = (s16[1040,128]{1,0:T(8,128)(2,1)}, s16[1040,128]{1,0:T(8,128)(2,1)S(1)}, u32[]{:S(2)}, u32[]{:S(2)}) collective-permute-start(s16[1040,128]{1,0:T(8,128)(2,1)} %get-tuple-element.46), channel_id=1, source_target_pairs={{0,1},{1,2},{2,3},{3,0},{4,5},{5,6},{6,7},{7,4},{8,9},{9,10},{10,1... | collective-permute-start | bytes 798728 | tf_op jit(solution)/shard_map/ppermute | solution.py:341
  110.2 16.5 %collective-permute-start.7 = (s16[1040,128]{1,0:T(8,128)(2,1)}, s16[1040,128]{1,0:T(8,128)(2,1)S(1)}, u32[]{:S(2)}, u32[]{:S(2)}) collective-permute-start(s16[1040,128]{1,0:T(8,128)(2,1)} %get-tuple-element.47), channel_id=1, source_target_pairs={{0,2},{1,3},{2,0},{3,1},{4,6},{5,7},{6,4},{7,5},{8,10},{9,11},{10,... | collective-permute-start | bytes 798728 | tf_op jit(solution)/shard_map/ppermute | solution.py:341
  113.3 14.3 %collective-permute-start.8 = (s16[1040,128]{1,0:T(8,128)(2,1)}, s16[1040,128]{1,0:T(8,128)(2,1)S(1)}, u32[]{:S(2)}, u32[]{:S(2)}) collective-permute-start(s16[1040,128]{1,0:T(8,128)(2,1)} %get-tuple-element.48), channel_id=1, source_target_pairs={{0,3},{1,0},{2,1},{3,2},{4,7},{5,4},{6,5},{7,6},{8,11},{9,8},{10,9... | collective-permute-start | bytes 798728 | tf_op jit(solution)/shard_map/ppermute | solution.py:341
  113.4 20.6 %collective-permute-start.3 = (s16[1040,128]{1,0:T(8,128)(2,1)}, s16[1040,128]{1,0:T(8,128)(2,1)S(1)}, u32[]{:S(2)}, u32[]{:S(2)}) collective-permute-start(s16[1040,128]{1,0:T(8,128)(2,1)} %get-tuple-element.42), channel_id=1, source_target_pairs={{0,1},{1,2},{2,3},{3,0},{4,5},{5,6},{6,7},{7,4},{8,9},{9,10},{10,1... | collective-permute-start | bytes 798728 | tf_op jit(solution)/shard_map/ppermute | solution.py:346
  115.3 18.7 %collective-permute-start.4 = (s16[1040,128]{1,0:T(8,128)(2,1)}, s16[1040,128]{1,0:T(8,128)(2,1)S(1)}, u32[]{:S(2)}, u32[]{:S(2)}) collective-permute-start(s16[1040,128]{1,0:T(8,128)(2,1)} %get-tuple-element.43), channel_id=1, source_target_pairs={{0,2},{1,3},{2,0},{3,1},{4,6},{5,7},{6,4},{7,5},{8,10},{9,11},{10,... | collective-permute-start | bytes 798728 | tf_op jit(solution)/shard_map/ppermute | solution.py:346
  126.6 8.1 %collective-permute-start.5 = (s16[1040,128]{1,0:T(8,128)(2,1)}, s16[1040,128]{1,0:T(8,128)(2,1)S(1)}, u32[]{:S(2)}, u32[]{:S(2)}) collective-permute-start(s16[1040,128]{1,0:T(8,128)(2,1)} %get-tuple-element.44), channel_id=1, source_target_pairs={{0,3},{1,0},{2,1},{3,2},{4,7},{5,4},{6,5},{7,6},{8,11},{9,8},{10,9... | collective-permute-start | bytes 798728 | tf_op jit(solution)/shard_map/ppermute | solution.py:346
  130.7 8.1 %collective-permute-start.9 = (s16[1040,128]{1,0:T(8,128)(2,1)}, s16[1040,128]{1,0:T(8,128)(2,1)S(1)}, u32[]{:S(2)}, u32[]{:S(2)}) collective-permute-start(s16[1040,128]{1,0:T(8,128)(2,1)} %middle.5), channel_id=1, source_target_pairs={{0,4},{1,5},{2,6},{3,7},{4,0},{5,1},{6,2},{7,3},{8,12},{9,13},{10,... | collective-permute-start | bytes 798728 | tf_op jit(solution)/shard_map/ppermute | solution.py:345
  152.3 11.8 %collective-permute-start.14 = (s16[1040,128]{1,0:T(8,128)(2,1)}, s16[1040,128]{1,0:T(8,128)(2,1)S(1)}, u32[]{:S(2)}, u32[]{:S(2)}) collective-permute-start(s16[1040,128]{1,0:T(8,128)(2,1)} %get-tuple-element.54), channel_id=1, source_target_pairs={{0,1},{1,2},{2,3},{3,0},{4,5},{5,6},{6,7},{7,4},{8,9},{9,10},{10,1... | collective-permute-start | bytes 798728 | tf_op jit(solution)/shard_map/ppermute | solution.py:341
  158.6 10.4 %collective-permute-start.15 = (s16[1040,128]{1,0:T(8,128)(2,1)}, s16[1040,128]{1,0:T(8,128)(2,1)S(1)}, u32[]{:S(2)}, u32[]{:S(2)}) collective-permute-start(s16[1040,128]{1,0:T(8,128)(2,1)} %get-tuple-element.55), channel_id=1, source_target_pairs={{0,2},{1,3},{2,0},{3,1},{4,6},{5,7},{6,4},{7,5},{8,10},{9,11},{10,... | collective-permute-start | bytes 798728 | tf_op jit(solution)/shard_map/ppermute | solution.py:341
  158.6 11.3 %collective-permute-start.16 = (s16[1040,128]{1,0:T(8,128)(2,1)}, s16[1040,128]{1,0:T(8,128)(2,1)S(1)}, u32[]{:S(2)}, u32[]{:S(2)}) collective-permute-start(s16[1040,128]{1,0:T(8,128)(2,1)} %get-tuple-element.56), channel_id=1, source_target_pairs={{0,3},{1,0},{2,1},{3,2},{4,7},{5,4},{6,5},{7,6},{8,11},{9,8},{10,9... | collective-permute-start | bytes 798728 | tf_op jit(solution)/shard_map/ppermute | solution.py:341
  186.7 12.4 %collective-permute-start.20 = (s16[1040,128]{1,0:T(8,128)(2,1)}, s16[1040,128]{1,0:T(8,128)(2,1)S(1)}, u32[]{:S(2)}, u32[]{:S(2)}) collective-permute-start(s16[1040,128]{1,0:T(8,128)(2,1)} %get-tuple-element.62), channel_id=1, source_target_pairs={{0,1},{1,2},{2,3},{3,0},{4,5},{5,6},{6,7},{7,4},{8,9},{9,10},{10,1... | collective-permute-start | bytes 798728 | tf_op jit(solution)/shard_map/ppermute | solution.py:341
  192.3 12.5 %collective-permute-start.21 = (s16[1040,128]{1,0:T(8,128)(2,1)}, s16[1040,128]{1,0:T(8,128)(2,1)S(1)}, u32[]{:S(2)}, u32[]{:S(2)}) collective-permute-start(s16[1040,128]{1,0:T(8,128)(2,1)} %get-tuple-element.63), channel_id=1, source_target_pairs={{0,2},{1,3},{2,0},{3,1},{4,6},{5,7},{6,4},{7,5},{8,10},{9,11},{10,... | collective-permute-start | bytes 798728 | tf_op jit(solution)/shard_map/ppermute | solution.py:341
  192.3 17.4 %collective-permute-start.22 = (s16[1040,128]{1,0:T(8,128)(2,1)}, s16[1040,128]{1,0:T(8,128)(2,1)S(1)}, u32[]{:S(2)}, u32[]{:S(2)}) collective-permute-start(s16[1040,128]{1,0:T(8,128)(2,1)} %get-tuple-element.64), channel_id=1, source_target_pairs={{0,3},{1,0},{2,1},{3,2},{4,7},{5,4},{6,5},{7,6},{8,11},{9,8},{10,9... | collective-permute-start | bytes 798728 | tf_op jit(solution)/shard_map/ppermute | solution.py:341
  195.1 17.9 %collective-permute-start.24 = (s16[1040,128]{1,0:T(8,128)(2,1)S(1)}, s16[1040,128]{1,0:T(8,128)(2,1)S(1)}, u32[]{:S(2)}, u32[]{:S(2)}) collective-permute-start(s16[1040,128]{1,0:T(8,128)(2,1)S(1)} %copy-done.32), channel_id=1, source_target_pairs={{0,1},{1,2},{2,3},{3,0},{4,5},{5,6},{6,7},{7,4},{8,9},{9,10},{10,1... | collective-permute-start | bytes 798728 | tf_op jit(solution)/shard_map/ppermute | solution.py:346
  195.1 22.8 %collective-permute-start.25 = (s16[1040,128]{1,0:T(8,128)(2,1)S(1)}, s16[1040,128]{1,0:T(8,128)(2,1)S(1)}, u32[]{:S(2)}, u32[]{:S(2)}) collective-permute-start(s16[1040,128]{1,0:T(8,128)(2,1)S(1)} %copy-done.31), channel_id=1, source_target_pairs={{0,2},{1,3},{2,0},{3,1},{4,6},{5,7},{6,4},{7,5},{8,10},{9,11},{10,... | collective-permute-start | bytes 798728 | tf_op jit(solution)/shard_map/ppermute | solution.py:346
  199.1 19.3 %collective-permute-start.26 = (s16[1040,128]{1,0:T(8,128)(2,1)S(1)}, s16[1040,128]{1,0:T(8,128)(2,1)S(1)}, u32[]{:S(2)}, u32[]{:S(2)}) collective-permute-start(s16[1040,128]{1,0:T(8,128)(2,1)S(1)} %copy-done.30), channel_id=1, source_target_pairs={{0,3},{1,0},{2,1},{3,2},{4,7},{5,4},{6,5},{7,6},{8,11},{9,8},{10,9... | collective-permute-start | bytes 798728 | tf_op jit(solution)/shard_map/ppermute | solution.py:346
  204.8 16.5 %collective-permute-start.27 = (s16[1040,128]{1,0:T(8,128)(2,1)S(1)}, s16[1040,128]{1,0:T(8,128)(2,1)S(1)}, u32[]{:S(2)}, u32[]{:S(2)}) collective-permute-start(s16[1040,128]{1,0:T(8,128)(2,1)S(1)} %copy-done.8), channel_id=1, source_target_pairs={{0,4},{1,5},{2,6},{3,7},{4,0},{5,1},{6,2},{7,3},{8,12},{9,13},{10,... | collective-permute-start | bytes 798728 | tf_op jit(solution)/shard_map/ppermute | solution.py:345
  209.8 14.8 %collective-permute-start.17 = (s16[1040,128]{1,0:T(8,128)(2,1)}, s16[1040,128]{1,0:T(8,128)(2,1)S(1)}, u32[]{:S(2)}, u32[]{:S(2)}) collective-permute-start(s16[1040,128]{1,0:T(8,128)(2,1)} %get-tuple-element.58), channel_id=1, source_target_pairs={{0,1},{1,2},{2,3},{3,0},{4,5},{5,6},{6,7},{7,4},{8,9},{9,10},{10,1... | collective-permute-start | bytes 798728 | tf_op jit(solution)/shard_map/ppermute | solution.py:346
  212.9 13.3 %collective-permute-start.18 = (s16[1040,128]{1,0:T(8,128)(2,1)}, s16[1040,128]{1,0:T(8,128)(2,1)S(1)}, u32[]{:S(2)}, u32[]{:S(2)}) collective-permute-start(s16[1040,128]{1,0:T(8,128)(2,1)} %get-tuple-element.59), channel_id=1, source_target_pairs={{0,2},{1,3},{2,0},{3,1},{4,6},{5,7},{6,4},{7,5},{8,10},{9,11},{10,... | collective-permute-start | bytes 798728 | tf_op jit(solution)/shard_map/ppermute | solution.py:346
  217.9 10.7 %collective-permute-start.19 = (s16[1040,128]{1,0:T(8,128)(2,1)}, s16[1040,128]{1,0:T(8,128)(2,1)S(1)}, u32[]{:S(2)}, u32[]{:S(2)}) collective-permute-start(s16[1040,128]{1,0:T(8,128)(2,1)} %get-tuple-element.60), channel_id=1, source_target_pairs={{0,3},{1,0},{2,1},{3,2},{4,7},{5,4},{6,5},{7,6},{8,11},{9,8},{10,9... | collective-permute-start | bytes 798728 | tf_op jit(solution)/shard_map/ppermute | solution.py:346
  218.4 10.1 %collective-permute-start.23 = (s16[1040,128]{1,0:T(8,128)(2,1)}, s16[1040,128]{1,0:T(8,128)(2,1)S(1)}, u32[]{:S(2)}, u32[]{:S(2)}) collective-permute-start(s16[1040,128]{1,0:T(8,128)(2,1)} %middle.7), channel_id=1, source_target_pairs={{0,4},{1,5},{2,6},{3,7},{4,0},{5,1},{6,2},{7,3},{8,12},{9,13},{10,... | collective-permute-start | bytes 798728 | tf_op jit(solution)/shard_map/ppermute | solution.py:345
  (33 other events, 196.3 us)
Sparse Core Ops, SparseCore 0:
  9.1 39.9 all-gather.10
  50.7 37.3 all-gather.8
  96.2 37.0 all-gather.14
  142.3 35.4 all-gather.12

commit v2 on v1

v2 whole, which is shorter than its diff:
```python
import functools

import jax
import jax.numpy as jnp
from jax import lax
from jax.experimental import pallas as pl
from jax.experimental.pallas import tpu as pltpu
from jax.sharding import PartitionSpec as P

BLK = 128
CB = 32
N_ROW = 16
N_COL = 8
N_Y = 4
SUB = CB // N_COL
HALF = CB // 2
GROUP = 16
ROW_AT, COLUMN_AT = 9, 15
HEIGHTS = (256, 256)
STEPS = 16.0
TOP = 32000.0
VMEM = pl.BlockSpec(memory_space=pltpu.VMEM)
SMEM = pl.BlockSpec(memory_space=pltpu.SMEM)
ANY = pl.BlockSpec(memory_space=pl.ANY)
HBM = pl.BlockSpec(memory_space=pltpu.HBM)

def to_col(e, d):
    return [(c, ((c & 4) ^ (4 * e)) + ((c + d) & 3)) for c in range(N_COL)]


def plan(block_rows, block_cols, counts, z_hi, y):
    slots = block_cols.shape[1]
    index = jnp.arange(slots, dtype=jnp.int32)
    live = index[None, :] < counts[:, None]
    apart_z = (block_cols >> 4) ^ z_hi
    apart_y = ((block_cols >> 2) - y) & (N_Y - 1)
    column = apart_y * SUB + (block_cols & (SUB - 1))
    code = index[None, :] | (block_rows << ROW_AT) | (column << COLUMN_AT)
    unused = HALF << COLUMN_AT
    halves = jnp.arange(2, dtype=jnp.int32)[None, :, None]
    member = live[:, None, :] & (apart_z[:, None, :] == halves)
    lower = index[None, :] < index[:, None]
    rank = jnp.sum(member[:, :, None, :] & lower[None, None], axis=3, dtype=jnp.int32)
    at = (member & (rank < slots))[:, :, None, :] & (
        rank[:, :, None, :] == index[None, None, :, None]
    )
    codes = unused + jnp.sum(jnp.where(at, code[:, None, None, :] - unused, 0), axis=3)
    return codes, jnp.sum(member, axis=2, dtype=jnp.int32)


def product_kernel(layer, codes, count, gathered, values, *refs):
    *outs, panel, held, acc, part_sem, sems = refs[-N_Y - 5 :]
    height = panel.shape[1]
    groups = (count[0] + GROUP - 1) // GROUP
    ahead = 4

    def fetch(group):
        @pl.when(group < groups)
        def _():
            for j in range(GROUP):
                spot = group * GROUP + j
                slot = codes[spot] & ((1 << ROW_AT) - 1)
                pltpu.make_async_copy(
                    values.at[layer, 0, 0, slot], held.at[spot], sems.at[group]
                ).start()

    whole = pltpu.make_async_copy(gathered, panel, part_sem)
    whole.start()
    for group in range(ahead):
        fetch(group)
    acc[...] = jnp.zeros_like(acc)
    whole.wait()

    def one_group(group, _):
        fetch(group + ahead)
        spots = pl.ds(group * GROUP, GROUP)
        pltpu.make_async_copy(
            values.at[layer, 0, 0, pl.ds(0, GROUP)], held.at[spots], sems.at[group]
        ).wait()
        for j in range(GROUP):
            spot = group * GROUP + j
            code = codes[spot]
            row = (code >> ROW_AT) & ((1 << (COLUMN_AT - ROW_AT)) - 1)
            lanes = pl.ds(pl.multiple_of((row & (SUB - 1)) * BLK, BLK), BLK)
            left = panel[row >> 2, :, lanes]
            acc[code >> COLUMN_AT] += jnp.dot(
                left, held[spot], preferred_element_type=jnp.float32
            )
        return 0

    lax.fori_loop(0, groups, one_group, 0)
    for d in range(N_Y):
        encode(lambda t, d=d: acc[d * SUB + t], outs[d], height)


def encode(sums_of, out, height):
    codes = []
    for t in range(SUB):
        sums = sums_of(t)
        most = jnp.max(jnp.abs(sums), axis=0, keepdims=True)
        code = jnp.ceil(jnp.log2(jnp.maximum(most, 1e-30)) * STEPS)
        codes.append(code)
        inverse = TOP * jnp.exp2(code * (-1.0 / STEPS))
        whole = jnp.round(sums * inverse).astype(jnp.int32)
        out[pl.ds(t * height, height), :] = whole.astype(jnp.int16)
    codes = jnp.concatenate(codes + [jnp.zeros((16 - SUB, BLK), jnp.float32)], axis=0)
    out[pl.ds(SUB * height, 16), :] = codes.astype(jnp.int32).astype(jnp.int16)


def product(layer, codes, count, gathered, values, after=()):
    slots, height = values.shape[3], gathered.shape[1]
    piece = jax.ShapeDtypeStruct((SUB * height + 16, BLK), jnp.int16)
    return pl.pallas_call(
        functools.partial(product_kernel, layer),
        out_shape=(piece,) * N_Y,
        in_specs=[SMEM] * 2 + [HBM] * 2 + [ANY] * len(after),
        out_specs=(VMEM,) * N_Y,
        scratch_shapes=[
            pltpu.VMEM((N_ROW, height, SUB * BLK), jnp.bfloat16),
            pltpu.VMEM((slots, BLK, BLK), jnp.bfloat16),
            pltpu.VMEM((HALF + 1, height, BLK), jnp.float32),
            pltpu.SemaphoreType.DMA,
            pltpu.SemaphoreType.DMA((slots // GROUP,)),
        ],
        compiler_params=pltpu.CompilerParams(vmem_limit_bytes=58 * 1024 * 1024),
        cost_estimate=pl.CostEstimate(
            flops=8 * height * BLK * BLK * slots,
            bytes_accessed=slots * BLK * BLK * 2,
            transcendentals=0,
        ),
        name="product",
    )(codes, count, gathered, values, *after)


def rows_at_once(height):
    return next(r for r in (64, 48, 32, 16) if height % r == 0)


def scales_of(piece, height):
    codes = piece[pl.ds(SUB * height, 16), :].astype(jnp.int32).astype(jnp.float32)
    return jnp.exp2(codes * (1.0 / STEPS)) * (1.0 / TOP)


def add_pieces(pieces, scales, t, spot):
    total = None
    for piece, scale in zip(pieces, scales):
        term = piece[spot, :].astype(jnp.int32).astype(jnp.float32) * scale[t : t + 1, :]
        total = term if total is None else total + term
    return total


def middle_kernel(a, b, c, d, out, totals):
    height = totals.shape[0]
    rows = rows_at_once(height)
    pieces = (a, b, c, d)
    scales = [scales_of(piece, height) for piece in pieces]
    codes = []
    for t in range(SUB):

        def add(i, most, t=t):
            first = pl.multiple_of(i * rows, rows)
            total = add_pieces(pieces, scales, t, pl.ds(t * height + first, rows))
            totals[pl.ds(first, rows), :] = total
            return jnp.maximum(most, jnp.max(jnp.abs(total).reshape(rows // 8, 8, BLK), axis=0))

        most = lax.fori_loop(0, height // rows, add, jnp.zeros((8, BLK), jnp.float32))
        most = jnp.max(most, axis=0, keepdims=True)
        code = jnp.ceil(jnp.log2(jnp.maximum(most, 1e-30)) * STEPS)
        codes.append(code)
        inverse = TOP * jnp.exp2(code * (-1.0 / STEPS))

        def store(i, _, t=t, inverse=inverse):
            first = pl.multiple_of(i * rows, rows)
            whole = jnp.round(totals[pl.ds(first, rows), :] * inverse).astype(jnp.int32)
            out[pl.ds(t * height + first, rows), :] = whole.astype(jnp.int16)
            return 0

        lax.fori_loop(0, height // rows, store, 0)
    codes = jnp.concatenate(codes + [jnp.zeros((16 - SUB, BLK), jnp.float32)], axis=0)
    out[pl.ds(SUB * height, 16), :] = codes.astype(jnp.int32).astype(jnp.int16)


def middle(pieces):
    height = (pieces[0].shape[0] - 16) // SUB
    return pl.pallas_call(
        middle_kernel,
        out_shape=jax.ShapeDtypeStruct(pieces[0].shape, jnp.int16),
        in_specs=[VMEM] * 4,
        out_specs=VMEM,
        scratch_shapes=[pltpu.VMEM((height, BLK), jnp.float32)],
        cost_estimate=pl.CostEstimate(
            flops=16 * pieces[0].size, bytes_accessed=8 * pieces[0].size, transcendentals=0
        ),
        name="middle",
    )(*pieces)


def add_and_clip(pieces, bias, out, height):
    rows = rows_at_once(height)
    scales = [scales_of(piece, height) for piece in pieces]
    for t in range(SUB):
        lanes = slice(t * BLK, (t + 1) * BLK)

        def part(i, _, t=t, lanes=lanes):
            first = pl.multiple_of(i * rows, rows)
            total = add_pieces(pieces, scales, t, pl.ds(t * height + first, rows)) + bias[:, lanes]
            kept = jnp.minimum(jnp.maximum(total, 0.0), 32.0)
            out[pl.ds(first, rows), lanes] = kept.astype(jnp.bfloat16)
            return 0

        lax.fori_loop(0, height // rows, part, 0)


def combine_kernel(n_pieces, first, *refs):
    pieces, bias, (out, kept, sem) = refs[:n_pieces], refs[n_pieces], refs[-3:]
    height = kept.shape[0]
    add_and_clip(pieces, bias, kept, height)
    copy = pltpu.make_async_copy(kept, out.at[pl.ds(first, height)], sem)
    copy.start()
    copy.wait()


def combine(pieces, bias, first=0, batch=None, earlier=None):
    height = (pieces[0].shape[0] - 16) // SUB
    more = [] if earlier is None else [earlier]
    n_pieces = len(pieces)
    return pl.pallas_call(
        functools.partial(combine_kernel, n_pieces, first),
        out_shape=jax.ShapeDtypeStruct((batch or height, SUB * BLK), jnp.bfloat16),
        in_specs=[VMEM] * (n_pieces + 1) + [ANY] * len(more),
        out_specs=HBM,
        scratch_shapes=[
            pltpu.VMEM((height, SUB * BLK), jnp.bfloat16),
            pltpu.SemaphoreType.DMA,
        ],
        input_output_aliases={n_pieces + 1: 0} if more else {},
        cost_estimate=pl.CostEstimate(
            flops=16 * pieces[0].size, bytes_accessed=10 * pieces[0].size, transcendentals=0
        ),
        name="combine",
    )(*pieces, bias, *more)


def exchange(layer, codes, counts, gathered, values, after):
    far = product(layer, codes[1], counts[1:], gathered, values, after)
    away = [far[0]] + [lax.ppermute(far[d], "col", to_col(0, d)) for d in range(1, N_Y)]
    near = product(layer, codes[0], counts[:1], gathered, values)
    sent = middle(away)
    pieces = [near[0], lax.ppermute(sent, "col", to_col(1, 0))]
    pieces += [lax.ppermute(near[d], "col", to_col(0, d)) for d in range(1, N_Y)]
    return pieces, [sent, near[0]]


def on_device(features, block_values, block_rows, block_cols, block_counts, bias):
    layers = block_values.shape[0]
    batch = features.shape[0]
    there = lax.axis_index("col")
    codes, counts = plan(
        block_rows[:, 0, 0], block_cols[:, 0, 0], block_counts[:, 0, 0], there >> 2, there & 3
    )
    firsts = [sum(HEIGHTS[:c]) for c in range(len(HEIGHTS))]
    current = [features[f : f + h, 0, :] for f, h in zip(firsts, HEIGHTS)]
    result = None
    for layer in range(layers):
        after = []
        for c in range(len(HEIGHTS)):
            gathered = lax.all_gather(current[c], "row", axis=0, tiled=False)
            pieces, sent = exchange(
                layer, codes[layer], counts[layer], gathered, block_values, after
            )
            after = sent
            if layer < layers - 1:
                current[c] = combine(pieces, bias[layer])
            else:
                result = combine(pieces, bias[layer], firsts[c], batch, result)
                after = [result]
    return result[:, None, :]


def solution(mesh):
    in_specs = (
        P(None, "col", "row"),
        P(None, "row", "col", None, None, None),
        P(None, "row", "col", None),
        P(None, "row", "col", None),
        P(None, "row", "col"),
        P(None, "col", "row"),
    )
    out_specs = P(None, "col", "row")
    return jax.shard_map(
        on_device, mesh=mesh, in_specs=in_specs, out_specs=out_specs, check_vma=False
    )
```

time: 241 us -> 232 us (0.963); the launches traced: 238 us -> 233 us
  waiting for transfers between devices: 96.9 us -> 72.8 us
  Pallas kernels: 69.1 us -> 92.4 us
  starting transfers between devices: 46.1 us -> 41.9 us
    pallas_call x10 -> x12, Pallas kernels: 59.1 us -> 82.4 us  [the longest x8 72.3 us: product(): pl.pallas_call(functools.partial(product_kernel, layer), out_shape=(piece...]
    ppermute x28, waiting for transfers between devices: 58.5 us -> 36 us  [the longest x12 25.2 us: exchange(): lax.ppermute(near[d], 'col', to_col(0, d))]
    ppermute x28, starting transfers between devices: 45.9 us -> 41.8 us  [the longest x12 22 us: exchange(): lax.ppermute(far[d], 'col', to_col(0, d))]
    another operation x2 -> x0, other arithmetic: 2.61 us -> none  [on_device(): info = jnp.stack([counts[layer], there >> 2, there & 3])]
    unnamed x66 -> x59, local copies, waits for them, and re-layouts: 5.68 us -> 6.03 us
  transfers between devices with their start and end apart: 32 -> 32, of which waited for: 19 -> 14; matrix products, arithmetic and copies ran while one was open for 3% -> 2% of each run, Pallas kernels for 23% -> 35%
where the time goes in v2:
time: 232 us; the launch traced here: 233 us
  Pallas kernels  92.4 us (40%)
  waiting for transfers between devices  72.8 us (31%)
  starting transfers between devices  41.9 us (18%)
  between operations  13.5 us (6%)
  local copies, waits for them, and re-layouts  9.79 us (4%)
  other arithmetic  2.49 us (1%)
    pallas_call x8, Pallas kernels, product(): pl.pallas_call(functools.partial(product_kernel, layer), out_shape=(piece...  72.3 us
    all_gather x4, waiting for transfers between devices, on_device(): gathered = lax.all_gather(current[c], 'row', axis=0, tiled=False)  36.1 us
    ppermute x12, waiting for transfers between devices, exchange(): lax.ppermute(near[d], 'col', to_col(0, d))  25.2 us
    ppermute x12, starting transfers between devices, exchange(): lax.ppermute(far[d], 'col', to_col(0, d))  22 us
    ppermute x12, starting transfers between devices, exchange(): lax.ppermute(near[d], 'col', to_col(0, d))  15.5 us
    ppermute x4, waiting for transfers between devices, exchange(): pieces = [near[0], lax.ppermute(sent, 'col', to_col(1, 0))]  10.7 us
    pallas_call x4, Pallas kernels, combine(): pl.pallas_call(functools.partial(combine_kernel, n_pieces, first), out_sh...  10.1 us
    pallas_call x4, Pallas kernels, middle(): pl.pallas_call(middle_kernel, out_shape=jax.ShapeDtypeStruct(pieces[0].sh...  10 us
  transfers between devices with their start and end apart: 32, of which 14 were waited for; matrix products, arithmetic and copies ran while one was open for 2% of the time, Pallas kernels for 35%

profile of v2, /device:TPU:0, one launch (start us, length us, event | category | flops | bytes accessed | tf_op | source)
XLA Modules:
  0.0 232.8 jit_solution(8833783907632724168)
XLA Ops:
  13.0 36.0 %all-gather.11.cloned.1.call-done = bf16[4096,1,512]{2,0,1:T(8,128)(2,1)} async-done(((bf16[256,1,512]{2,0,1:T(8,128)(2,1)}), bf16[4096,1,512]{2,0,1:T(8,128)(2,1)}) %all-gather.11.cloned.1.call-update) | async-done | bytes 4194320 | tf_op jit(solution)/shard_map/all_gather | solution.py:267
  49.0 9.5 %product.9 = (s16[1040,128]{1,0:T(8,128)(2,1)}, s16[1040,128]{1,0:T(8,128)(2,1)}, s16[1040,128]{1,0:T(8,128)(2,1)}, s16[1040,128]{1,0:T(8,128)(2,1)}) custom-call(s32[320]{0:T(512)} %get-tuple-element.70.codes, s32[1]{0:T(128)} %bitcast.4.count, bf16[16,256,512]{2,1,0:T(8,128)(2,1)} %bitcast.25, bf16[2,1,1,320,128,128]{5,4,3,2,1,0:T(8,128)(2,1)} %values.15), custom_call_target="tpu_custom_call" | custom-call | flops 10737418240 | bytes 10485760 | tf_op jit(solution)/shard_map/product/pallas_call | solution.py:113
  58.6 3.9 %collective-permute-start.1 = (s16[1040,128]{1,0:T(8,128)(2,1)}, s16[1040,128]{1,0:T(8,128)(2,1)S(1)}, u32[]{:S(2)}, u32[]{:S(2)}) collective-permute-start(s16[1040,128]{1,0:T(8,128)(2,1)} %get-tuple-element.40), channel_id=1, source_target_pairs={{0,2},{1,3},{2,0},{3,1},{4,6},{5,7},{6,4},{7,5},{8,10},{9,11},{10,... | collective-permute-start | bytes 798728 | tf_op jit(solution)/shard_map/ppermute | solution.py:246
  62.6 2.5 %collective-permute-start.2 = (s16[1040,128]{1,0:T(8,128)(2,1)}, s16[1040,128]{1,0:T(8,128)(2,1)S(1)}, u32[]{:S(2)}, u32[]{:S(2)}) collective-permute-start(s16[1040,128]{1,0:T(8,128)(2,1)} %get-tuple-element.41), channel_id=1, source_target_pairs={{0,3},{1,0},{2,1},{3,2},{4,7},{5,4},{6,5},{7,6},{8,11},{9,8},{10,9... | collective-permute-start | bytes 798728 | tf_op jit(solution)/shard_map/ppermute | solution.py:246
  65.1 9.1 %product.10 = (s16[1040,128]{1,0:T(8,128)(2,1)}, s16[1040,128]{1,0:T(8,128)(2,1)}, s16[1040,128]{1,0:T(8,128)(2,1)}, s16[1040,128]{1,0:T(8,128)(2,1)}) custom-call(s32[320]{0:T(512)} %get-tuple-element.71.codes, s32[1]{0:T(128)} %bitcast.2.count, bf16[16,256,512]{2,1,0:T(8,128)(2,1)} %bitcast.26, bf16[2,1,1,320,128,128]{5,4,3,2,1,0:T(8,128)(2,1)} %values.15), custom_call_target="tpu_custom_call" | custom-call | flops 10737418240 | bytes 10485760 | tf_op jit(solution)/shard_map/product/pallas_call | solution.py:113
  74.6 3.1 %collective-permute-start.13 = (s16[1040,128]{1,0:T(8,128)(2,1)}, s16[1040,128]{1,0:T(8,128)(2,1)S(1)}, u32[]{:S(2)}, u32[]{:S(2)}) collective-permute-start(s16[1040,128]{1,0:T(8,128)(2,1)} %get-tuple-element.53), channel_id=1, source_target_pairs={{0,3},{1,0},{2,1},{3,2},{4,7},{5,4},{6,5},{7,6},{8,11},{9,8},{10,9... | collective-permute-start | bytes 798728 | tf_op jit(solution)/shard_map/ppermute | solution.py:250
  82.1 5.9 %collective-permute-done.11.refs_2_ = s16[1040,128]{1,0:T(8,128)(2,1)S(1)} collective-permute-done((s16[1040,128]{1,0:T(8,128)(2,1)}, s16[1040,128]{1,0:T(8,128)(2,1)S(1)}, u32[]{:S(2)}, u32[]{:S(2)}) %collective-permute-start.11) | collective-permute-done | bytes 266272 | tf_op jit(solution)/shard_map/ppermute | solution.py:250
  88.6 3.7 %collective-permute-done.10.refs_1_ = s16[1040,128]{1,0:T(8,128)(2,1)S(1)} collective-permute-done((s16[1040,128]{1,0:T(8,128)(2,1)}, s16[1040,128]{1,0:T(8,128)(2,1)S(1)}, u32[]{:S(2)}, u32[]{:S(2)}) %collective-permute-start.10) | collective-permute-done | bytes 266272 | tf_op jit(solution)/shard_map/ppermute | solution.py:249
  93.0 2.5 %combine.5 = bf16[256,512]{1,0:T(8,128)(2,1)} custom-call(s16[1040,128]{1,0:T(8,128)(2,1)} %get-tuple-element.42.refs_1_.refs_0_, s16[1040,128]{1,0:T(8,128)(2,1)} %copy-done.6, s16[1040,128]{1,0:T(8,128)(2,1)} %copy-done, s16[1040,128]{1,0:T(8,128)(2,1)} %copy-done.2, s16[1040,128]{1,0:T(8,128)(2,1)} %copy-done.4, f32[1,512]{1,0:T(1,128)} %get-tuple-element.78.refs_5_), custom_call_target="tpu_custom_call" | custom-call | flops 2129920 | bytes 1331200 | tf_op jit(solution)/shard_map/combine/pallas_call | solution.py:227
  95.6 9.6 %product.11 = (s16[1040,128]{1,0:T(8,128)(2,1)}, s16[1040,128]{1,0:T(8,128)(2,1)}, s16[1040,128]{1,0:T(8,128)(2,1)}, s16[1040,128]{1,0:T(8,128)(2,1)}) custom-call(s32[320]{0:T(512)} %get-tuple-element.70.codes, s32[1]{0:T(128)} %bitcast.4.count, bf16[16,256,512]{2,1,0:T(8,128)(2,1)} %bitcast.19, bf16[2,1,1,320,128,128]{5,4,3,2,1,0:T(8,128)(2,1)} %values.15, ...), custom_call_target="tpu_custom_call" | custom-call | flops 10737418240 | bytes 10485760 | tf_op jit(solution)/shard_map/product/pallas_call | solution.py:113
  105.3 3.8 %collective-permute-start.4 = (s16[1040,128]{1,0:T(8,128)(2,1)}, s16[1040,128]{1,0:T(8,128)(2,1)S(1)}, u32[]{:S(2)}, u32[]{:S(2)}) collective-permute-start(s16[1040,128]{1,0:T(8,128)(2,1)} %get-tuple-element.45), channel_id=1, source_target_pairs={{0,2},{1,3},{2,0},{3,1},{4,6},{5,7},{6,4},{7,5},{8,10},{9,11},{10,... | collective-permute-start | bytes 798728 | tf_op jit(solution)/shard_map/ppermute | solution.py:246
  109.1 2.5 %collective-permute-start.5 = (s16[1040,128]{1,0:T(8,128)(2,1)}, s16[1040,128]{1,0:T(8,128)(2,1)S(1)}, u32[]{:S(2)}, u32[]{:S(2)}) collective-permute-start(s16[1040,128]{1,0:T(8,128)(2,1)} %get-tuple-element.46), channel_id=1, source_target_pairs={{0,3},{1,0},{2,1},{3,2},{4,7},{5,4},{6,5},{7,6},{8,11},{9,8},{10,9... | collective-permute-start | bytes 798728 | tf_op jit(solution)/shard_map/ppermute | solution.py:246
  111.6 9.0 %product.8 = (s16[1040,128]{1,0:T(8,128)(2,1)}, s16[1040,128]{1,0:T(8,128)(2,1)}, s16[1040,128]{1,0:T(8,128)(2,1)}, s16[1040,128]{1,0:T(8,128)(2,1)}) custom-call(s32[320]{0:T(512)} %get-tuple-element.71.codes, s32[1]{0:T(128)} %bitcast.2.count, bf16[16,256,512]{2,1,0:T(8,128)(2,1)} %bitcast.20, bf16[2,1,1,320,128,128]{5,4,3,2,1,0:T(8,128)(2,1)} %values.15), custom_call_target="tpu_custom_call" | custom-call | flops 10737418240 | bytes 10485760 | tf_op jit(solution)/shard_map/product/pallas_call | solution.py:113
  121.1 2.9 %collective-permute-start.9 = (s16[1040,128]{1,0:T(8,128)(2,1)}, s16[1040,128]{1,0:T(8,128)(2,1)S(1)}, u32[]{:S(2)}, u32[]{:S(2)}) collective-permute-start(s16[1040,128]{1,0:T(8,128)(2,1)} %get-tuple-element.49), channel_id=1, source_target_pairs={{0,3},{1,0},{2,1},{3,2},{4,7},{5,4},{6,5},{7,6},{8,11},{9,8},{10,9... | collective-permute-start | bytes 798728 | tf_op jit(solution)/shard_map/ppermute | solution.py:250
  124.8 2.5 %middle.5 = s16[1040,128]{1,0:T(8,128)(2,1)} custom-call(s16[1040,128]{1,0:T(8,128)(2,1)} %get-tuple-element.43.a, s16[1040,128]{1,0:T(8,128)(2,1)} %copy-done.10, s16[1040,128]{1,0:T(8,128)(2,1)} %copy-done.14, s16[1040,128]{1,0:T(8,128)(2,1)} %copy-done.19), custom_call_target="tpu_custom_call" | custom-call | flops 2129920 | bytes 1064960 | tf_op jit(solution)/shard_map/middle/pallas_call | solution.py:185
  128.8 5.3 %collective-permute-done.8.refs_3_ = s16[1040,128]{1,0:T(8,128)(2,1)S(1)} collective-permute-done((s16[1040,128]{1,0:T(8,128)(2,1)}, s16[1040,128]{1,0:T(8,128)(2,1)S(1)}, u32[]{:S(2)}, u32[]{:S(2)}) %collective-permute-start.8) | collective-permute-done | bytes 266272 | tf_op jit(solution)/shard_map/ppermute | solution.py:250
  137.4 2.5 %combine.4 = bf16[256,512]{1,0:T(8,128)(2,1)} custom-call(s16[1040,128]{1,0:T(8,128)(2,1)} %get-tuple-element.37.refs_0_, s16[1040,128]{1,0:T(8,128)(2,1)} %copy-done.7, s16[1040,128]{1,0:T(8,128)(2,1)} %copy-done.1, s16[1040,128]{1,0:T(8,128)(2,1)} %copy-done.3, s16[1040,128]{1,0:T(8,128)(2,1)} %copy-done.5, f32[1,512]{1,0:T(1,128)} %get-tuple-element.78.refs_5_), custom_call_target="tpu_custom_call" | custom-call | flops 2129920 | bytes 1331200 | tf_op jit(solution)/shard_map/combine/pallas_call | solution.py:227
  140.0 8.8 %product.14 = (s16[1040,128]{1,0:T(8,128)(2,1)}, s16[1040,128]{1,0:T(8,128)(2,1)}, s16[1040,128]{1,0:T(8,128)(2,1)}, s16[1040,128]{1,0:T(8,128)(2,1)}) custom-call(s32[320]{0:T(512)} %get-tuple-element.69.codes, s32[1]{0:T(128)} %bitcast.8.count, bf16[16,256,512]{2,1,0:T(8,128)(2,1)} %bitcast.21, bf16[2,1,1,320,128,128]{5,4,3,2,1,0:T(8,128)(2,1)} %values.15), custom_call_target="tpu_custom_call" | custom-call | flops 10737418240 | bytes 10485760 | tf_op jit(solution)/shard_map/product/pallas_call | solution.py:113
  150.3 3.4 %collective-permute-start.15 = (s16[1040,128]{1,0:T(8,128)(2,1)}, s16[1040,128]{1,0:T(8,128)(2,1)S(1)}, u32[]{:S(2)}, u32[]{:S(2)}) collective-permute-start(s16[1040,128]{1,0:T(8,128)(2,1)} %get-tuple-element.57), channel_id=1, source_target_pairs={{0,2},{1,3},{2,0},{3,1},{4,6},{5,7},{6,4},{7,5},{8,10},{9,11},{10,... | collective-permute-start | bytes 798728 | tf_op jit(solution)/shard_map/ppermute | solution.py:246
  153.7 8.8 %product.13 = (s16[1040,128]{1,0:T(8,128)(2,1)}, s16[1040,128]{1,0:T(8,128)(2,1)}, s16[1040,128]{1,0:T(8,128)(2,1)}, s16[1040,128]{1,0:T(8,128)(2,1)}) custom-call(s32[320]{0:T(512)} %get-tuple-element.72.codes, s32[1]{0:T(128)} %bitcast.1.count, bf16[16,256,512]{2,1,0:T(8,128)(2,1)} %bitcast.22, bf16[2,1,1,320,128,128]{5,4,3,2,1,0:T(8,128)(2,1)} %values.15), custom_call_target="tpu_custom_call" | custom-call | flops 10737418240 | bytes 10485760 | tf_op jit(solution)/shard_map/product/pallas_call | solution.py:113
  164.2 2.7 %collective-permute-start.20 = (s16[1040,128]{1,0:T(8,128)(2,1)}, s16[1040,128]{1,0:T(8,128)(2,1)S(1)}, u32[]{:S(2)}, u32[]{:S(2)}) collective-permute-start(s16[1040,128]{1,0:T(8,128)(2,1)} %get-tuple-element.61), channel_id=1, source_target_pairs={{0,3},{1,0},{2,1},{3,2},{4,7},{5,4},{6,5},{7,6},{8,11},{9,8},{10,9... | collective-permute-start | bytes 798728 | tf_op jit(solution)/shard_map/ppermute | solution.py:250
  167.7 2.5 %middle.6 = s16[1040,128]{1,0:T(8,128)(2,1)} custom-call(s16[1040,128]{1,0:T(8,128)(2,1)} %get-tuple-element.55.a, s16[1040,128]{1,0:T(8,128)(2,1)} %copy-done.11, s16[1040,128]{1,0:T(8,128)(2,1)} %copy-done.15, s16[1040,128]{1,0:T(8,128)(2,1)} %copy-done.20), custom_call_target="tpu_custom_call" | custom-call | flops 2129920 | bytes 1064960 | tf_op jit(solution)/shard_map/middle/pallas_call | solution.py:185
  172.3 5.6 %collective-permute-done.19.refs_3_ = s16[1040,128]{1,0:T(8,128)(2,1)S(1)} collective-permute-done((s16[1040,128]{1,0:T(8,128)(2,1)}, s16[1040,128]{1,0:T(8,128)(2,1)S(1)}, u32[]{:S(2)}, u32[]{:S(2)}) %collective-permute-start.19) | collective-permute-done | bytes 266272 | tf_op jit(solution)/shard_map/ppermute | solution.py:250
  177.9 3.3 %collective-permute-done.17.refs_1_ = s16[1040,128]{1,0:T(8,128)(2,1)S(1)} collective-permute-done((s16[1040,128]{1,0:T(8,128)(2,1)}, s16[1040,128]{1,0:T(8,128)(2,1)S(1)}, u32[]{:S(2)}, u32[]{:S(2)}) %collective-permute-start.17) | collective-permute-done | bytes 266272 | tf_op jit(solution)/shard_map/ppermute | solution.py:249
  181.9 2.5 %combine.6.refs_0_.refs_6_ = bf16[512,512]{1,0:T(8,128)(2,1)} custom-call(s16[1040,128]{1,0:T(8,128)(2,1)} %get-tuple-element.54.refs_0_, s16[1040,128]{1,0:T(8,128)(2,1)} %copy-done.23, s16[1040,128]{1,0:T(8,128)(2,1)} %copy-done.8, s16[1040,128]{1,0:T(8,128)(2,1)} %copy-done.9, s16[1040,128]{1,0:T(8,128)(2,1)} %copy-done.16, ...), custom_call_target="tpu_custom_call" | custom-call | flops 2129920 | bytes 1331200 | tf_op jit(solution)/shard_map/combine/pallas_call | solution.py:227
  184.5 8.8 %product.15 = (s16[1040,128]{1,0:T(8,128)(2,1)}, s16[1040,128]{1,0:T(8,128)(2,1)}, s16[1040,128]{1,0:T(8,128)(2,1)}, s16[1040,128]{1,0:T(8,128)(2,1)}) custom-call(s32[320]{0:T(512)} %get-tuple-element.69.codes, s32[1]{0:T(128)} %bitcast.8.count, bf16[16,256,512]{2,1,0:T(8,128)(2,1)} %bitcast.23, bf16[2,1,1,320,128,128]{5,4,3,2,1,0:T(8,128)(2,1)} %values.15, ...), custom_call_target="tpu_custom_call" | custom-call | flops 10737418240 | bytes 10485760 | tf_op jit(solution)/shard_map/product/pallas_call | solution.py:113
  194.2 3.3 %collective-permute-start.22 = (s16[1040,128]{1,0:T(8,128)(2,1)}, s16[1040,128]{1,0:T(8,128)(2,1)S(1)}, u32[]{:S(2)}, u32[]{:S(2)}) collective-permute-start(s16[1040,128]{1,0:T(8,128)(2,1)} %get-tuple-element.64), channel_id=1, source_target_pairs={{0,2},{1,3},{2,0},{3,1},{4,6},{5,7},{6,4},{7,5},{8,10},{9,11},{10,... | collective-permute-start | bytes 798728 | tf_op jit(solution)/shard_map/ppermute | solution.py:246
  197.4 8.7 %product.12 = (s16[1040,128]{1,0:T(8,128)(2,1)}, s16[1040,128]{1,0:T(8,128)(2,1)}, s16[1040,128]{1,0:T(8,128)(2,1)}, s16[1040,128]{1,0:T(8,128)(2,1)}) custom-call(s32[320]{0:T(512)} %get-tuple-element.72.codes, s32[1]{0:T(128)} %bitcast.1.count, bf16[16,256,512]{2,1,0:T(8,128)(2,1)} %bitcast.24, bf16[2,1,1,320,128,128]{5,4,3,2,1,0:T(8,128)(2,1)} %values.15), custom_call_target="tpu_custom_call" | custom-call | flops 10737418240 | bytes 10485760 | tf_op jit(solution)/shard_map/product/pallas_call | solution.py:113
  208.0 2.5 %collective-permute-start.27 = (s16[1040,128]{1,0:T(8,128)(2,1)}, s16[1040,128]{1,0:T(8,128)(2,1)S(1)}, u32[]{:S(2)}, u32[]{:S(2)}) collective-permute-start(s16[1040,128]{1,0:T(8,128)(2,1)} %get-tuple-element.68), channel_id=1, source_target_pairs={{0,3},{1,0},{2,1},{3,2},{4,7},{5,4},{6,5},{7,6},{8,11},{9,8},{10,9... | collective-permute-start | bytes 798728 | tf_op jit(solution)/shard_map/ppermute | solution.py:250
  211.3 2.5 %middle.7 = s16[1040,128]{1,0:T(8,128)(2,1)} custom-call(s16[1040,128]{1,0:T(8,128)(2,1)} %get-tuple-element.62.a, s16[1040,128]{1,0:T(8,128)(2,1)} %copy-done.12, s16[1040,128]{1,0:T(8,128)(2,1)} %copy-done.17, s16[1040,128]{1,0:T(8,128)(2,1)} %copy-done.21), custom_call_target="tpu_custom_call" | custom-call | flops 2129920 | bytes 1064960 | tf_op jit(solution)/shard_map/middle/pallas_call | solution.py:185
  216.1 4.5 %collective-permute-done.26.refs_3_ = s16[1040,128]{1,0:T(8,128)(2,1)S(1)} collective-permute-done((s16[1040,128]{1,0:T(8,128)(2,1)}, s16[1040,128]{1,0:T(8,128)(2,1)S(1)}, u32[]{:S(2)}, u32[]{:S(2)}) %collective-permute-start.26) | collective-permute-done | bytes 266272 | tf_op jit(solution)/shard_map/ppermute | solution.py:250
  223.8 2.5 %combine.7 = bf16[512,512]{1,0:T(8,128)(2,1)} custom-call(s16[1040,128]{1,0:T(8,128)(2,1)} %get-tuple-element.50.refs_0_, s16[1040,128]{1,0:T(8,128)(2,1)} %copy-done.27, s16[1040,128]{1,0:T(8,128)(2,1)} %copy-done.24, s16[1040,128]{1,0:T(8,128)(2,1)} %copy-done.25, s16[1040,128]{1,0:T(8,128)(2,1)} %copy-done.26, ...), custom_call_target="tpu_custom_call", output_to_operand_aliasing={{}: (6, {})} | custom-call | flops 2129920 | bytes 1331200 | tf_op jit(solution)/shard_map/combine/pallas_call | solution.py:227
  (123 shorter events, 34.5 us)
Async XLA Ops:
  6.5 42.5 %all-gather.11.cloned.1.call-start = ((), (), s32[]{:S(2)}) async-start(), calls=%async_computation.1 | async-start | bytes 4456448 | tf_op jit(solution)/shard_map/all_gather | solution.py:267
  8.4 87.2 %all-gather.9.cloned.1.call-start = ((), (), s32[]{:S(2)}) async-start(), calls=%async_computation | async-start | bytes 4456448 | tf_op jit(solution)/shard_map/all_gather | solution.py:267
  9.2 130.8 %all-gather.15.cloned.1.call-start = ((), (), s32[]{:S(2)}) async-start(), calls=%async_computation.3 | async-start | bytes 4456448 | tf_op jit(solution)/shard_map/all_gather | solution.py:267
  58.6 16.0 %collective-permute-start = (s16[1040,128]{1,0:T(8,128)(2,1)}, s16[1040,128]{1,0:T(8,128)(2,1)S(1)}, u32[]{:S(2)}, u32[]{:S(2)}) collective-permute-start(s16[1040,128]{1,0:T(8,128)(2,1)} %get-tuple-element.39), channel_id=1, source_target_pairs={{0,1},{1,2},{2,3},{3,0},{4,5},{5,6},{6,7},{7,4},{8,9},{9,10},{10,1... | collective-permute-start | bytes 798728 | tf_op jit(solution)/shard_map/ppermute | solution.py:246
  58.6 19.0 %collective-permute-start.1 = (s16[1040,128]{1,0:T(8,128)(2,1)}, s16[1040,128]{1,0:T(8,128)(2,1)S(1)}, u32[]{:S(2)}, u32[]{:S(2)}) collective-permute-start(s16[1040,128]{1,0:T(8,128)(2,1)} %get-tuple-element.40), channel_id=1, source_target_pairs={{0,2},{1,3},{2,0},{3,1},{4,6},{5,7},{6,4},{7,5},{8,10},{9,11},{10,... | collective-permute-start | bytes 798728 | tf_op jit(solution)/shard_map/ppermute | solution.py:246
  62.6 15.0 %collective-permute-start.2 = (s16[1040,128]{1,0:T(8,128)(2,1)}, s16[1040,128]{1,0:T(8,128)(2,1)S(1)}, u32[]{:S(2)}, u32[]{:S(2)}) collective-permute-start(s16[1040,128]{1,0:T(8,128)(2,1)} %get-tuple-element.41), channel_id=1, source_target_pairs={{0,3},{1,0},{2,1},{3,2},{4,7},{5,4},{6,5},{7,6},{8,11},{9,8},{10,9... | collective-permute-start | bytes 798728 | tf_op jit(solution)/shard_map/ppermute | solution.py:246
  74.2 13.7 %collective-permute-start.11 = (s16[1040,128]{1,0:T(8,128)(2,1)}, s16[1040,128]{1,0:T(8,128)(2,1)S(1)}, u32[]{:S(2)}, u32[]{:S(2)}) collective-permute-start(s16[1040,128]{1,0:T(8,128)(2,1)} %get-tuple-element.51), channel_id=1, source_target_pairs={{0,1},{1,2},{2,3},{3,0},{4,5},{5,6},{6,7},{7,4},{8,9},{9,10},{10,1... | collective-permute-start | bytes 798728 | tf_op jit(solution)/shard_map/ppermute | solution.py:250
  74.3 13.6 %collective-permute-start.12 = (s16[1040,128]{1,0:T(8,128)(2,1)}, s16[1040,128]{1,0:T(8,128)(2,1)S(1)}, u32[]{:S(2)}, u32[]{:S(2)}) collective-permute-start(s16[1040,128]{1,0:T(8,128)(2,1)} %get-tuple-element.52), channel_id=1, source_target_pairs={{0,2},{1,3},{2,0},{3,1},{4,6},{5,7},{6,4},{7,5},{8,10},{9,11},{10,... | collective-permute-start | bytes 798728 | tf_op jit(solution)/shard_map/ppermute | solution.py:250
  74.6 14.0 %collective-permute-start.13 = (s16[1040,128]{1,0:T(8,128)(2,1)}, s16[1040,128]{1,0:T(8,128)(2,1)S(1)}, u32[]{:S(2)}, u32[]{:S(2)}) collective-permute-start(s16[1040,128]{1,0:T(8,128)(2,1)} %get-tuple-element.53), channel_id=1, source_target_pairs={{0,3},{1,0},{2,1},{3,2},{4,7},{5,4},{6,5},{7,6},{8,11},{9,8},{10,9... | collective-permute-start | bytes 798728 | tf_op jit(solution)/shard_map/ppermute | solution.py:250
  81.0 11.3 %collective-permute-start.10 = (s16[1040,128]{1,0:T(8,128)(2,1)}, s16[1040,128]{1,0:T(8,128)(2,1)S(1)}, u32[]{:S(2)}, u32[]{:S(2)}) collective-permute-start(s16[1040,128]{1,0:T(8,128)(2,1)} %middle.4.refs_0_), channel_id=1, source_target_pairs={{0,4},{1,5},{2,6},{3,7},{4,0},{5,1},{6,2},{7,3},{8,12},{9,13},{10,... | collective-permute-start | bytes 798728 | tf_op jit(solution)/shard_map/ppermute | solution.py:249
  95.5 88.9 %all-gather.13.cloned.1.call-start = ((), (), s32[]{:S(2)}) async-start(), calls=%async_computation.2 | async-start | bytes 4456448 | tf_op jit(solution)/shard_map/all_gather | solution.py:267
  105.2 15.9 %collective-permute-start.3 = (s16[1040,128]{1,0:T(8,128)(2,1)}, s16[1040,128]{1,0:T(8,128)(2,1)S(1)}, u32[]{:S(2)}, u32[]{:S(2)}) collective-permute-start(s16[1040,128]{1,0:T(8,128)(2,1)} %get-tuple-element.44), channel_id=1, source_target_pairs={{0,1},{1,2},{2,3},{3,0},{4,5},{5,6},{6,7},{7,4},{8,9},{9,10},{10,1... | collective-permute-start | bytes 798728 | tf_op jit(solution)/shard_map/ppermute | solution.py:246
  105.3 18.8 %collective-permute-start.4 = (s16[1040,128]{1,0:T(8,128)(2,1)}, s16[1040,128]{1,0:T(8,128)(2,1)S(1)}, u32[]{:S(2)}, u32[]{:S(2)}) collective-permute-start(s16[1040,128]{1,0:T(8,128)(2,1)} %get-tuple-element.45), channel_id=1, source_target_pairs={{0,2},{1,3},{2,0},{3,1},{4,6},{5,7},{6,4},{7,5},{8,10},{9,11},{10,... | collective-permute-start | bytes 798728 | tf_op jit(solution)/shard_map/ppermute | solution.py:246
  109.1 14.9 %collective-permute-start.5 = (s16[1040,128]{1,0:T(8,128)(2,1)}, s16[1040,128]{1,0:T(8,128)(2,1)S(1)}, u32[]{:S(2)}, u32[]{:S(2)}) collective-permute-start(s16[1040,128]{1,0:T(8,128)(2,1)} %get-tuple-element.46), channel_id=1, source_target_pairs={{0,3},{1,0},{2,1},{3,2},{4,7},{5,4},{6,5},{7,6},{8,11},{9,8},{10,9... | collective-permute-start | bytes 798728 | tf_op jit(solution)/shard_map/ppermute | solution.py:246
  120.7 8.1 %collective-permute-start.7 = (s16[1040,128]{1,0:T(8,128)(2,1)}, s16[1040,128]{1,0:T(8,128)(2,1)S(1)}, u32[]{:S(2)}, u32[]{:S(2)}) collective-permute-start(s16[1040,128]{1,0:T(8,128)(2,1)} %get-tuple-element.47), channel_id=1, source_target_pairs={{0,1},{1,2},{2,3},{3,0},{4,5},{5,6},{6,7},{7,4},{8,9},{9,10},{10,1... | collective-permute-start | bytes 798728 | tf_op jit(solution)/shard_map/ppermute | solution.py:250
  120.7 13.3 %collective-permute-start.8 = (s16[1040,128]{1,0:T(8,128)(2,1)}, s16[1040,128]{1,0:T(8,128)(2,1)S(1)}, u32[]{:S(2)}, u32[]{:S(2)}) collective-permute-start(s16[1040,128]{1,0:T(8,128)(2,1)} %get-tuple-element.48), channel_id=1, source_target_pairs={{0,2},{1,3},{2,0},{3,1},{4,6},{5,7},{6,4},{7,5},{8,10},{9,11},{10,... | collective-permute-start | bytes 798728 | tf_op jit(solution)/shard_map/ppermute | solution.py:250
  121.1 13.6 %collective-permute-start.9 = (s16[1040,128]{1,0:T(8,128)(2,1)}, s16[1040,128]{1,0:T(8,128)(2,1)S(1)}, u32[]{:S(2)}, u32[]{:S(2)}) collective-permute-start(s16[1040,128]{1,0:T(8,128)(2,1)} %get-tuple-element.49), channel_id=1, source_target_pairs={{0,3},{1,0},{2,1},{3,2},{4,7},{5,4},{6,5},{7,6},{8,11},{9,8},{10,9... | collective-permute-start | bytes 798728 | tf_op jit(solution)/shard_map/ppermute | solution.py:250
  127.4 9.4 %collective-permute-start.6 = (s16[1040,128]{1,0:T(8,128)(2,1)}, s16[1040,128]{1,0:T(8,128)(2,1)S(1)}, u32[]{:S(2)}, u32[]{:S(2)}) collective-permute-start(s16[1040,128]{1,0:T(8,128)(2,1)} %middle.5), channel_id=1, source_target_pairs={{0,4},{1,5},{2,6},{3,7},{4,0},{5,1},{6,2},{7,3},{8,12},{9,13},{10,... | collective-permute-start | bytes 798728 | tf_op jit(solution)/shard_map/ppermute | solution.py:249
  148.8 15.4 %collective-permute-start.14 = (s16[1040,128]{1,0:T(8,128)(2,1)}, s16[1040,128]{1,0:T(8,128)(2,1)S(1)}, u32[]{:S(2)}, u32[]{:S(2)}) collective-permute-start(s16[1040,128]{1,0:T(8,128)(2,1)} %get-tuple-element.56), channel_id=1, source_target_pairs={{0,1},{1,2},{2,3},{3,0},{4,5},{5,6},{6,7},{7,4},{8,9},{9,10},{10,1... | collective-permute-start | bytes 798728 | tf_op jit(solution)/shard_map/ppermute | solution.py:246
  150.3 16.6 %collective-permute-start.15 = (s16[1040,128]{1,0:T(8,128)(2,1)}, s16[1040,128]{1,0:T(8,128)(2,1)S(1)}, u32[]{:S(2)}, u32[]{:S(2)}) collective-permute-start(s16[1040,128]{1,0:T(8,128)(2,1)} %get-tuple-element.57), channel_id=1, source_target_pairs={{0,2},{1,3},{2,0},{3,1},{4,6},{5,7},{6,4},{7,5},{8,10},{9,11},{10,... | collective-permute-start | bytes 798728 | tf_op jit(solution)/shard_map/ppermute | solution.py:246
  153.7 13.2 %collective-permute-start.16 = (s16[1040,128]{1,0:T(8,128)(2,1)}, s16[1040,128]{1,0:T(8,128)(2,1)S(1)}, u32[]{:S(2)}, u32[]{:S(2)}) collective-permute-start(s16[1040,128]{1,0:T(8,128)(2,1)} %get-tuple-element.58), channel_id=1, source_target_pairs={{0,3},{1,0},{2,1},{3,2},{4,7},{5,4},{6,5},{7,6},{8,11},{9,8},{10,9... | collective-permute-start | bytes 798728 | tf_op jit(solution)/shard_map/ppermute | solution.py:246
  162.5 9.9 %collective-permute-start.18 = (s16[1040,128]{1,0:T(8,128)(2,1)}, s16[1040,128]{1,0:T(8,128)(2,1)S(1)}, u32[]{:S(2)}, u32[]{:S(2)}) collective-permute-start(s16[1040,128]{1,0:T(8,128)(2,1)} %get-tuple-element.59), channel_id=1, source_target_pairs={{0,1},{1,2},{2,3},{3,0},{4,5},{5,6},{6,7},{7,4},{8,9},{9,10},{10,1... | collective-permute-start | bytes 798728 | tf_op jit(solution)/shard_map/ppermute | solution.py:250
  164.1 13.8 %collective-permute-start.19 = (s16[1040,128]{1,0:T(8,128)(2,1)}, s16[1040,128]{1,0:T(8,128)(2,1)S(1)}, u32[]{:S(2)}, u32[]{:S(2)}) collective-permute-start(s16[1040,128]{1,0:T(8,128)(2,1)} %get-tuple-element.60), channel_id=1, source_target_pairs={{0,2},{1,3},{2,0},{3,1},{4,6},{5,7},{6,4},{7,5},{8,10},{9,11},{10,... | collective-permute-start | bytes 798728 | tf_op jit(solution)/shard_map/ppermute | solution.py:250
  164.2 13.7 %collective-permute-start.20 = (s16[1040,128]{1,0:T(8,128)(2,1)}, s16[1040,128]{1,0:T(8,128)(2,1)S(1)}, u32[]{:S(2)}, u32[]{:S(2)}) collective-permute-start(s16[1040,128]{1,0:T(8,128)(2,1)} %get-tuple-element.61), channel_id=1, source_target_pairs={{0,3},{1,0},{2,1},{3,2},{4,7},{5,4},{6,5},{7,6},{8,11},{9,8},{10,9... | collective-permute-start | bytes 798728 | tf_op jit(solution)/shard_map/ppermute | solution.py:250
  170.2 11.0 %collective-permute-start.17 = (s16[1040,128]{1,0:T(8,128)(2,1)}, s16[1040,128]{1,0:T(8,128)(2,1)S(1)}, u32[]{:S(2)}, u32[]{:S(2)}) collective-permute-start(s16[1040,128]{1,0:T(8,128)(2,1)} %middle.6), channel_id=1, source_target_pairs={{0,4},{1,5},{2,6},{3,7},{4,0},{5,1},{6,2},{7,3},{8,12},{9,13},{10,... | collective-permute-start | bytes 798728 | tf_op jit(solution)/shard_map/ppermute | solution.py:249
  193.3 14.7 %collective-permute-start.21 = (s16[1040,128]{1,0:T(8,128)(2,1)}, s16[1040,128]{1,0:T(8,128)(2,1)S(1)}, u32[]{:S(2)}, u32[]{:S(2)}) collective-permute-start(s16[1040,128]{1,0:T(8,128)(2,1)} %get-tuple-element.63), channel_id=1, source_target_pairs={{0,1},{1,2},{2,3},{3,0},{4,5},{5,6},{6,7},{7,4},{8,9},{9,10},{10,1... | collective-permute-start | bytes 798728 | tf_op jit(solution)/shard_map/ppermute | solution.py:246
  194.2 16.4 %collective-permute-start.22 = (s16[1040,128]{1,0:T(8,128)(2,1)}, s16[1040,128]{1,0:T(8,128)(2,1)S(1)}, u32[]{:S(2)}, u32[]{:S(2)}) collective-permute-start(s16[1040,128]{1,0:T(8,128)(2,1)} %get-tuple-element.64), channel_id=1, source_target_pairs={{0,2},{1,3},{2,0},{3,1},{4,6},{5,7},{6,4},{7,5},{8,10},{9,11},{10,... | collective-permute-start | bytes 798728 | tf_op jit(solution)/shard_map/ppermute | solution.py:246
  197.4 13.1 %collective-permute-start.23 = (s16[1040,128]{1,0:T(8,128)(2,1)}, s16[1040,128]{1,0:T(8,128)(2,1)S(1)}, u32[]{:S(2)}, u32[]{:S(2)}) collective-permute-start(s16[1040,128]{1,0:T(8,128)(2,1)} %get-tuple-element.65), channel_id=1, source_target_pairs={{0,3},{1,0},{2,1},{3,2},{4,7},{5,4},{6,5},{7,6},{8,11},{9,8},{10,9... | collective-permute-start | bytes 798728 | tf_op jit(solution)/shard_map/ppermute | solution.py:246
  206.2 9.9 %collective-permute-start.25 = (s16[1040,128]{1,0:T(8,128)(2,1)}, s16[1040,128]{1,0:T(8,128)(2,1)S(1)}, u32[]{:S(2)}, u32[]{:S(2)}) collective-permute-start(s16[1040,128]{1,0:T(8,128)(2,1)} %get-tuple-element.66), channel_id=1, source_target_pairs={{0,1},{1,2},{2,3},{3,0},{4,5},{5,6},{6,7},{7,4},{8,9},{9,10},{10,1... | collective-permute-start | bytes 798728 | tf_op jit(solution)/shard_map/ppermute | solution.py:250
  207.8 12.9 %collective-permute-start.26 = (s16[1040,128]{1,0:T(8,128)(2,1)}, s16[1040,128]{1,0:T(8,128)(2,1)S(1)}, u32[]{:S(2)}, u32[]{:S(2)}) collective-permute-start(s16[1040,128]{1,0:T(8,128)(2,1)} %get-tuple-element.67), channel_id=1, source_target_pairs={{0,2},{1,3},{2,0},{3,1},{4,6},{5,7},{6,4},{7,5},{8,10},{9,11},{10,... | collective-permute-start | bytes 798728 | tf_op jit(solution)/shard_map/ppermute | solution.py:250
  208.0 13.2 %collective-permute-start.27 = (s16[1040,128]{1,0:T(8,128)(2,1)}, s16[1040,128]{1,0:T(8,128)(2,1)S(1)}, u32[]{:S(2)}, u32[]{:S(2)}) collective-permute-start(s16[1040,128]{1,0:T(8,128)(2,1)} %get-tuple-element.68), channel_id=1, source_target_pairs={{0,3},{1,0},{2,1},{3,2},{4,7},{5,4},{6,5},{7,6},{8,11},{9,8},{10,9... | collective-permute-start | bytes 798728 | tf_op jit(solution)/shard_map/ppermute | solution.py:250
  213.8 9.2 %collective-permute-start.24 = (s16[1040,128]{1,0:T(8,128)(2,1)}, s16[1040,128]{1,0:T(8,128)(2,1)S(1)}, u32[]{:S(2)}, u32[]{:S(2)}) collective-permute-start(s16[1040,128]{1,0:T(8,128)(2,1)} %middle.7), channel_id=1, source_target_pairs={{0,4},{1,5},{2,6},{3,7},{4,0},{5,1},{6,2},{7,3},{8,12},{9,13},{10,... | collective-permute-start | bytes 798728 | tf_op jit(solution)/shard_map/ppermute | solution.py:249
  (29 other events, 88.1 us)
Sparse Core Ops, SparseCore 0:
  9.1 39.9 all-gather.10
  50.7 38.3 all-gather.8
  95.6 37.1 all-gather.14
  140.1 37.5 all-gather.12

commit v3 on v2

--- a/solution.py
+++ b/solution.py
@@ -14,7 +14,7 @@
 N_Y = 4
 SUB = CB // N_COL
 HALF = CB // 2
-GROUP = 16
+GROUP = 32
 ROW_AT, COLUMN_AT = 9, 15
 HEIGHTS = (256, 256)
 STEPS = 16.0
@@ -52,7 +52,7 @@
     *outs, panel, held, acc, part_sem, sems = refs[-N_Y - 5 :]
     height = panel.shape[1]
     groups = (count[0] + GROUP - 1) // GROUP
-    ahead = 4
+    ahead = 2
 
     def fetch(group):
         @pl.when(group < groups)
@@ -273,7 +273,7 @@
                 current[c] = combine(pieces, bias[layer])
             else:
                 result = combine(pieces, bias[layer], firsts[c], batch, result)
-                after = [result]
+                after = after + pieces[2:]
     return result[:, None, :]
 
 

time: 232 us -> 226 us (0.974); the launches traced: 233 us -> 224 us
  Pallas kernels: 92.4 us -> 72.8 us
  starting transfers between devices: 41.9 us -> 54.5 us
  waiting for transfers between devices: 72.8 us -> 69.9 us
    pallas_call x8, Pallas kernels: 72.3 us -> 52.7 us  [product(): pl.pallas_call(functools.partial(product_kernel, layer), out_shape=(piece...]
    ppermute x12, waiting for transfers between devices: 25.2 us -> 6.92 us  [exchange(): lax.ppermute(near[d], 'col', to_col(0, d))]
    ppermute x4, starting transfers between devices: 4.3 us -> 12.6 us  [exchange(): pieces = [near[0], lax.ppermute(sent, 'col', to_col(1, 0))]]
    all_gather x4, waiting for transfers between devices: 36.1 us -> 43.8 us  [on_device(): gathered = lax.all_gather(current[c], 'row', axis=0, tiled=False)]
    ppermute x4, waiting for transfers between devices: 10.7 us -> 17.1 us  [exchange(): pieces = [near[0], lax.ppermute(sent, 'col', to_col(1, 0))]]
    ppermute x12, starting transfers between devices: 22 us -> 25.2 us  [exchange(): lax.ppermute(far[d], 'col', to_col(0, d))]
    unnamed x59 -> x61, local copies, waits for them, and re-layouts: 6.03 us -> 6.85 us
  transfers between devices with their start and end apart: 32 -> 32, of which waited for: 14 -> 9; matrix products, arithmetic and copies ran while one was open for 2% -> 2% of each run, Pallas kernels for 35% -> 28%
where the time goes in v3:
time: 226 us; the launch traced here: 224 us
  Pallas kernels  72.8 us (32%)
  waiting for transfers between devices  69.9 us (31%)
  starting transfers between devices  54.5 us (24%)
  between operations  13.4 us (6%)
  local copies, waits for them, and re-layouts  10.6 us (5%)
  other arithmetic  2.49 us (1%)
    pallas_call x8, Pallas kernels, product(): pl.pallas_call(functools.partial(product_kernel, layer), out_shape=(piece...  52.7 us
    all_gather x4, waiting for transfers between devices, on_device(): gathered = lax.all_gather(current[c], 'row', axis=0, tiled=False)  43.8 us
    ppermute x12, starting transfers between devices, exchange(): lax.ppermute(far[d], 'col', to_col(0, d))  25.2 us
    ppermute x4, waiting for transfers between devices, exchange(): pieces = [near[0], lax.ppermute(sent, 'col', to_col(1, 0))]  17.1 us
    ppermute x12, starting transfers between devices, exchange(): lax.ppermute(near[d], 'col', to_col(0, d))  16.6 us
    ppermute x4, starting transfers between devices, exchange(): pieces = [near[0], lax.ppermute(sent, 'col', to_col(1, 0))]  12.6 us
    pallas_call x4, Pallas kernels, combine(): pl.pallas_call(functools.partial(combine_kernel, n_pieces, first), out_sh...  10.1 us
    pallas_call x4, Pallas kernels, middle(): pl.pallas_call(middle_kernel, out_shape=jax.ShapeDtypeStruct(pieces[0].sh...  10 us
  transfers between devices with their start and end apart: 32, of which 9 were waited for; matrix products, arithmetic and copies ran while one was open for 2% of the time, Pallas kernels for 28%

profile of v3, /device:TPU:0, one launch (start us, length us, event | category | flops | bytes accessed | tf_op | source)
XLA Modules:
  0.0 223.7 jit_solution(16690260160293218130)
XLA Ops:
  13.0 36.0 %all-gather.11.cloned.1.call-done = bf16[4096,1,512]{2,0,1:T(8,128)(2,1)} async-done(((bf16[256,1,512]{2,0,1:T(8,128)(2,1)}), bf16[4096,1,512]{2,0,1:T(8,128)(2,1)}) %all-gather.11.cloned.1.call-update) | async-done | bytes 4194320 | tf_op jit(solution)/shard_map/all_gather | solution.py:267
  49.0 6.5 %product.9 = (s16[1040,128]{1,0:T(8,128)(2,1)}, s16[1040,128]{1,0:T(8,128)(2,1)}, s16[1040,128]{1,0:T(8,128)(2,1)}, s16[1040,128]{1,0:T(8,128)(2,1)}) custom-call(s32[320]{0:T(512)} %get-tuple-element.70.codes, s32[1]{0:T(128)} %bitcast.4.count, bf16[16,256,512]{2,1,0:T(8,128)(2,1)} %bitcast.25, bf16[2,1,1,320,128,128]{5,4,3,2,1,0:T(8,128)(2,1)} %values.15), custom_call_target="tpu_custom_call" | custom-call | flops 10737418240 | bytes 10485760 | tf_op jit(solution)/shard_map/product/pallas_call | solution.py:113
  55.6 2.4 %collective-permute-start = (s16[1040,128]{1,0:T(8,128)(2,1)}, s16[1040,128]{1,0:T(8,128)(2,1)S(1)}, u32[]{:S(2)}, u32[]{:S(2)}) collective-permute-start(s16[1040,128]{1,0:T(8,128)(2,1)} %get-tuple-element.39), channel_id=1, source_target_pairs={{0,1},{1,2},{2,3},{3,0},{4,5},{5,6},{6,7},{7,4},{8,9},{9,10},{10,1... | collective-permute-start | bytes 798728 | tf_op jit(solution)/shard_map/ppermute | solution.py:246
  62.0 6.7 %product.10 = (s16[1040,128]{1,0:T(8,128)(2,1)}, s16[1040,128]{1,0:T(8,128)(2,1)}, s16[1040,128]{1,0:T(8,128)(2,1)}, s16[1040,128]{1,0:T(8,128)(2,1)}) custom-call(s32[320]{0:T(512)} %get-tuple-element.71.codes, s32[1]{0:T(128)} %bitcast.2.count, bf16[16,256,512]{2,1,0:T(8,128)(2,1)} %bitcast.26, bf16[2,1,1,320,128,128]{5,4,3,2,1,0:T(8,128)(2,1)} %values.15), custom_call_target="tpu_custom_call" | custom-call | flops 10737418240 | bytes 10485760 | tf_op jit(solution)/shard_map/product/pallas_call | solution.py:113
  69.5 2.6 %collective-permute-start.13 = (s16[1040,128]{1,0:T(8,128)(2,1)}, s16[1040,128]{1,0:T(8,128)(2,1)S(1)}, u32[]{:S(2)}, u32[]{:S(2)}) collective-permute-start(s16[1040,128]{1,0:T(8,128)(2,1)} %get-tuple-element.53), channel_id=1, source_target_pairs={{0,3},{1,0},{2,1},{3,2},{4,7},{5,4},{6,5},{7,6},{8,11},{9,8},{10,9... | collective-permute-start | bytes 798728 | tf_op jit(solution)/shard_map/ppermute | solution.py:250
  73.8 2.5 %middle.4.refs_0_ = s16[1040,128]{1,0:T(8,128)(2,1)} custom-call(s16[1040,128]{1,0:T(8,128)(2,1)} %get-tuple-element.38.a, s16[1040,128]{1,0:T(8,128)(2,1)} %copy-done.16, s16[1040,128]{1,0:T(8,128)(2,1)} %copy-done.20, s16[1040,128]{1,0:T(8,128)(2,1)} %copy-done.23), custom_call_target="tpu_custom_call" | custom-call | flops 2129920 | bytes 1064960 | tf_op jit(solution)/shard_map/middle/pallas_call | solution.py:185
  76.3 4.7 %collective-permute-start.10 = (s16[1040,128]{1,0:T(8,128)(2,1)}, s16[1040,128]{1,0:T(8,128)(2,1)S(1)}, u32[]{:S(2)}, u32[]{:S(2)}) collective-permute-start(s16[1040,128]{1,0:T(8,128)(2,1)} %middle.4.refs_0_), channel_id=1, source_target_pairs={{0,4},{1,5},{2,6},{3,7},{4,0},{5,1},{6,2},{7,3},{8,12},{9,13},{10,... | collective-permute-start | bytes 798728 | tf_op jit(solution)/shard_map/ppermute | solution.py:249
  81.6 2.7 %collective-permute-done.12.refs_3_ = s16[1040,128]{1,0:T(8,128)(2,1)S(1)} collective-permute-done((s16[1040,128]{1,0:T(8,128)(2,1)}, s16[1040,128]{1,0:T(8,128)(2,1)S(1)}, u32[]{:S(2)}, u32[]{:S(2)}) %collective-permute-start.12) | collective-permute-done | bytes 266272 | tf_op jit(solution)/shard_map/ppermute | solution.py:250
  84.3 7.5 %collective-permute-done.10.refs_1_ = s16[1040,128]{1,0:T(8,128)(2,1)S(1)} collective-permute-done((s16[1040,128]{1,0:T(8,128)(2,1)}, s16[1040,128]{1,0:T(8,128)(2,1)S(1)}, u32[]{:S(2)}, u32[]{:S(2)}) %collective-permute-start.10) | collective-permute-done | bytes 266272 | tf_op jit(solution)/shard_map/ppermute | solution.py:249
  92.5 2.5 %combine.5 = bf16[256,512]{1,0:T(8,128)(2,1)} custom-call(s16[1040,128]{1,0:T(8,128)(2,1)} %get-tuple-element.42.refs_1_.refs_0_, s16[1040,128]{1,0:T(8,128)(2,1)} %copy-done.6, s16[1040,128]{1,0:T(8,128)(2,1)} %copy-done, s16[1040,128]{1,0:T(8,128)(2,1)} %copy-done.2, s16[1040,128]{1,0:T(8,128)(2,1)} %copy-done.4, f32[1,512]{1,0:T(1,128)} %get-tuple-element.78.refs_5_), custom_call_target="tpu_custom_call" | custom-call | flops 2129920 | bytes 1331200 | tf_op jit(solution)/shard_map/combine/pallas_call | solution.py:227
  95.1 6.6 %product.11 = (s16[1040,128]{1,0:T(8,128)(2,1)}, s16[1040,128]{1,0:T(8,128)(2,1)}, s16[1040,128]{1,0:T(8,128)(2,1)}, s16[1040,128]{1,0:T(8,128)(2,1)}) custom-call(s32[320]{0:T(512)} %get-tuple-element.70.codes, s32[1]{0:T(128)} %bitcast.4.count, bf16[16,256,512]{2,1,0:T(8,128)(2,1)} %bitcast.19, bf16[2,1,1,320,128,128]{5,4,3,2,1,0:T(8,128)(2,1)} %values.15, ...), custom_call_target="tpu_custom_call" | custom-call | flops 10737418240 | bytes 10485760 | tf_op jit(solution)/shard_map/product/pallas_call | solution.py:113
  105.8 2.5 %collective-permute-start.5 = (s16[1040,128]{1,0:T(8,128)(2,1)}, s16[1040,128]{1,0:T(8,128)(2,1)S(1)}, u32[]{:S(2)}, u32[]{:S(2)}) collective-permute-start(s16[1040,128]{1,0:T(8,128)(2,1)} %get-tuple-element.46), channel_id=1, source_target_pairs={{0,3},{1,0},{2,1},{3,2},{4,7},{5,4},{6,5},{7,6},{8,11},{9,8},{10,9... | collective-permute-start | bytes 798728 | tf_op jit(solution)/shard_map/ppermute | solution.py:246
  108.2 6.6 %product.8 = (s16[1040,128]{1,0:T(8,128)(2,1)}, s16[1040,128]{1,0:T(8,128)(2,1)}, s16[1040,128]{1,0:T(8,128)(2,1)}, s16[1040,128]{1,0:T(8,128)(2,1)}) custom-call(s32[320]{0:T(512)} %get-tuple-element.71.codes, s32[1]{0:T(128)} %bitcast.2.count, bf16[16,256,512]{2,1,0:T(8,128)(2,1)} %bitcast.20, bf16[2,1,1,320,128,128]{5,4,3,2,1,0:T(8,128)(2,1)} %values.15), custom_call_target="tpu_custom_call" | custom-call | flops 10737418240 | bytes 10485760 | tf_op jit(solution)/shard_map/product/pallas_call | solution.py:113
  115.7 2.8 %collective-permute-start.9 = (s16[1040,128]{1,0:T(8,128)(2,1)}, s16[1040,128]{1,0:T(8,128)(2,1)S(1)}, u32[]{:S(2)}, u32[]{:S(2)}) collective-permute-start(s16[1040,128]{1,0:T(8,128)(2,1)} %get-tuple-element.49), channel_id=1, source_target_pairs={{0,3},{1,0},{2,1},{3,2},{4,7},{5,4},{6,5},{7,6},{8,11},{9,8},{10,9... | collective-permute-start | bytes 798728 | tf_op jit(solution)/shard_map/ppermute | solution.py:250
  119.7 2.5 %middle.5 = s16[1040,128]{1,0:T(8,128)(2,1)} custom-call(s16[1040,128]{1,0:T(8,128)(2,1)} %get-tuple-element.43.a, s16[1040,128]{1,0:T(8,128)(2,1)} %copy-done.14, s16[1040,128]{1,0:T(8,128)(2,1)} %copy-done.18, s16[1040,128]{1,0:T(8,128)(2,1)} %copy-done.21), custom_call_target="tpu_custom_call" | custom-call | flops 2129920 | bytes 1064960 | tf_op jit(solution)/shard_map/middle/pallas_call | solution.py:185
  122.2 3.2 %collective-permute-start.6 = (s16[1040,128]{1,0:T(8,128)(2,1)}, s16[1040,128]{1,0:T(8,128)(2,1)S(1)}, u32[]{:S(2)}, u32[]{:S(2)}) collective-permute-start(s16[1040,128]{1,0:T(8,128)(2,1)} %middle.5), channel_id=1, source_target_pairs={{0,4},{1,5},{2,6},{3,7},{4,0},{5,1},{6,2},{7,3},{8,12},{9,13},{10,... | collective-permute-start | bytes 798728 | tf_op jit(solution)/shard_map/ppermute | solution.py:249
  125.4 4.2 %collective-permute-done.8.refs_3_ = s16[1040,128]{1,0:T(8,128)(2,1)S(1)} collective-permute-done((s16[1040,128]{1,0:T(8,128)(2,1)}, s16[1040,128]{1,0:T(8,128)(2,1)S(1)}, u32[]{:S(2)}, u32[]{:S(2)}) %collective-permute-start.8) | collective-permute-done | bytes 266272 | tf_op jit(solution)/shard_map/ppermute | solution.py:250
  129.6 4.8 %collective-permute-done.6.refs_1_ = s16[1040,128]{1,0:T(8,128)(2,1)S(1)} collective-permute-done((s16[1040,128]{1,0:T(8,128)(2,1)}, s16[1040,128]{1,0:T(8,128)(2,1)S(1)}, u32[]{:S(2)}, u32[]{:S(2)}) %collective-permute-start.6) | collective-permute-done | bytes 266272 | tf_op jit(solution)/shard_map/ppermute | solution.py:249
  135.1 2.5 %combine.4 = bf16[256,512]{1,0:T(8,128)(2,1)} custom-call(s16[1040,128]{1,0:T(8,128)(2,1)} %get-tuple-element.37.refs_0_, s16[1040,128]{1,0:T(8,128)(2,1)} %copy-done.7, s16[1040,128]{1,0:T(8,128)(2,1)} %copy-done.1, s16[1040,128]{1,0:T(8,128)(2,1)} %copy-done.3, s16[1040,128]{1,0:T(8,128)(2,1)} %copy-done.5, f32[1,512]{1,0:T(1,128)} %get-tuple-element.78.refs_5_), custom_call_target="tpu_custom_call" | custom-call | flops 2129920 | bytes 1331200 | tf_op jit(solution)/shard_map/combine/pallas_call | solution.py:227
  137.7 6.5 %product.13 = (s16[1040,128]{1,0:T(8,128)(2,1)}, s16[1040,128]{1,0:T(8,128)(2,1)}, s16[1040,128]{1,0:T(8,128)(2,1)}, s16[1040,128]{1,0:T(8,128)(2,1)}) custom-call(s32[320]{0:T(512)} %get-tuple-element.69.codes, s32[1]{0:T(128)} %bitcast.8.count, bf16[16,256,512]{2,1,0:T(8,128)(2,1)} %bitcast.21, bf16[2,1,1,320,128,128]{5,4,3,2,1,0:T(8,128)(2,1)} %values.15), custom_call_target="tpu_custom_call" | custom-call | flops 10737418240 | bytes 10485760 | tf_op jit(solution)/shard_map/product/pallas_call | solution.py:113
  144.2 3.4 %collective-permute-start.14 = (s16[1040,128]{1,0:T(8,128)(2,1)}, s16[1040,128]{1,0:T(8,128)(2,1)S(1)}, u32[]{:S(2)}, u32[]{:S(2)}) collective-permute-start(s16[1040,128]{1,0:T(8,128)(2,1)} %get-tuple-element.55), channel_id=1, source_target_pairs={{0,1},{1,2},{2,3},{3,0},{4,5},{5,6},{6,7},{7,4},{8,9},{9,10},{10,1... | collective-permute-start | bytes 798728 | tf_op jit(solution)/shard_map/ppermute | solution.py:246
  150.3 6.7 %product.14 = (s16[1040,128]{1,0:T(8,128)(2,1)}, s16[1040,128]{1,0:T(8,128)(2,1)}, s16[1040,128]{1,0:T(8,128)(2,1)}, s16[1040,128]{1,0:T(8,128)(2,1)}) custom-call(s32[320]{0:T(512)} %get-tuple-element.72.codes, s32[1]{0:T(128)} %bitcast.1.count, bf16[16,256,512]{2,1,0:T(8,128)(2,1)} %bitcast.22, bf16[2,1,1,320,128,128]{5,4,3,2,1,0:T(8,128)(2,1)} %values.15), custom_call_target="tpu_custom_call" | custom-call | flops 10737418240 | bytes 10485760 | tf_op jit(solution)/shard_map/product/pallas_call | solution.py:113
  162.4 2.5 %middle.6.refs_0_ = s16[1040,128]{1,0:T(8,128)(2,1)} custom-call(s16[1040,128]{1,0:T(8,128)(2,1)} %get-tuple-element.54.a, s16[1040,128]{1,0:T(8,128)(2,1)} %copy-done.15, s16[1040,128]{1,0:T(8,128)(2,1)} %copy-done.19, s16[1040,128]{1,0:T(8,128)(2,1)} %copy-done.22), custom_call_target="tpu_custom_call" | custom-call | flops 2129920 | bytes 1064960 | tf_op jit(solution)/shard_map/middle/pallas_call | solution.py:185
  164.9 7.8 %all-gather.13.cloned.1.call-done = bf16[4096,512]{1,0:T(8,128)(2,1)} async-done(((bf16[256,512]{1,0:T(8,128)(2,1)}), bf16[4096,512]{1,0:T(8,128)(2,1)}) %all-gather.13.cloned.1.call-update) | async-done | bytes 4194320 | tf_op jit(solution)/shard_map/all_gather | solution.py:267
  173.7 6.5 %product.15 = (s16[1040,128]{1,0:T(8,128)(2,1)}, s16[1040,128]{1,0:T(8,128)(2,1)}, s16[1040,128]{1,0:T(8,128)(2,1)}, s16[1040,128]{1,0:T(8,128)(2,1)}) custom-call(s32[320]{0:T(512)} %get-tuple-element.69.codes, s32[1]{0:T(128)} %bitcast.8.count, bf16[16,256,512]{2,1,0:T(8,128)(2,1)} %bitcast.23, bf16[2,1,1,320,128,128]{5,4,3,2,1,0:T(8,128)(2,1)} %values.15, ...), custom_call_target="tpu_custom_call" | custom-call | flops 10737418240 | bytes 10485760 | tf_op jit(solution)/shard_map/product/pallas_call | solution.py:113
  180.2 3.3 %collective-permute-start.20 = (s16[1040,128]{1,0:T(8,128)(2,1)}, s16[1040,128]{1,0:T(8,128)(2,1)S(1)}, u32[]{:S(2)}, u32[]{:S(2)}) collective-permute-start(s16[1040,128]{1,0:T(8,128)(2,1)} %get-tuple-element.63), channel_id=1, source_target_pairs={{0,1},{1,2},{2,3},{3,0},{4,5},{5,6},{6,7},{7,4},{8,9},{9,10},{10,1... | collective-permute-start | bytes 798728 | tf_op jit(solution)/shard_map/ppermute | solution.py:246
  186.2 6.6 %product.12 = (s16[1040,128]{1,0:T(8,128)(2,1)}, s16[1040,128]{1,0:T(8,128)(2,1)}, s16[1040,128]{1,0:T(8,128)(2,1)}, s16[1040,128]{1,0:T(8,128)(2,1)}) custom-call(s32[320]{0:T(512)} %get-tuple-element.72.codes, s32[1]{0:T(128)} %bitcast.1.count, bf16[16,256,512]{2,1,0:T(8,128)(2,1)} %bitcast.24, bf16[2,1,1,320,128,128]{5,4,3,2,1,0:T(8,128)(2,1)} %values.15), custom_call_target="tpu_custom_call" | custom-call | flops 10737418240 | bytes 10485760 | tf_op jit(solution)/shard_map/product/pallas_call | solution.py:113
  195.7 4.7 %collective-permute-start.27 = (s16[1040,128]{1,0:T(8,128)(2,1)S(1)}, s16[1040,128]{1,0:T(8,128)(2,1)S(1)}, u32[]{:S(2)}, u32[]{:S(2)}) collective-permute-start(s16[1040,128]{1,0:T(8,128)(2,1)S(1)} %copy-done.11), channel_id=1, source_target_pairs={{0,4},{1,5},{2,6},{3,7},{4,0},{5,1},{6,2},{7,3},{8,12},{9,13},{10,... | collective-permute-start | bytes 798728 | tf_op jit(solution)/shard_map/ppermute | solution.py:249
  203.3 2.5 %middle.7 = s16[1040,128]{1,0:T(8,128)(2,1)} custom-call(s16[1040,128]{1,0:T(8,128)(2,1)} %get-tuple-element.62.a, s16[1040,128]{1,0:T(8,128)(2,1)} %copy-done.12, s16[1040,128]{1,0:T(8,128)(2,1)} %copy-done.13, s16[1040,128]{1,0:T(8,128)(2,1)} %copy-done.17), custom_call_target="tpu_custom_call" | custom-call | flops 2129920 | bytes 1064960 | tf_op jit(solution)/shard_map/middle/pallas_call | solution.py:185
  206.6 2.5 %combine.6.refs_6_ = bf16[512,512]{1,0:T(8,128)(2,1)} custom-call(s16[1040,128]{1,0:T(8,128)(2,1)} %get-tuple-element.58.refs_1_.refs_0_, s16[1040,128]{1,0:T(8,128)(2,1)} %copy-done.24, s16[1040,128]{1,0:T(8,128)(2,1)} %copy-done.8, s16[1040,128]{1,0:T(8,128)(2,1)} %copy-done.9, s16[1040,128]{1,0:T(8,128)(2,1)} %copy-done.10, ...), custom_call_target="tpu_custom_call" | custom-call | flops 2129920 | bytes 1331200 | tf_op jit(solution)/shard_map/combine/pallas_call | solution.py:227
  209.2 4.7 %collective-permute-done.23.refs_1_ = s16[1040,128]{1,0:T(8,128)(2,1)S(1)} collective-permute-done((s16[1040,128]{1,0:T(8,128)(2,1)}, s16[1040,128]{1,0:T(8,128)(2,1)S(1)}, u32[]{:S(2)}, u32[]{:S(2)}) %collective-permute-start.23) | collective-permute-done | bytes 266272 | tf_op jit(solution)/shard_map/ppermute | solution.py:249
  214.7 2.5 %combine.7 = bf16[512,512]{1,0:T(8,128)(2,1)} custom-call(s16[1040,128]{1,0:T(8,128)(2,1)} %get-tuple-element.50.refs_0_, s16[1040,128]{1,0:T(8,128)(2,1)} %copy-done.28, s16[1040,128]{1,0:T(8,128)(2,1)} %copy-done.25, s16[1040,128]{1,0:T(8,128)(2,1)} %copy-done.26, s16[1040,128]{1,0:T(8,128)(2,1)} %copy-done.27, ...), custom_call_target="tpu_custom_call", output_to_operand_aliasing={{}: (6, {})} | custom-call | flops 2129920 | bytes 1331200 | tf_op jit(solution)/shard_map/combine/pallas_call | solution.py:227
  (125 shorter events, 40.4 us)
Async XLA Ops:
  6.5 42.5 %all-gather.11.cloned.1.call-start = ((), (), s32[]{:S(2)}) async-start(), calls=%async_computation.1 | async-start | bytes 4456448 | tf_op jit(solution)/shard_map/all_gather | solution.py:267
  8.4 86.7 %all-gather.9.cloned.1.call-start = ((), (), s32[]{:S(2)}) async-start(), calls=%async_computation | async-start | bytes 4456448 | tf_op jit(solution)/shard_map/all_gather | solution.py:267
  9.2 128.5 %all-gather.15.cloned.1.call-start = ((), (), s32[]{:S(2)}) async-start(), calls=%async_computation.3 | async-start | bytes 4456448 | tf_op jit(solution)/shard_map/all_gather | solution.py:267
  55.6 13.9 %collective-permute-start = (s16[1040,128]{1,0:T(8,128)(2,1)}, s16[1040,128]{1,0:T(8,128)(2,1)S(1)}, u32[]{:S(2)}, u32[]{:S(2)}) collective-permute-start(s16[1040,128]{1,0:T(8,128)(2,1)} %get-tuple-element.39), channel_id=1, source_target_pairs={{0,1},{1,2},{2,3},{3,0},{4,5},{5,6},{6,7},{7,4},{8,9},{9,10},{10,1... | collective-permute-start | bytes 798728 | tf_op jit(solution)/shard_map/ppermute | solution.py:246
  58.0 15.0 %collective-permute-start.1 = (s16[1040,128]{1,0:T(8,128)(2,1)}, s16[1040,128]{1,0:T(8,128)(2,1)S(1)}, u32[]{:S(2)}, u32[]{:S(2)}) collective-permute-start(s16[1040,128]{1,0:T(8,128)(2,1)} %get-tuple-element.40), channel_id=1, source_target_pairs={{0,2},{1,3},{2,0},{3,1},{4,6},{5,7},{6,4},{7,5},{8,10},{9,11},{10,... | collective-permute-start | bytes 798728 | tf_op jit(solution)/shard_map/ppermute | solution.py:246
  59.8 13.2 %collective-permute-start.2 = (s16[1040,128]{1,0:T(8,128)(2,1)}, s16[1040,128]{1,0:T(8,128)(2,1)S(1)}, u32[]{:S(2)}, u32[]{:S(2)}) collective-permute-start(s16[1040,128]{1,0:T(8,128)(2,1)} %get-tuple-element.41), channel_id=1, source_target_pairs={{0,3},{1,0},{2,1},{3,2},{4,7},{5,4},{6,5},{7,6},{8,11},{9,8},{10,9... | collective-permute-start | bytes 798728 | tf_op jit(solution)/shard_map/ppermute | solution.py:246
  68.7 12.9 %collective-permute-start.11 = (s16[1040,128]{1,0:T(8,128)(2,1)}, s16[1040,128]{1,0:T(8,128)(2,1)S(1)}, u32[]{:S(2)}, u32[]{:S(2)}) collective-permute-start(s16[1040,128]{1,0:T(8,128)(2,1)} %get-tuple-element.51), channel_id=1, source_target_pairs={{0,1},{1,2},{2,3},{3,0},{4,5},{5,6},{6,7},{7,4},{8,9},{9,10},{10,1... | collective-permute-start | bytes 798728 | tf_op jit(solution)/shard_map/ppermute | solution.py:250
  69.2 15.0 %collective-permute-start.12 = (s16[1040,128]{1,0:T(8,128)(2,1)}, s16[1040,128]{1,0:T(8,128)(2,1)S(1)}, u32[]{:S(2)}, u32[]{:S(2)}) collective-permute-start(s16[1040,128]{1,0:T(8,128)(2,1)} %get-tuple-element.52), channel_id=1, source_target_pairs={{0,2},{1,3},{2,0},{3,1},{4,6},{5,7},{6,4},{7,5},{8,10},{9,11},{10,... | collective-permute-start | bytes 798728 | tf_op jit(solution)/shard_map/ppermute | solution.py:250
  69.5 14.8 %collective-permute-start.13 = (s16[1040,128]{1,0:T(8,128)(2,1)}, s16[1040,128]{1,0:T(8,128)(2,1)S(1)}, u32[]{:S(2)}, u32[]{:S(2)}) collective-permute-start(s16[1040,128]{1,0:T(8,128)(2,1)} %get-tuple-element.53), channel_id=1, source_target_pairs={{0,3},{1,0},{2,1},{3,2},{4,7},{5,4},{6,5},{7,6},{8,11},{9,8},{10,9... | collective-permute-start | bytes 798728 | tf_op jit(solution)/shard_map/ppermute | solution.py:250
  76.3 15.5 %collective-permute-start.10 = (s16[1040,128]{1,0:T(8,128)(2,1)}, s16[1040,128]{1,0:T(8,128)(2,1)S(1)}, u32[]{:S(2)}, u32[]{:S(2)}) collective-permute-start(s16[1040,128]{1,0:T(8,128)(2,1)} %middle.4.refs_0_), channel_id=1, source_target_pairs={{0,4},{1,5},{2,6},{3,7},{4,0},{5,1},{6,2},{7,3},{8,12},{9,13},{10,... | collective-permute-start | bytes 798728 | tf_op jit(solution)/shard_map/ppermute | solution.py:249
  95.1 77.7 %all-gather.13.cloned.1.call-start = ((), (), s32[]{:S(2)}) async-start(), calls=%async_computation.2 | async-start | bytes 4456448 | tf_op jit(solution)/shard_map/all_gather | solution.py:267
  101.7 14.0 %collective-permute-start.3 = (s16[1040,128]{1,0:T(8,128)(2,1)}, s16[1040,128]{1,0:T(8,128)(2,1)S(1)}, u32[]{:S(2)}, u32[]{:S(2)}) collective-permute-start(s16[1040,128]{1,0:T(8,128)(2,1)} %get-tuple-element.44), channel_id=1, source_target_pairs={{0,1},{1,2},{2,3},{3,0},{4,5},{5,6},{6,7},{7,4},{8,9},{9,10},{10,1... | collective-permute-start | bytes 798728 | tf_op jit(solution)/shard_map/ppermute | solution.py:246
  103.8 15.1 %collective-permute-start.4 = (s16[1040,128]{1,0:T(8,128)(2,1)}, s16[1040,128]{1,0:T(8,128)(2,1)S(1)}, u32[]{:S(2)}, u32[]{:S(2)}) collective-permute-start(s16[1040,128]{1,0:T(8,128)(2,1)} %get-tuple-element.45), channel_id=1, source_target_pairs={{0,2},{1,3},{2,0},{3,1},{4,6},{5,7},{6,4},{7,5},{8,10},{9,11},{10,... | collective-permute-start | bytes 798728 | tf_op jit(solution)/shard_map/ppermute | solution.py:246
  105.8 13.1 %collective-permute-start.5 = (s16[1040,128]{1,0:T(8,128)(2,1)}, s16[1040,128]{1,0:T(8,128)(2,1)S(1)}, u32[]{:S(2)}, u32[]{:S(2)}) collective-permute-start(s16[1040,128]{1,0:T(8,128)(2,1)} %get-tuple-element.46), channel_id=1, source_target_pairs={{0,3},{1,0},{2,1},{3,2},{4,7},{5,4},{6,5},{7,6},{8,11},{9,8},{10,9... | collective-permute-start | bytes 798728 | tf_op jit(solution)/shard_map/ppermute | solution.py:246
  114.9 10.5 %collective-permute-start.7 = (s16[1040,128]{1,0:T(8,128)(2,1)}, s16[1040,128]{1,0:T(8,128)(2,1)S(1)}, u32[]{:S(2)}, u32[]{:S(2)}) collective-permute-start(s16[1040,128]{1,0:T(8,128)(2,1)} %get-tuple-element.47), channel_id=1, source_target_pairs={{0,1},{1,2},{2,3},{3,0},{4,5},{5,6},{6,7},{7,4},{8,9},{9,10},{10,1... | collective-permute-start | bytes 798728 | tf_op jit(solution)/shard_map/ppermute | solution.py:250
  115.3 14.3 %collective-permute-start.8 = (s16[1040,128]{1,0:T(8,128)(2,1)}, s16[1040,128]{1,0:T(8,128)(2,1)S(1)}, u32[]{:S(2)}, u32[]{:S(2)}) collective-permute-start(s16[1040,128]{1,0:T(8,128)(2,1)} %get-tuple-element.48), channel_id=1, source_target_pairs={{0,2},{1,3},{2,0},{3,1},{4,6},{5,7},{6,4},{7,5},{8,10},{9,11},{10,... | collective-permute-start | bytes 798728 | tf_op jit(solution)/shard_map/ppermute | solution.py:250
  115.7 13.9 %collective-permute-start.9 = (s16[1040,128]{1,0:T(8,128)(2,1)}, s16[1040,128]{1,0:T(8,128)(2,1)S(1)}, u32[]{:S(2)}, u32[]{:S(2)}) collective-permute-start(s16[1040,128]{1,0:T(8,128)(2,1)} %get-tuple-element.49), channel_id=1, source_target_pairs={{0,3},{1,0},{2,1},{3,2},{4,7},{5,4},{6,5},{7,6},{8,11},{9,8},{10,9... | collective-permute-start | bytes 798728 | tf_op jit(solution)/shard_map/ppermute | solution.py:250
  122.2 12.2 %collective-permute-start.6 = (s16[1040,128]{1,0:T(8,128)(2,1)}, s16[1040,128]{1,0:T(8,128)(2,1)S(1)}, u32[]{:S(2)}, u32[]{:S(2)}) collective-permute-start(s16[1040,128]{1,0:T(8,128)(2,1)} %middle.5), channel_id=1, source_target_pairs={{0,4},{1,5},{2,6},{3,7},{4,0},{5,1},{6,2},{7,3},{8,12},{9,13},{10,... | collective-permute-start | bytes 798728 | tf_op jit(solution)/shard_map/ppermute | solution.py:249
  144.2 15.6 %collective-permute-start.14 = (s16[1040,128]{1,0:T(8,128)(2,1)}, s16[1040,128]{1,0:T(8,128)(2,1)S(1)}, u32[]{:S(2)}, u32[]{:S(2)}) collective-permute-start(s16[1040,128]{1,0:T(8,128)(2,1)} %get-tuple-element.55), channel_id=1, source_target_pairs={{0,1},{1,2},{2,3},{3,0},{4,5},{5,6},{6,7},{7,4},{8,9},{9,10},{10,1... | collective-permute-start | bytes 798728 | tf_op jit(solution)/shard_map/ppermute | solution.py:246
  147.6 14.0 %collective-permute-start.15 = (s16[1040,128]{1,0:T(8,128)(2,1)}, s16[1040,128]{1,0:T(8,128)(2,1)S(1)}, u32[]{:S(2)}, u32[]{:S(2)}) collective-permute-start(s16[1040,128]{1,0:T(8,128)(2,1)} %get-tuple-element.56), channel_id=1, source_target_pairs={{0,2},{1,3},{2,0},{3,1},{4,6},{5,7},{6,4},{7,5},{8,10},{9,11},{10,... | collective-permute-start | bytes 798728 | tf_op jit(solution)/shard_map/ppermute | solution.py:246
  148.4 13.2 %collective-permute-start.16 = (s16[1040,128]{1,0:T(8,128)(2,1)}, s16[1040,128]{1,0:T(8,128)(2,1)S(1)}, u32[]{:S(2)}, u32[]{:S(2)}) collective-permute-start(s16[1040,128]{1,0:T(8,128)(2,1)} %get-tuple-element.57), channel_id=1, source_target_pairs={{0,3},{1,0},{2,1},{3,2},{4,7},{5,4},{6,5},{7,6},{8,11},{9,8},{10,9... | collective-permute-start | bytes 798728 | tf_op jit(solution)/shard_map/ppermute | solution.py:246
  157.0 15.7 %collective-permute-start.17 = (s16[1040,128]{1,0:T(8,128)(2,1)}, s16[1040,128]{1,0:T(8,128)(2,1)S(1)}, u32[]{:S(2)}, u32[]{:S(2)}) collective-permute-start(s16[1040,128]{1,0:T(8,128)(2,1)} %get-tuple-element.59), channel_id=1, source_target_pairs={{0,1},{1,2},{2,3},{3,0},{4,5},{5,6},{6,7},{7,4},{8,9},{9,10},{10,1... | collective-permute-start | bytes 798728 | tf_op jit(solution)/shard_map/ppermute | solution.py:250
  158.8 13.9 %collective-permute-start.18 = (s16[1040,128]{1,0:T(8,128)(2,1)}, s16[1040,128]{1,0:T(8,128)(2,1)S(1)}, u32[]{:S(2)}, u32[]{:S(2)}) collective-permute-start(s16[1040,128]{1,0:T(8,128)(2,1)} %get-tuple-element.60), channel_id=1, source_target_pairs={{0,2},{1,3},{2,0},{3,1},{4,6},{5,7},{6,4},{7,5},{8,10},{9,11},{10,... | collective-permute-start | bytes 798728 | tf_op jit(solution)/shard_map/ppermute | solution.py:250
  159.8 12.9 %collective-permute-start.19 = (s16[1040,128]{1,0:T(8,128)(2,1)}, s16[1040,128]{1,0:T(8,128)(2,1)S(1)}, u32[]{:S(2)}, u32[]{:S(2)}) collective-permute-start(s16[1040,128]{1,0:T(8,128)(2,1)} %get-tuple-element.61), channel_id=1, source_target_pairs={{0,3},{1,0},{2,1},{3,2},{4,7},{5,4},{6,5},{7,6},{8,11},{9,8},{10,9... | collective-permute-start | bytes 798728 | tf_op jit(solution)/shard_map/ppermute | solution.py:250
  180.2 15.5 %collective-permute-start.20 = (s16[1040,128]{1,0:T(8,128)(2,1)}, s16[1040,128]{1,0:T(8,128)(2,1)S(1)}, u32[]{:S(2)}, u32[]{:S(2)}) collective-permute-start(s16[1040,128]{1,0:T(8,128)(2,1)} %get-tuple-element.63), channel_id=1, source_target_pairs={{0,1},{1,2},{2,3},{3,0},{4,5},{5,6},{6,7},{7,4},{8,9},{9,10},{10,1... | collective-permute-start | bytes 798728 | tf_op jit(solution)/shard_map/ppermute | solution.py:246
  183.5 16.9 %collective-permute-start.21 = (s16[1040,128]{1,0:T(8,128)(2,1)}, s16[1040,128]{1,0:T(8,128)(2,1)S(1)}, u32[]{:S(2)}, u32[]{:S(2)}) collective-permute-start(s16[1040,128]{1,0:T(8,128)(2,1)} %get-tuple-element.64), channel_id=1, source_target_pairs={{0,2},{1,3},{2,0},{3,1},{4,6},{5,7},{6,4},{7,5},{8,10},{9,11},{10,... | collective-permute-start | bytes 798728 | tf_op jit(solution)/shard_map/ppermute | solution.py:246
  184.4 18.2 %collective-permute-start.22 = (s16[1040,128]{1,0:T(8,128)(2,1)}, s16[1040,128]{1,0:T(8,128)(2,1)S(1)}, u32[]{:S(2)}, u32[]{:S(2)}) collective-permute-start(s16[1040,128]{1,0:T(8,128)(2,1)} %get-tuple-element.65), channel_id=1, source_target_pairs={{0,3},{1,0},{2,1},{3,2},{4,7},{5,4},{6,5},{7,6},{8,11},{9,8},{10,9... | collective-permute-start | bytes 798728 | tf_op jit(solution)/shard_map/ppermute | solution.py:246
  192.9 16.3 %collective-permute-start.24 = (s16[1040,128]{1,0:T(8,128)(2,1)}, s16[1040,128]{1,0:T(8,128)(2,1)S(1)}, u32[]{:S(2)}, u32[]{:S(2)}) collective-permute-start(s16[1040,128]{1,0:T(8,128)(2,1)} %get-tuple-element.66), channel_id=1, source_target_pairs={{0,1},{1,2},{2,3},{3,0},{4,5},{5,6},{6,7},{7,4},{8,9},{9,10},{10,1... | collective-permute-start | bytes 798728 | tf_op jit(solution)/shard_map/ppermute | solution.py:250
  194.7 14.4 %collective-permute-start.25 = (s16[1040,128]{1,0:T(8,128)(2,1)}, s16[1040,128]{1,0:T(8,128)(2,1)S(1)}, u32[]{:S(2)}, u32[]{:S(2)}) collective-permute-start(s16[1040,128]{1,0:T(8,128)(2,1)} %get-tuple-element.67), channel_id=1, source_target_pairs={{0,2},{1,3},{2,0},{3,1},{4,6},{5,7},{6,4},{7,5},{8,10},{9,11},{10,... | collective-permute-start | bytes 798728 | tf_op jit(solution)/shard_map/ppermute | solution.py:250
  195.7 10.2 %collective-permute-start.27 = (s16[1040,128]{1,0:T(8,128)(2,1)S(1)}, s16[1040,128]{1,0:T(8,128)(2,1)S(1)}, u32[]{:S(2)}, u32[]{:S(2)}) collective-permute-start(s16[1040,128]{1,0:T(8,128)(2,1)S(1)} %copy-done.11), channel_id=1, source_target_pairs={{0,4},{1,5},{2,6},{3,7},{4,0},{5,1},{6,2},{7,3},{8,12},{9,13},{10,... | collective-permute-start | bytes 798728 | tf_op jit(solution)/shard_map/ppermute | solution.py:249
  200.4 8.8 %collective-permute-start.26 = (s16[1040,128]{1,0:T(8,128)(2,1)}, s16[1040,128]{1,0:T(8,128)(2,1)S(1)}, u32[]{:S(2)}, u32[]{:S(2)}) collective-permute-start(s16[1040,128]{1,0:T(8,128)(2,1)} %get-tuple-element.68), channel_id=1, source_target_pairs={{0,3},{1,0},{2,1},{3,2},{4,7},{5,4},{6,5},{7,6},{8,11},{9,8},{10,9... | collective-permute-start | bytes 798728 | tf_op jit(solution)/shard_map/ppermute | solution.py:250
  205.8 8.1 %collective-permute-start.23 = (s16[1040,128]{1,0:T(8,128)(2,1)}, s16[1040,128]{1,0:T(8,128)(2,1)S(1)}, u32[]{:S(2)}, u32[]{:S(2)}) collective-permute-start(s16[1040,128]{1,0:T(8,128)(2,1)} %middle.7), channel_id=1, source_target_pairs={{0,4},{1,5},{2,6},{3,7},{4,0},{5,1},{6,2},{7,3},{8,12},{9,13},{10,... | collective-permute-start | bytes 798728 | tf_op jit(solution)/shard_map/ppermute | solution.py:249
  (30 other events, 116.8 us)
Sparse Core Ops, SparseCore 0:
  9.1 39.9 all-gather.10
  50.7 39.1 all-gather.8
  95.2 35.3 all-gather.14
  137.8 34.9 all-gather.12

commit v4 on v3

--- a/solution.py
+++ b/solution.py
@@ -133,7 +133,7 @@
 
 
 def rows_at_once(height):
-    return next(r for r in (64, 48, 32, 16) if height % r == 0)
+    return next(r for r in (256, 64, 48, 32, 16) if height % r == 0)
 
 
 def scales_of(piece, height):

time: 226 us -> 226 us (level)
  starting transfers between devices: 54.5 us -> 38.2 us
  waiting for transfers between devices: 69.9 us -> 79.7 us
  Pallas kernels: 72.8 us -> 79.8 us
    ppermute x4, starting transfers between devices: 12.6 us -> 2.95 us  [exchange(): pieces = [near[0], lax.ppermute(sent, 'col', to_col(1, 0))]]
    ppermute x12, waiting for transfers between devices: 6.92 us -> 16 us  [exchange(): lax.ppermute(near[d], 'col', to_col(0, d))]
    pallas_call x8, Pallas kernels: 52.7 us -> 61.3 us  [product(): pl.pallas_call(functools.partial(product_kernel, layer), out_shape=(piece...]
    ppermute x12, starting transfers between devices: 25.2 us -> 19 us  [exchange(): lax.ppermute(far[d], 'col', to_col(0, d))]
    ppermute x12, waiting for transfers between devices: 1.4 us -> 4.38 us  [exchange(): lax.ppermute(far[d], 'col', to_col(0, d))]
  transfers between devices with their start and end apart: 32 -> 32, of which waited for: 9 -> 16; matrix products, arithmetic and copies ran while one was open for 2% -> 2% of each run, Pallas kernels for 28% -> 31%
where the time goes in v4:
time: 226 us; the launch traced here: 224 us
  Pallas kernels  79.8 us (35%)
  waiting for transfers between devices  79.7 us (35%)
  starting transfers between devices  38.2 us (17%)
  between operations  13.4 us (6%)
  local copies, waits for them, and re-layouts  10.3 us (5%)
  other arithmetic  2.49 us (1%)
    pallas_call x8, Pallas kernels, product(): pl.pallas_call(functools.partial(product_kernel, layer), out_shape=(piece...  61.3 us
    all_gather x4, waiting for transfers between devices, on_device(): gathered = lax.all_gather(current[c], 'row', axis=0, tiled=False)  42.7 us
    ppermute x12, starting transfers between devices, exchange(): lax.ppermute(far[d], 'col', to_col(0, d))  19 us
    ppermute x12, starting transfers between devices, exchange(): lax.ppermute(near[d], 'col', to_col(0, d))  16.1 us
    ppermute x12, waiting for transfers between devices, exchange(): lax.ppermute(near[d], 'col', to_col(0, d))  16 us
    ppermute x4, waiting for transfers between devices, exchange(): pieces = [near[0], lax.ppermute(sent, 'col', to_col(1, 0))]  15.9 us
    pallas_call x4, Pallas kernels, combine(): pl.pallas_call(functools.partial(combine_kernel, n_pieces, first), out_sh...  9.48 us
    pallas_call x4, Pallas kernels, middle(): pl.pallas_call(middle_kernel, out_shape=jax.ShapeDtypeStruct(pieces[0].sh...  9.05 us
  transfers between devices with their start and end apart: 32, of which 16 were waited for; matrix products, arithmetic and copies ran while one was open for 2% of the time, Pallas kernels for 31%

profile of v4, /device:TPU:0, one launch (start us, length us, event | category | flops | bytes accessed | tf_op | source)
XLA Modules:
  0.0 224.0 jit_solution(16584830351354665615)
XLA Ops:
  13.0 36.0 %all-gather.11.cloned.1.call-done = bf16[4096,1,512]{2,0,1:T(8,128)(2,1)} async-done(((bf16[256,1,512]{2,0,1:T(8,128)(2,1)}), bf16[4096,1,512]{2,0,1:T(8,128)(2,1)}) %all-gather.11.cloned.1.call-update) | async-done | bytes 4194320 | tf_op jit(solution)/shard_map/all_gather | solution.py:267
  49.0 6.5 %product.9 = (s16[1040,128]{1,0:T(8,128)(2,1)}, s16[1040,128]{1,0:T(8,128)(2,1)}, s16[1040,128]{1,0:T(8,128)(2,1)}, s16[1040,128]{1,0:T(8,128)(2,1)}) custom-call(s32[320]{0:T(512)} %get-tuple-element.70.codes, s32[1]{0:T(128)} %bitcast.4.count, bf16[16,256,512]{2,1,0:T(8,128)(2,1)} %bitcast.25, bf16[2,1,1,320,128,128]{5,4,3,2,1,0:T(8,128)(2,1)} %values.15), custom_call_target="tpu_custom_call" | custom-call | flops 10737418240 | bytes 10485760 | tf_op jit(solution)/shard_map/product/pallas_call | solution.py:113
  55.6 3.1 %collective-permute-start = (s16[1040,128]{1,0:T(8,128)(2,1)}, s16[1040,128]{1,0:T(8,128)(2,1)S(1)}, u32[]{:S(2)}, u32[]{:S(2)}) collective-permute-start(s16[1040,128]{1,0:T(8,128)(2,1)} %get-tuple-element.39), channel_id=1, source_target_pairs={{0,1},{1,2},{2,3},{3,0},{4,5},{5,6},{6,7},{7,4},{8,9},{9,10},{10,1... | collective-permute-start | bytes 798728 | tf_op jit(solution)/shard_map/ppermute | solution.py:246
  61.4 6.7 %product.10 = (s16[1040,128]{1,0:T(8,128)(2,1)}, s16[1040,128]{1,0:T(8,128)(2,1)}, s16[1040,128]{1,0:T(8,128)(2,1)}, s16[1040,128]{1,0:T(8,128)(2,1)}) custom-call(s32[320]{0:T(512)} %get-tuple-element.71.codes, s32[1]{0:T(128)} %bitcast.2.count, bf16[16,256,512]{2,1,0:T(8,128)(2,1)} %bitcast.26, bf16[2,1,1,320,128,128]{5,4,3,2,1,0:T(8,128)(2,1)} %values.15), custom_call_target="tpu_custom_call" | custom-call | flops 10737418240 | bytes 10485760 | tf_op jit(solution)/shard_map/product/pallas_call | solution.py:113
  68.1 2.8 %collective-permute-start.11 = (s16[1040,128]{1,0:T(8,128)(2,1)}, s16[1040,128]{1,0:T(8,128)(2,1)S(1)}, u32[]{:S(2)}, u32[]{:S(2)}) collective-permute-start(s16[1040,128]{1,0:T(8,128)(2,1)} %get-tuple-element.51), channel_id=1, source_target_pairs={{0,1},{1,2},{2,3},{3,0},{4,5},{5,6},{6,7},{7,4},{8,9},{9,10},{10,1... | collective-permute-start | bytes 798728 | tf_op jit(solution)/shard_map/ppermute | solution.py:250
  74.6 2.3 %middle.4.refs_0_ = s16[1040,128]{1,0:T(8,128)(2,1)} custom-call(s16[1040,128]{1,0:T(8,128)(2,1)} %get-tuple-element.38.a, s16[1040,128]{1,0:T(8,128)(2,1)} %copy-done.16, s16[1040,128]{1,0:T(8,128)(2,1)} %copy-done.20, s16[1040,128]{1,0:T(8,128)(2,1)} %copy-done.23), custom_call_target="tpu_custom_call" | custom-call | flops 2129920 | bytes 1064960 | tf_op jit(solution)/shard_map/middle/pallas_call | solution.py:185
  78.8 5.8 %collective-permute-done.12.refs_3_ = s16[1040,128]{1,0:T(8,128)(2,1)S(1)} collective-permute-done((s16[1040,128]{1,0:T(8,128)(2,1)}, s16[1040,128]{1,0:T(8,128)(2,1)S(1)}, u32[]{:S(2)}, u32[]{:S(2)}) %collective-permute-start.12) | collective-permute-done | bytes 266272 | tf_op jit(solution)/shard_map/ppermute | solution.py:250
  84.6 7.1 %collective-permute-done.10.refs_1_ = s16[1040,128]{1,0:T(8,128)(2,1)S(1)} collective-permute-done((s16[1040,128]{1,0:T(8,128)(2,1)}, s16[1040,128]{1,0:T(8,128)(2,1)S(1)}, u32[]{:S(2)}, u32[]{:S(2)}) %collective-permute-start.10) | collective-permute-done | bytes 266272 | tf_op jit(solution)/shard_map/ppermute | solution.py:249
  92.4 2.4 %combine.5 = bf16[256,512]{1,0:T(8,128)(2,1)} custom-call(s16[1040,128]{1,0:T(8,128)(2,1)} %get-tuple-element.42.refs_1_.refs_0_, s16[1040,128]{1,0:T(8,128)(2,1)} %copy-done.6, s16[1040,128]{1,0:T(8,128)(2,1)} %copy-done, s16[1040,128]{1,0:T(8,128)(2,1)} %copy-done.2, s16[1040,128]{1,0:T(8,128)(2,1)} %copy-done.4, f32[1,512]{1,0:T(1,128)} %get-tuple-element.78.refs_5_), custom_call_target="tpu_custom_call" | custom-call | flops 2129920 | bytes 1331200 | tf_op jit(solution)/shard_map/combine/pallas_call | solution.py:227
  94.9 6.6 %product.11 = (s16[1040,128]{1,0:T(8,128)(2,1)}, s16[1040,128]{1,0:T(8,128)(2,1)}, s16[1040,128]{1,0:T(8,128)(2,1)}, s16[1040,128]{1,0:T(8,128)(2,1)}) custom-call(s32[320]{0:T(512)} %get-tuple-element.70.codes, s32[1]{0:T(128)} %bitcast.4.count, bf16[16,256,512]{2,1,0:T(8,128)(2,1)} %bitcast.19, bf16[2,1,1,320,128,128]{5,4,3,2,1,0:T(8,128)(2,1)} %values.15, ...), custom_call_target="tpu_custom_call" | custom-call | flops 10737418240 | bytes 10485760 | tf_op jit(solution)/shard_map/product/pallas_call | solution.py:113
  101.5 3.1 %collective-permute-start.3 = (s16[1040,128]{1,0:T(8,128)(2,1)}, s16[1040,128]{1,0:T(8,128)(2,1)S(1)}, u32[]{:S(2)}, u32[]{:S(2)}) collective-permute-start(s16[1040,128]{1,0:T(8,128)(2,1)} %get-tuple-element.44), channel_id=1, source_target_pairs={{0,1},{1,2},{2,3},{3,0},{4,5},{5,6},{6,7},{7,4},{8,9},{9,10},{10,1... | collective-permute-start | bytes 798728 | tf_op jit(solution)/shard_map/ppermute | solution.py:246
  107.3 6.6 %product.8 = (s16[1040,128]{1,0:T(8,128)(2,1)}, s16[1040,128]{1,0:T(8,128)(2,1)}, s16[1040,128]{1,0:T(8,128)(2,1)}, s16[1040,128]{1,0:T(8,128)(2,1)}) custom-call(s32[320]{0:T(512)} %get-tuple-element.71.codes, s32[1]{0:T(128)} %bitcast.2.count, bf16[16,256,512]{2,1,0:T(8,128)(2,1)} %bitcast.20, bf16[2,1,1,320,128,128]{5,4,3,2,1,0:T(8,128)(2,1)} %values.15), custom_call_target="tpu_custom_call" | custom-call | flops 10737418240 | bytes 10485760 | tf_op jit(solution)/shard_map/product/pallas_call | solution.py:113
  114.0 2.8 %collective-permute-start.7 = (s16[1040,128]{1,0:T(8,128)(2,1)}, s16[1040,128]{1,0:T(8,128)(2,1)S(1)}, u32[]{:S(2)}, u32[]{:S(2)}) collective-permute-start(s16[1040,128]{1,0:T(8,128)(2,1)} %get-tuple-element.47), channel_id=1, source_target_pairs={{0,1},{1,2},{2,3},{3,0},{4,5},{5,6},{6,7},{7,4},{8,9},{9,10},{10,1... | collective-permute-start | bytes 798728 | tf_op jit(solution)/shard_map/ppermute | solution.py:250
  120.4 2.3 %middle.5 = s16[1040,128]{1,0:T(8,128)(2,1)} custom-call(s16[1040,128]{1,0:T(8,128)(2,1)} %get-tuple-element.43.a, s16[1040,128]{1,0:T(8,128)(2,1)} %copy-done.14, s16[1040,128]{1,0:T(8,128)(2,1)} %copy-done.18, s16[1040,128]{1,0:T(8,128)(2,1)} %copy-done.21), custom_call_target="tpu_custom_call" | custom-call | flops 2129920 | bytes 1064960 | tf_op jit(solution)/shard_map/middle/pallas_call | solution.py:185
  122.6 2.3 %collective-permute-done.7.refs_2_ = s16[1040,128]{1,0:T(8,128)(2,1)S(1)} collective-permute-done((s16[1040,128]{1,0:T(8,128)(2,1)}, s16[1040,128]{1,0:T(8,128)(2,1)S(1)}, u32[]{:S(2)}, u32[]{:S(2)}) %collective-permute-start.7) | collective-permute-done | bytes 266272 | tf_op jit(solution)/shard_map/ppermute | solution.py:250
  124.9 5.2 %collective-permute-done.8.refs_3_ = s16[1040,128]{1,0:T(8,128)(2,1)S(1)} collective-permute-done((s16[1040,128]{1,0:T(8,128)(2,1)}, s16[1040,128]{1,0:T(8,128)(2,1)S(1)}, u32[]{:S(2)}, u32[]{:S(2)}) %collective-permute-start.8) | collective-permute-done | bytes 266272 | tf_op jit(solution)/shard_map/ppermute | solution.py:250
  131.0 3.9 %collective-permute-done.6.refs_1_ = s16[1040,128]{1,0:T(8,128)(2,1)S(1)} collective-permute-done((s16[1040,128]{1,0:T(8,128)(2,1)}, s16[1040,128]{1,0:T(8,128)(2,1)S(1)}, u32[]{:S(2)}, u32[]{:S(2)}) %collective-permute-start.6) | collective-permute-done | bytes 266272 | tf_op jit(solution)/shard_map/ppermute | solution.py:249
  135.6 2.4 %combine.4 = bf16[256,512]{1,0:T(8,128)(2,1)} custom-call(s16[1040,128]{1,0:T(8,128)(2,1)} %get-tuple-element.37.refs_0_, s16[1040,128]{1,0:T(8,128)(2,1)} %copy-done.7, s16[1040,128]{1,0:T(8,128)(2,1)} %copy-done.1, s16[1040,128]{1,0:T(8,128)(2,1)} %copy-done.3, s16[1040,128]{1,0:T(8,128)(2,1)} %copy-done.5, f32[1,512]{1,0:T(1,128)} %get-tuple-element.78.refs_5_), custom_call_target="tpu_custom_call" | custom-call | flops 2129920 | bytes 1331200 | tf_op jit(solution)/shard_map/combine/pallas_call | solution.py:227
  138.1 8.1 %product.13 = (s16[1040,128]{1,0:T(8,128)(2,1)}, s16[1040,128]{1,0:T(8,128)(2,1)}, s16[1040,128]{1,0:T(8,128)(2,1)}, s16[1040,128]{1,0:T(8,128)(2,1)}) custom-call(s32[320]{0:T(512)} %get-tuple-element.69.codes, s32[1]{0:T(128)} %bitcast.8.count, bf16[16,256,512]{2,1,0:T(8,128)(2,1)} %bitcast.21, bf16[2,1,1,320,128,128]{5,4,3,2,1,0:T(8,128)(2,1)} %values.15), custom_call_target="tpu_custom_call" | custom-call | flops 10737418240 | bytes 10485760 | tf_op jit(solution)/shard_map/product/pallas_call | solution.py:113
  146.3 2.5 %collective-permute-start.15 = (s16[1040,128]{1,0:T(8,128)(2,1)}, s16[1040,128]{1,0:T(8,128)(2,1)S(1)}, u32[]{:S(2)}, u32[]{:S(2)}) collective-permute-start(s16[1040,128]{1,0:T(8,128)(2,1)} %get-tuple-element.56), channel_id=1, source_target_pairs={{0,2},{1,3},{2,0},{3,1},{4,6},{5,7},{6,4},{7,5},{8,10},{9,11},{10,... | collective-permute-start | bytes 798728 | tf_op jit(solution)/shard_map/ppermute | solution.py:246
  150.2 9.3 %product.14 = (s16[1040,128]{1,0:T(8,128)(2,1)}, s16[1040,128]{1,0:T(8,128)(2,1)}, s16[1040,128]{1,0:T(8,128)(2,1)}, s16[1040,128]{1,0:T(8,128)(2,1)}) custom-call(s32[320]{0:T(512)} %get-tuple-element.72.codes, s32[1]{0:T(128)} %bitcast.1.count, bf16[16,256,512]{2,1,0:T(8,128)(2,1)} %bitcast.22, bf16[2,1,1,320,128,128]{5,4,3,2,1,0:T(8,128)(2,1)} %values.15), custom_call_target="tpu_custom_call" | custom-call | flops 10737418240 | bytes 10485760 | tf_op jit(solution)/shard_map/product/pallas_call | solution.py:113
  164.2 2.3 %middle.6.refs_0_ = s16[1040,128]{1,0:T(8,128)(2,1)} custom-call(s16[1040,128]{1,0:T(8,128)(2,1)} %get-tuple-element.54.a, s16[1040,128]{1,0:T(8,128)(2,1)} %copy-done.15, s16[1040,128]{1,0:T(8,128)(2,1)} %copy-done.19, s16[1040,128]{1,0:T(8,128)(2,1)} %copy-done.22), custom_call_target="tpu_custom_call" | custom-call | flops 2129920 | bytes 1064960 | tf_op jit(solution)/shard_map/middle/pallas_call | solution.py:185
  166.5 6.7 %all-gather.13.cloned.1.call-done = bf16[4096,512]{1,0:T(8,128)(2,1)} async-done(((bf16[256,512]{1,0:T(8,128)(2,1)}), bf16[4096,512]{1,0:T(8,128)(2,1)}) %all-gather.13.cloned.1.call-update) | async-done | bytes 4194320 | tf_op jit(solution)/shard_map/all_gather | solution.py:267
  175.1 8.1 %product.15 = (s16[1040,128]{1,0:T(8,128)(2,1)}, s16[1040,128]{1,0:T(8,128)(2,1)}, s16[1040,128]{1,0:T(8,128)(2,1)}, s16[1040,128]{1,0:T(8,128)(2,1)}) custom-call(s32[320]{0:T(512)} %get-tuple-element.69.codes, s32[1]{0:T(128)} %bitcast.8.count, bf16[16,256,512]{2,1,0:T(8,128)(2,1)} %bitcast.23, bf16[2,1,1,320,128,128]{5,4,3,2,1,0:T(8,128)(2,1)} %values.15, ...), custom_call_target="tpu_custom_call" | custom-call | flops 10737418240 | bytes 10485760 | tf_op jit(solution)/shard_map/product/pallas_call | solution.py:113
  183.3 2.4 %collective-permute-start.21 = (s16[1040,128]{1,0:T(8,128)(2,1)}, s16[1040,128]{1,0:T(8,128)(2,1)S(1)}, u32[]{:S(2)}, u32[]{:S(2)}) collective-permute-start(s16[1040,128]{1,0:T(8,128)(2,1)} %get-tuple-element.64), channel_id=1, source_target_pairs={{0,2},{1,3},{2,0},{3,1},{4,6},{5,7},{6,4},{7,5},{8,10},{9,11},{10,... | collective-permute-start | bytes 798728 | tf_op jit(solution)/shard_map/ppermute | solution.py:246
  186.5 9.3 %product.12 = (s16[1040,128]{1,0:T(8,128)(2,1)}, s16[1040,128]{1,0:T(8,128)(2,1)}, s16[1040,128]{1,0:T(8,128)(2,1)}, s16[1040,128]{1,0:T(8,128)(2,1)}) custom-call(s32[320]{0:T(512)} %get-tuple-element.72.codes, s32[1]{0:T(128)} %bitcast.1.count, bf16[16,256,512]{2,1,0:T(8,128)(2,1)} %bitcast.24, bf16[2,1,1,320,128,128]{5,4,3,2,1,0:T(8,128)(2,1)} %values.15), custom_call_target="tpu_custom_call" | custom-call | flops 10737418240 | bytes 10485760 | tf_op jit(solution)/shard_map/product/pallas_call | solution.py:113
  196.2 2.2 collective-permute-done.20.b
  199.3 2.7 %collective-permute-start.26 = (s16[1040,128]{1,0:T(8,128)(2,1)}, s16[1040,128]{1,0:T(8,128)(2,1)S(1)}, u32[]{:S(2)}, u32[]{:S(2)}) collective-permute-start(s16[1040,128]{1,0:T(8,128)(2,1)} %get-tuple-element.68), channel_id=1, source_target_pairs={{0,3},{1,0},{2,1},{3,2},{4,7},{5,4},{6,5},{7,6},{8,11},{9,8},{10,9... | collective-permute-start | bytes 798728 | tf_op jit(solution)/shard_map/ppermute | solution.py:250
  202.8 2.3 %middle.7 = s16[1040,128]{1,0:T(8,128)(2,1)} custom-call(s16[1040,128]{1,0:T(8,128)(2,1)} %get-tuple-element.62.a, s16[1040,128]{1,0:T(8,128)(2,1)} %copy-done.12, s16[1040,128]{1,0:T(8,128)(2,1)} %copy-done.13, s16[1040,128]{1,0:T(8,128)(2,1)} %copy-done.17), custom_call_target="tpu_custom_call" | custom-call | flops 2129920 | bytes 1064960 | tf_op jit(solution)/shard_map/middle/pallas_call | solution.py:185
  208.2 2.4 %combine.6.refs_6_ = bf16[512,512]{1,0:T(8,128)(2,1)} custom-call(s16[1040,128]{1,0:T(8,128)(2,1)} %get-tuple-element.58.refs_1_.refs_0_, s16[1040,128]{1,0:T(8,128)(2,1)} %copy-done.24, s16[1040,128]{1,0:T(8,128)(2,1)} %copy-done.8, s16[1040,128]{1,0:T(8,128)(2,1)} %copy-done.9, s16[1040,128]{1,0:T(8,128)(2,1)} %copy-done.10, ...), custom_call_target="tpu_custom_call" | custom-call | flops 2129920 | bytes 1331200 | tf_op jit(solution)/shard_map/combine/pallas_call | solution.py:227
  211.2 3.1 %collective-permute-done.23.refs_1_ = s16[1040,128]{1,0:T(8,128)(2,1)S(1)} collective-permute-done((s16[1040,128]{1,0:T(8,128)(2,1)}, s16[1040,128]{1,0:T(8,128)(2,1)S(1)}, u32[]{:S(2)}, u32[]{:S(2)}) %collective-permute-start.23) | collective-permute-done | bytes 266272 | tf_op jit(solution)/shard_map/ppermute | solution.py:249
  215.1 2.4 %combine.7 = bf16[512,512]{1,0:T(8,128)(2,1)} custom-call(s16[1040,128]{1,0:T(8,128)(2,1)} %get-tuple-element.50.refs_0_, s16[1040,128]{1,0:T(8,128)(2,1)} %copy-done.28, s16[1040,128]{1,0:T(8,128)(2,1)} %copy-done.25, s16[1040,128]{1,0:T(8,128)(2,1)} %copy-done.26, s16[1040,128]{1,0:T(8,128)(2,1)} %copy-done.27, ...), custom_call_target="tpu_custom_call", output_to_operand_aliasing={{}: (6, {})} | custom-call | flops 2129920 | bytes 1331200 | tf_op jit(solution)/shard_map/combine/pallas_call | solution.py:227
  (125 shorter events, 39.1 us)
Async XLA Ops:
  6.5 42.5 %all-gather.11.cloned.1.call-start = ((), (), s32[]{:S(2)}) async-start(), calls=%async_computation.1 | async-start | bytes 4456448 | tf_op jit(solution)/shard_map/all_gather | solution.py:267
  8.4 86.5 %all-gather.9.cloned.1.call-start = ((), (), s32[]{:S(2)}) async-start(), calls=%async_computation | async-start | bytes 4456448 | tf_op jit(solution)/shard_map/all_gather | solution.py:267
  9.2 128.9 %all-gather.15.cloned.1.call-start = ((), (), s32[]{:S(2)}) async-start(), calls=%async_computation.3 | async-start | bytes 4456448 | tf_op jit(solution)/shard_map/all_gather | solution.py:267
  55.6 16.1 %collective-permute-start = (s16[1040,128]{1,0:T(8,128)(2,1)}, s16[1040,128]{1,0:T(8,128)(2,1)S(1)}, u32[]{:S(2)}, u32[]{:S(2)}) collective-permute-start(s16[1040,128]{1,0:T(8,128)(2,1)} %get-tuple-element.39), channel_id=1, source_target_pairs={{0,1},{1,2},{2,3},{3,0},{4,5},{5,6},{6,7},{7,4},{8,9},{9,10},{10,1... | collective-permute-start | bytes 798728 | tf_op jit(solution)/shard_map/ppermute | solution.py:246
  58.7 15.1 %collective-permute-start.1 = (s16[1040,128]{1,0:T(8,128)(2,1)}, s16[1040,128]{1,0:T(8,128)(2,1)S(1)}, u32[]{:S(2)}, u32[]{:S(2)}) collective-permute-start(s16[1040,128]{1,0:T(8,128)(2,1)} %get-tuple-element.40), channel_id=1, source_target_pairs={{0,2},{1,3},{2,0},{3,1},{4,6},{5,7},{6,4},{7,5},{8,10},{9,11},{10,... | collective-permute-start | bytes 798728 | tf_op jit(solution)/shard_map/ppermute | solution.py:246
  60.5 13.2 %collective-permute-start.2 = (s16[1040,128]{1,0:T(8,128)(2,1)}, s16[1040,128]{1,0:T(8,128)(2,1)S(1)}, u32[]{:S(2)}, u32[]{:S(2)}) collective-permute-start(s16[1040,128]{1,0:T(8,128)(2,1)} %get-tuple-element.41), channel_id=1, source_target_pairs={{0,3},{1,0},{2,1},{3,2},{4,7},{5,4},{6,5},{7,6},{8,11},{9,8},{10,9... | collective-permute-start | bytes 798728 | tf_op jit(solution)/shard_map/ppermute | solution.py:246
  68.1 10.7 %collective-permute-start.11 = (s16[1040,128]{1,0:T(8,128)(2,1)}, s16[1040,128]{1,0:T(8,128)(2,1)S(1)}, u32[]{:S(2)}, u32[]{:S(2)}) collective-permute-start(s16[1040,128]{1,0:T(8,128)(2,1)} %get-tuple-element.51), channel_id=1, source_target_pairs={{0,1},{1,2},{2,3},{3,0},{4,5},{5,6},{6,7},{7,4},{8,9},{9,10},{10,1... | collective-permute-start | bytes 798728 | tf_op jit(solution)/shard_map/ppermute | solution.py:250
  70.9 13.7 %collective-permute-start.12 = (s16[1040,128]{1,0:T(8,128)(2,1)}, s16[1040,128]{1,0:T(8,128)(2,1)S(1)}, u32[]{:S(2)}, u32[]{:S(2)}) collective-permute-start(s16[1040,128]{1,0:T(8,128)(2,1)} %get-tuple-element.52), channel_id=1, source_target_pairs={{0,2},{1,3},{2,0},{3,1},{4,6},{5,7},{6,4},{7,5},{8,10},{9,11},{10,... | collective-permute-start | bytes 798728 | tf_op jit(solution)/shard_map/ppermute | solution.py:250
  71.7 12.9 %collective-permute-start.13 = (s16[1040,128]{1,0:T(8,128)(2,1)}, s16[1040,128]{1,0:T(8,128)(2,1)S(1)}, u32[]{:S(2)}, u32[]{:S(2)}) collective-permute-start(s16[1040,128]{1,0:T(8,128)(2,1)} %get-tuple-element.53), channel_id=1, source_target_pairs={{0,3},{1,0},{2,1},{3,2},{4,7},{5,4},{6,5},{7,6},{8,11},{9,8},{10,9... | collective-permute-start | bytes 798728 | tf_op jit(solution)/shard_map/ppermute | solution.py:250
  76.8 14.9 %collective-permute-start.10 = (s16[1040,128]{1,0:T(8,128)(2,1)}, s16[1040,128]{1,0:T(8,128)(2,1)S(1)}, u32[]{:S(2)}, u32[]{:S(2)}) collective-permute-start(s16[1040,128]{1,0:T(8,128)(2,1)} %middle.4.refs_0_), channel_id=1, source_target_pairs={{0,4},{1,5},{2,6},{3,7},{4,0},{5,1},{6,2},{7,3},{8,12},{9,13},{10,... | collective-permute-start | bytes 798728 | tf_op jit(solution)/shard_map/ppermute | solution.py:249
  94.8 78.4 %all-gather.13.cloned.1.call-start = ((), (), s32[]{:S(2)}) async-start(), calls=%async_computation.2 | async-start | bytes 4456448 | tf_op jit(solution)/shard_map/all_gather | solution.py:267
  101.5 16.4 %collective-permute-start.3 = (s16[1040,128]{1,0:T(8,128)(2,1)}, s16[1040,128]{1,0:T(8,128)(2,1)S(1)}, u32[]{:S(2)}, u32[]{:S(2)}) collective-permute-start(s16[1040,128]{1,0:T(8,128)(2,1)} %get-tuple-element.44), channel_id=1, source_target_pairs={{0,1},{1,2},{2,3},{3,0},{4,5},{5,6},{6,7},{7,4},{8,9},{9,10},{10,1... | collective-permute-start | bytes 798728 | tf_op jit(solution)/shard_map/ppermute | solution.py:246
  104.6 15.0 %collective-permute-start.4 = (s16[1040,128]{1,0:T(8,128)(2,1)}, s16[1040,128]{1,0:T(8,128)(2,1)S(1)}, u32[]{:S(2)}, u32[]{:S(2)}) collective-permute-start(s16[1040,128]{1,0:T(8,128)(2,1)} %get-tuple-element.45), channel_id=1, source_target_pairs={{0,2},{1,3},{2,0},{3,1},{4,6},{5,7},{6,4},{7,5},{8,10},{9,11},{10,... | collective-permute-start | bytes 798728 | tf_op jit(solution)/shard_map/ppermute | solution.py:246
  106.3 13.3 %collective-permute-start.5 = (s16[1040,128]{1,0:T(8,128)(2,1)}, s16[1040,128]{1,0:T(8,128)(2,1)S(1)}, u32[]{:S(2)}, u32[]{:S(2)}) collective-permute-start(s16[1040,128]{1,0:T(8,128)(2,1)} %get-tuple-element.46), channel_id=1, source_target_pairs={{0,3},{1,0},{2,1},{3,2},{4,7},{5,4},{6,5},{7,6},{8,11},{9,8},{10,9... | collective-permute-start | bytes 798728 | tf_op jit(solution)/shard_map/ppermute | solution.py:246
  114.0 10.9 %collective-permute-start.7 = (s16[1040,128]{1,0:T(8,128)(2,1)}, s16[1040,128]{1,0:T(8,128)(2,1)S(1)}, u32[]{:S(2)}, u32[]{:S(2)}) collective-permute-start(s16[1040,128]{1,0:T(8,128)(2,1)} %get-tuple-element.47), channel_id=1, source_target_pairs={{0,1},{1,2},{2,3},{3,0},{4,5},{5,6},{6,7},{7,4},{8,9},{9,10},{10,1... | collective-permute-start | bytes 798728 | tf_op jit(solution)/shard_map/ppermute | solution.py:250
  116.8 13.4 %collective-permute-start.8 = (s16[1040,128]{1,0:T(8,128)(2,1)}, s16[1040,128]{1,0:T(8,128)(2,1)S(1)}, u32[]{:S(2)}, u32[]{:S(2)}) collective-permute-start(s16[1040,128]{1,0:T(8,128)(2,1)} %get-tuple-element.48), channel_id=1, source_target_pairs={{0,2},{1,3},{2,0},{3,1},{4,6},{5,7},{6,4},{7,5},{8,10},{9,11},{10,... | collective-permute-start | bytes 798728 | tf_op jit(solution)/shard_map/ppermute | solution.py:250
  117.9 13.2 %collective-permute-start.9 = (s16[1040,128]{1,0:T(8,128)(2,1)}, s16[1040,128]{1,0:T(8,128)(2,1)S(1)}, u32[]{:S(2)}, u32[]{:S(2)}) collective-permute-start(s16[1040,128]{1,0:T(8,128)(2,1)} %get-tuple-element.49), channel_id=1, source_target_pairs={{0,3},{1,0},{2,1},{3,2},{4,7},{5,4},{6,5},{7,6},{8,11},{9,8},{10,9... | collective-permute-start | bytes 798728 | tf_op jit(solution)/shard_map/ppermute | solution.py:250
  122.6 12.3 %collective-permute-start.6 = (s16[1040,128]{1,0:T(8,128)(2,1)}, s16[1040,128]{1,0:T(8,128)(2,1)S(1)}, u32[]{:S(2)}, u32[]{:S(2)}) collective-permute-start(s16[1040,128]{1,0:T(8,128)(2,1)} %middle.5), channel_id=1, source_target_pairs={{0,4},{1,5},{2,6},{3,7},{4,0},{5,1},{6,2},{7,3},{8,12},{9,13},{10,... | collective-permute-start | bytes 798728 | tf_op jit(solution)/shard_map/ppermute | solution.py:249
  146.2 15.1 %collective-permute-start.14 = (s16[1040,128]{1,0:T(8,128)(2,1)}, s16[1040,128]{1,0:T(8,128)(2,1)S(1)}, u32[]{:S(2)}, u32[]{:S(2)}) collective-permute-start(s16[1040,128]{1,0:T(8,128)(2,1)} %get-tuple-element.55), channel_id=1, source_target_pairs={{0,1},{1,2},{2,3},{3,0},{4,5},{5,6},{6,7},{7,4},{8,9},{9,10},{10,1... | collective-permute-start | bytes 798728 | tf_op jit(solution)/shard_map/ppermute | solution.py:246
  146.3 16.6 %collective-permute-start.15 = (s16[1040,128]{1,0:T(8,128)(2,1)}, s16[1040,128]{1,0:T(8,128)(2,1)S(1)}, u32[]{:S(2)}, u32[]{:S(2)}) collective-permute-start(s16[1040,128]{1,0:T(8,128)(2,1)} %get-tuple-element.56), channel_id=1, source_target_pairs={{0,2},{1,3},{2,0},{3,1},{4,6},{5,7},{6,4},{7,5},{8,10},{9,11},{10,... | collective-permute-start | bytes 798728 | tf_op jit(solution)/shard_map/ppermute | solution.py:246
  148.8 14.7 %collective-permute-start.16 = (s16[1040,128]{1,0:T(8,128)(2,1)}, s16[1040,128]{1,0:T(8,128)(2,1)S(1)}, u32[]{:S(2)}, u32[]{:S(2)}) collective-permute-start(s16[1040,128]{1,0:T(8,128)(2,1)} %get-tuple-element.57), channel_id=1, source_target_pairs={{0,3},{1,0},{2,1},{3,2},{4,7},{5,4},{6,5},{7,6},{8,11},{9,8},{10,9... | collective-permute-start | bytes 798728 | tf_op jit(solution)/shard_map/ppermute | solution.py:246
  159.5 14.1 %collective-permute-start.17 = (s16[1040,128]{1,0:T(8,128)(2,1)}, s16[1040,128]{1,0:T(8,128)(2,1)S(1)}, u32[]{:S(2)}, u32[]{:S(2)}) collective-permute-start(s16[1040,128]{1,0:T(8,128)(2,1)} %get-tuple-element.59), channel_id=1, source_target_pairs={{0,1},{1,2},{2,3},{3,0},{4,5},{5,6},{6,7},{7,4},{8,9},{9,10},{10,1... | collective-permute-start | bytes 798728 | tf_op jit(solution)/shard_map/ppermute | solution.py:250
  159.6 14.0 %collective-permute-start.18 = (s16[1040,128]{1,0:T(8,128)(2,1)}, s16[1040,128]{1,0:T(8,128)(2,1)S(1)}, u32[]{:S(2)}, u32[]{:S(2)}) collective-permute-start(s16[1040,128]{1,0:T(8,128)(2,1)} %get-tuple-element.60), channel_id=1, source_target_pairs={{0,2},{1,3},{2,0},{3,1},{4,6},{5,7},{6,4},{7,5},{8,10},{9,11},{10,... | collective-permute-start | bytes 798728 | tf_op jit(solution)/shard_map/ppermute | solution.py:250
  161.3 13.0 %collective-permute-start.19 = (s16[1040,128]{1,0:T(8,128)(2,1)}, s16[1040,128]{1,0:T(8,128)(2,1)S(1)}, u32[]{:S(2)}, u32[]{:S(2)}) collective-permute-start(s16[1040,128]{1,0:T(8,128)(2,1)} %get-tuple-element.61), channel_id=1, source_target_pairs={{0,3},{1,0},{2,1},{3,2},{4,7},{5,4},{6,5},{7,6},{8,11},{9,8},{10,9... | collective-permute-start | bytes 798728 | tf_op jit(solution)/shard_map/ppermute | solution.py:250
  183.2 15.2 %collective-permute-start.20 = (s16[1040,128]{1,0:T(8,128)(2,1)}, s16[1040,128]{1,0:T(8,128)(2,1)S(1)}, u32[]{:S(2)}, u32[]{:S(2)}) collective-permute-start(s16[1040,128]{1,0:T(8,128)(2,1)} %get-tuple-element.63), channel_id=1, source_target_pairs={{0,1},{1,2},{2,3},{3,0},{4,5},{5,6},{6,7},{7,4},{8,9},{9,10},{10,1... | collective-permute-start | bytes 798728 | tf_op jit(solution)/shard_map/ppermute | solution.py:246
  183.3 16.1 %collective-permute-start.21 = (s16[1040,128]{1,0:T(8,128)(2,1)}, s16[1040,128]{1,0:T(8,128)(2,1)S(1)}, u32[]{:S(2)}, u32[]{:S(2)}) collective-permute-start(s16[1040,128]{1,0:T(8,128)(2,1)} %get-tuple-element.64), channel_id=1, source_target_pairs={{0,2},{1,3},{2,0},{3,1},{4,6},{5,7},{6,4},{7,5},{8,10},{9,11},{10,... | collective-permute-start | bytes 798728 | tf_op jit(solution)/shard_map/ppermute | solution.py:246
  185.7 16.4 %collective-permute-start.22 = (s16[1040,128]{1,0:T(8,128)(2,1)}, s16[1040,128]{1,0:T(8,128)(2,1)S(1)}, u32[]{:S(2)}, u32[]{:S(2)}) collective-permute-start(s16[1040,128]{1,0:T(8,128)(2,1)} %get-tuple-element.65), channel_id=1, source_target_pairs={{0,3},{1,0},{2,1},{3,2},{4,7},{5,4},{6,5},{7,6},{8,11},{9,8},{10,9... | collective-permute-start | bytes 798728 | tf_op jit(solution)/shard_map/ppermute | solution.py:246
  195.8 14.8 %collective-permute-start.24 = (s16[1040,128]{1,0:T(8,128)(2,1)}, s16[1040,128]{1,0:T(8,128)(2,1)S(1)}, u32[]{:S(2)}, u32[]{:S(2)}) collective-permute-start(s16[1040,128]{1,0:T(8,128)(2,1)} %get-tuple-element.66), channel_id=1, source_target_pairs={{0,1},{1,2},{2,3},{3,0},{4,5},{5,6},{6,7},{7,4},{8,9},{9,10},{10,1... | collective-permute-start | bytes 798728 | tf_op jit(solution)/shard_map/ppermute | solution.py:250
  195.9 14.7 %collective-permute-start.25 = (s16[1040,128]{1,0:T(8,128)(2,1)}, s16[1040,128]{1,0:T(8,128)(2,1)S(1)}, u32[]{:S(2)}, u32[]{:S(2)}) collective-permute-start(s16[1040,128]{1,0:T(8,128)(2,1)} %get-tuple-element.67), channel_id=1, source_target_pairs={{0,2},{1,3},{2,0},{3,1},{4,6},{5,7},{6,4},{7,5},{8,10},{9,11},{10,... | collective-permute-start | bytes 798728 | tf_op jit(solution)/shard_map/ppermute | solution.py:250
  198.4 9.1 %collective-permute-start.27 = (s16[1040,128]{1,0:T(8,128)(2,1)S(1)}, s16[1040,128]{1,0:T(8,128)(2,1)S(1)}, u32[]{:S(2)}, u32[]{:S(2)}) collective-permute-start(s16[1040,128]{1,0:T(8,128)(2,1)S(1)} %copy-done.11), channel_id=1, source_target_pairs={{0,4},{1,5},{2,6},{3,7},{4,0},{5,1},{6,2},{7,3},{8,12},{9,13},{10,... | collective-permute-start | bytes 798728 | tf_op jit(solution)/shard_map/ppermute | solution.py:249
  199.3 11.9 %collective-permute-start.26 = (s16[1040,128]{1,0:T(8,128)(2,1)}, s16[1040,128]{1,0:T(8,128)(2,1)S(1)}, u32[]{:S(2)}, u32[]{:S(2)}) collective-permute-start(s16[1040,128]{1,0:T(8,128)(2,1)} %get-tuple-element.68), channel_id=1, source_target_pairs={{0,3},{1,0},{2,1},{3,2},{4,7},{5,4},{6,5},{7,6},{8,11},{9,8},{10,9... | collective-permute-start | bytes 798728 | tf_op jit(solution)/shard_map/ppermute | solution.py:250
  205.0 9.3 %collective-permute-start.23 = (s16[1040,128]{1,0:T(8,128)(2,1)}, s16[1040,128]{1,0:T(8,128)(2,1)S(1)}, u32[]{:S(2)}, u32[]{:S(2)}) collective-permute-start(s16[1040,128]{1,0:T(8,128)(2,1)} %middle.7), channel_id=1, source_target_pairs={{0,4},{1,5},{2,6},{3,7},{4,0},{5,1},{6,2},{7,3},{8,12},{9,13},{10,... | collective-permute-start | bytes 798728 | tf_op jit(solution)/shard_map/ppermute | solution.py:249
  (30 other events, 108.6 us)
Sparse Core Ops, SparseCore 0:
  9.1 39.9 all-gather.10
  50.7 39.6 all-gather.8
  94.9 36.6 all-gather.14
  138.1 35.0 all-gather.12
